TPU v7x, 32 devices: a whole 2x2x4 slice. The times are simulated.
32 devices in a mesh: ctx: 8 (over y, x, core), fsdp: 4 (over z).
Axes of the slice: x: 2, y: 2, z: 4, core: 2. Of those that a mesh axis runs over, the one named last changes fastest.
Arguments:
- tokens: bfloat16 [4, 1024, 1024], P('fsdp', 'ctx'), may hold values from -6 to 6
- segment_ids: int32 [4, 1024], P('fsdp', 'ctx'), may hold values from 0 to 3, never falling along the last dimension, each value on 1 to 512 neighbouring positions
- random_blocks: int32 [4, 16, 16, 3], P('fsdp', 'ctx'), may hold values from 0 to 15, as said below
- global_blocks: int32 [4, 2], P('fsdp'), may hold values from 0 to 15, as said below
- first_gain: bfloat16 [1024], P('fsdp'), may hold values from 0.5 to 1.5
- first_bias: bfloat16 [1024], P('fsdp'), may hold values from -1.796875 to 1.796875
- joint_weight: bfloat16 [1024, 3072], P('fsdp'), may hold values from -0.1875 to 0.1875
- output_weight: bfloat16 [1024, 1024], P('fsdp'), may hold values from -2 to 2
- second_gain: bfloat16 [1024], P('fsdp'), may hold values from 0.5 to 1.5
- second_bias: bfloat16 [1024], P('fsdp'), may hold values from -1.796875 to 1.796875
- up_weight: bfloat16 [1024, 4096], P('fsdp'), may hold values from -0.1875 to 0.1875
- up_bias: bfloat16 [4096], P('fsdp'), may hold values from -3 to 3
- down_weight: bfloat16 [4096, 1024], P('fsdp'), may hold values from -0.09375 to 0.09375
- down_bias: bfloat16 [1024], P('fsdp'), may hold values from -1.796875 to 1.796875
- cotangent: bfloat16 [4, 1024, 1024], P('fsdp', 'ctx'), may hold values from -6 to 6
Outputs:
- layer_out: bfloat16 [4, 1024, 1024], P('fsdp', 'ctx')
- tokens_grad: float32 [4, 1024, 1024], P('fsdp', 'ctx')
- first_gain_grad: float32 [1024], P('fsdp')
- first_bias_grad: float32 [1024], P('fsdp')
- joint_weight_grad: float32 [1024, 3072], P('fsdp')
- output_weight_grad: float32 [1024, 1024], P('fsdp')
- second_gain_grad: float32 [1024], P('fsdp')
- second_bias_grad: float32 [1024], P('fsdp')
- up_weight_grad: float32 [1024, 4096], P('fsdp')
- up_bias_grad: float32 [4096], P('fsdp')
- down_weight_grad: float32 [4096, 1024], P('fsdp')
- down_bias_grad: float32 [1024], P('fsdp')
Inputs may be any that keep to these rules, and one draw needn't show every extreme that they name: `random_blocks`: for each sequence, query block and head, 3 different blocks of the sequence, none of them the query block, a neighbour of it or a global block of the sequence. `global_blocks`: 2 different blocks of each sequence.
All inputs are finite; a program needn't handle non-finite values.
Results may differ from a plain program's by a relative error of at most 0.02.
Values may be sent and summed in bfloat16 or wider, within the bound.
A program may use at most 192 MiB of HBM per device.

v0:
```python
import jax
import jax.numpy as jnp
from jax import lax
from jax.sharding import PartitionSpec as P

BLOCK = 64
GLOBAL = 2


SCALE_QK = 0.125
NEG_FILL = -1e30


def for_sending(value):

    def short(part):
        return part.astype(jnp.bfloat16) if part.dtype == jnp.float32 else part

    return jax.tree.map(short, value)


def normalize(values, gain, shift):
    centre = jnp.mean(values, axis=-1, keepdims=True)
    offset = values - centre
    spread = jnp.mean(offset * offset, axis=-1, keepdims=True)
    return offset * lax.rsqrt(spread + 1e-05) * gain + shift


def exact_gelu(values):
    return jax.nn.gelu(values, approximate=False)


def key_lists(block_ids, random_part, global_pair, block_count):
    heads = random_part.shape[1]
    number = block_ids.shape[0]
    window = block_ids[:, None] + jnp.arange(-1, 2, dtype=jnp.int32)[None, :]
    window_ok = (window >= 0) & (window < block_count)
    near = jnp.abs(global_pair[None, :] - block_ids[:, None]) <= 1
    indices = jnp.concatenate(
        [
            jnp.broadcast_to(window[:, None, :], (number, heads, 3)),
            random_part,
            jnp.broadcast_to(global_pair[None, None, :], (number, heads, global_pair.shape[0])),
        ],
        axis=2,
    )
    valid = jnp.concatenate(
        [
            jnp.broadcast_to(window_ok[:, None, :], (number, heads, 3)),
            jnp.ones(random_part.shape, jnp.bool_),
            jnp.broadcast_to(~near[:, None, :], (number, heads, global_pair.shape[0])),
        ],
        axis=2,
    )
    return (jnp.clip(indices, 0, block_count - 1), valid)


def contract_rows(left, right):
    return lax.dot_general(
        left, right, (((0,), (0,)), ((), ())), preferred_element_type=jnp.float32
    )


def contract_cols(left, right):
    return lax.dot_general(
        left, right, (((1,), (1,)), ((), ())), preferred_element_type=jnp.float32
    )


def shards(
    tokens,
    segment_ids,
    random_blocks,
    global_blocks,
    first_gain,
    first_bias,
    joint_weight,
    output_weight,
    second_gain,
    second_bias,
    up_weight,
    up_bias,
    down_weight,
    down_bias,
    cotangent,
):
    residual_in = tokens[0].astype(jnp.float32)
    local_len, width = residual_in.shape
    seg_local = segment_ids[0]
    random_local = random_blocks[0]
    global_pair = global_blocks[0]
    heads = random_local.shape[1]
    head_size = width // heads
    local_blocks = local_len // BLOCK
    ctx_size = lax.axis_size("ctx")
    first_block = lax.axis_index("ctx") * local_blocks
    block_count = local_blocks * ctx_size
    seq_len = local_len * ctx_size
    block_ids = first_block + jnp.arange(local_blocks, dtype=jnp.int32)
    attn_params = (
        lax.all_gather(first_gain, "fsdp", axis=0, tiled=True),
        lax.all_gather(first_bias, "fsdp", axis=0, tiled=True),
        lax.all_gather(joint_weight, "fsdp", axis=0, tiled=True),
        lax.all_gather(output_weight, "fsdp", axis=0, tiled=True),
    )
    feed_params = (
        lax.all_gather(second_gain, "fsdp", axis=0, tiled=True),
        lax.all_gather(second_bias, "fsdp", axis=0, tiled=True),
        lax.all_gather(up_weight, "fsdp", axis=0, tiled=True),
        lax.all_gather(up_bias, "fsdp", axis=0, tiled=True),
        lax.all_gather(down_weight, "fsdp", axis=0, tiled=True),
        lax.all_gather(down_bias, "fsdp", axis=0, tiled=True),
    )
    gain_one = attn_params[0].astype(jnp.float32)
    bias_one = attn_params[1].astype(jnp.float32)
    normed_one = normalize(residual_in, gain_one, bias_one).astype(jnp.bfloat16)
    projected = jnp.dot(normed_one, attn_params[2], preferred_element_type=jnp.float32).astype(
        jnp.bfloat16
    )
    query = projected[:, :width]
    pair_full, seg_full = (
        lax.all_gather(projected[:, width:], "ctx", axis=0, tiled=True),
        lax.all_gather(seg_local, "ctx", axis=0, tiled=True),
    )
    keys_seq = pair_full[:, :width].reshape(seq_len, heads, head_size)
    values_seq = pair_full[:, width:].reshape(seq_len, heads, head_size)
    keys_blocks = keys_seq.reshape(block_count, BLOCK, heads, head_size)
    values_blocks = values_seq.reshape(block_count, BLOCK, heads, head_size)
    query_blocks = query.reshape(local_blocks, BLOCK, heads, head_size)
    seg_query = seg_local.reshape(local_blocks, BLOCK)
    seg_blocks = seg_full.reshape(block_count, BLOCK)
    indices, valid = key_lists(block_ids, random_local, global_pair, block_count)
    head_ids = jnp.arange(heads, dtype=jnp.int32)[None, :, None]
    key_sel = keys_blocks[indices, :, head_ids, :]
    value_sel = values_blocks[indices, :, head_ids, :]
    seg_sel = seg_blocks[indices]
    allow = valid[:, :, None, :, None] & (
        seg_query[:, None, :, None, None] == seg_sel[:, :, None, :, :]
    )

    def sparse_scores():
        raw = (
            jnp.einsum(
                "bphe,bhjqe->bhpjq", query_blocks, key_sel, preferred_element_type=jnp.float32
            )
            * SCALE_QK
        )
        return jnp.where(allow, raw, NEG_FILL)

    masked = sparse_scores()
    peak = jnp.max(masked, axis=(3, 4), keepdims=True)
    weights = jnp.where(allow, jnp.exp(masked - peak), 0.0)
    total = jnp.sum(weights, axis=(3, 4), keepdims=True)
    log_total = peak + jnp.log(total)
    shares = (weights / total).astype(jnp.bfloat16)
    attn_out = jnp.einsum(
        "bhpjq,bhjqe->bphe", shares, value_sel, preferred_element_type=jnp.float32
    )
    slot_info = []
    for slot in range(GLOBAL):
        local_index = global_pair[slot] - first_block
        owned = (local_index >= 0) & (local_index < local_blocks)
        clipped = jnp.clip(local_index, 0, local_blocks - 1)
        query_rows = lax.dynamic_index_in_dim(query_blocks, clipped, 0, keepdims=False)
        seg_rows = lax.dynamic_index_in_dim(seg_query, clipped, 0, keepdims=False)
        allow_rows = seg_rows[None, :, None] == seg_full[None, None, :]

        def global_forward():
            raw_rows = (
                jnp.einsum("phe,khe->hpk", query_rows, keys_seq, preferred_element_type=jnp.float32)
                * SCALE_QK
            )
            masked_rows = jnp.where(allow_rows, raw_rows, NEG_FILL)
            peak_rows = jnp.max(masked_rows, axis=2, keepdims=True)
            weights_rows = jnp.where(allow_rows, jnp.exp(masked_rows - peak_rows), 0.0)
            total_rows = jnp.sum(weights_rows, axis=2, keepdims=True)
            shares_rows = (weights_rows / total_rows).astype(jnp.bfloat16)
            rows_out = jnp.einsum(
                "hpk,khe->phe", shares_rows, values_seq, preferred_element_type=jnp.float32
            )
            return (rows_out, peak_rows + jnp.log(total_rows))

        def global_skip():
            return (
                jnp.zeros((BLOCK, heads, head_size), jnp.float32),
                jnp.zeros((heads, BLOCK, 1), jnp.float32),
            )

        rows_out, rows_log = lax.cond(owned, global_forward, global_skip)
        current = lax.dynamic_index_in_dim(attn_out, clipped, 0, keepdims=False)
        attn_out = lax.dynamic_update_index_in_dim(
            attn_out, jnp.where(owned, rows_out, current), clipped, 0
        )
        slot_info.append((owned, clipped, query_rows, allow_rows, rows_log))
    attended = attn_out.reshape(local_len, width).astype(jnp.bfloat16)
    middle = residual_in + jnp.dot(attended, attn_params[3], preferred_element_type=jnp.float32)
    gain_two = feed_params[0].astype(jnp.float32)
    bias_two = feed_params[1].astype(jnp.float32)
    normed_two = normalize(middle, gain_two, bias_two).astype(jnp.bfloat16)
    up_sum = jnp.dot(normed_two, feed_params[2], preferred_element_type=jnp.float32) + feed_params[
        3
    ].astype(jnp.float32)
    hidden = exact_gelu(up_sum).astype(jnp.bfloat16)
    result = (
        middle
        + jnp.dot(hidden, feed_params[4], preferred_element_type=jnp.float32)
        + feed_params[5].astype(jnp.float32)
    )
    layer_out = result.astype(jnp.bfloat16)
    grad_out = cotangent[0]
    grad_float = grad_out.astype(jnp.float32)
    feed_local, grad_float = lax.optimization_barrier(
        ((second_gain, second_bias, up_weight, up_bias, down_weight, down_bias), grad_float)
    )
    feed_back = (
        lax.all_gather(feed_local[0], "fsdp", axis=0, tiled=True),
        lax.all_gather(feed_local[1], "fsdp", axis=0, tiled=True),
        lax.all_gather(feed_local[2], "fsdp", axis=0, tiled=True),
        lax.all_gather(feed_local[3], "fsdp", axis=0, tiled=True),
        lax.all_gather(feed_local[4], "fsdp", axis=0, tiled=True),
        lax.all_gather(feed_local[5], "fsdp", axis=0, tiled=True),
    )
    attn_local, grad_float = lax.optimization_barrier(
        ((first_gain, first_bias, joint_weight, output_weight), grad_float)
    )
    attn_back = (
        lax.all_gather(attn_local[0], "fsdp", axis=0, tiled=True),
        lax.all_gather(attn_local[1], "fsdp", axis=0, tiled=True),
        lax.all_gather(attn_local[2], "fsdp", axis=0, tiled=True),
        lax.all_gather(attn_local[3], "fsdp", axis=0, tiled=True),
    )
    down_bias_grad = jnp.sum(grad_float, axis=0)
    down_weight_grad = contract_rows(hidden, grad_out)
    hidden_grad = contract_cols(grad_out, feed_back[4])
    gelu_pull = jax.vjp(exact_gelu, up_sum)[1]
    up_grad = gelu_pull(hidden_grad)[0].astype(jnp.bfloat16)
    up_bias_grad = jnp.sum(up_grad.astype(jnp.float32), axis=0)
    up_weight_grad = contract_rows(normed_two, up_grad)
    normed_two_grad = contract_cols(up_grad, feed_back[2])
    norm_pull = jax.vjp(
        normalize, middle, feed_back[0].astype(jnp.float32), feed_back[1].astype(jnp.float32)
    )[1]
    middle_part, second_gain_grad, second_bias_grad = norm_pull(normed_two_grad)
    middle_grad = grad_float + middle_part
    branch_grad = middle_grad.astype(jnp.bfloat16)
    output_weight_grad = contract_rows(attended, branch_grad)
    attended_grad = (
        contract_cols(branch_grad, attn_back[3])
        .astype(jnp.bfloat16)
        .reshape(local_blocks, BLOCK, heads, head_size)
    )
    is_global = jnp.any(block_ids[:, None] == global_pair[None, :], axis=1)
    sparse_grad = jnp.where(
        is_global[:, None, None, None], jnp.zeros_like(attended_grad), attended_grad
    )
    shares_back = jnp.where(allow, jnp.exp(sparse_scores() - log_total), 0.0)
    prob_grad = jnp.einsum(
        "bphe,bhjqe->bhpjq", sparse_grad, value_sel, preferred_element_type=jnp.float32
    )
    delta = jnp.sum(shares_back * prob_grad, axis=(3, 4), keepdims=True)
    score_grad = (shares_back * (prob_grad - delta)).astype(jnp.bfloat16)
    query_grad = (
        jnp.einsum("bhpjq,bhjqe->bphe", score_grad, key_sel, preferred_element_type=jnp.float32)
        * SCALE_QK
    )
    key_sel_grad = (
        jnp.einsum(
            "bhpjq,bphe->bhjqe", score_grad, query_blocks, preferred_element_type=jnp.float32
        )
        * SCALE_QK
    )
    value_sel_grad = jnp.einsum(
        "bhpjq,bphe->bhjqe",
        shares_back.astype(jnp.bfloat16),
        sparse_grad,
        preferred_element_type=jnp.float32,
    )
    keys_grad = (
        jnp.zeros((block_count, BLOCK, heads, head_size), jnp.float32)
        .at[indices, :, head_ids, :]
        .add(key_sel_grad)
        .reshape(seq_len, heads, head_size)
    )
    values_grad = (
        jnp.zeros((block_count, BLOCK, heads, head_size), jnp.float32)
        .at[indices, :, head_ids, :]
        .add(value_sel_grad)
        .reshape(seq_len, heads, head_size)
    )
    for owned, clipped, query_rows, allow_rows, rows_log in slot_info:
        rows_grad = lax.dynamic_index_in_dim(attended_grad, clipped, 0, keepdims=False)

        def global_backward():
            raw_rows = (
                jnp.einsum("phe,khe->hpk", query_rows, keys_seq, preferred_element_type=jnp.float32)
                * SCALE_QK
            )
            shares_rows = jnp.where(
                allow_rows, jnp.exp(jnp.where(allow_rows, raw_rows, NEG_FILL) - rows_log), 0.0
            )
            prob_rows = jnp.einsum(
                "phe,khe->hpk", rows_grad, values_seq, preferred_element_type=jnp.float32
            )
            delta_rows = jnp.sum(shares_rows * prob_rows, axis=2, keepdims=True)
            score_rows = (shares_rows * (prob_rows - delta_rows)).astype(jnp.bfloat16)
            query_part = (
                jnp.einsum("hpk,khe->phe", score_rows, keys_seq, preferred_element_type=jnp.float32)
                * SCALE_QK
            )
            keys_part = (
                jnp.einsum(
                    "hpk,phe->khe", score_rows, query_rows, preferred_element_type=jnp.float32
                )
                * SCALE_QK
            )
            values_part = jnp.einsum(
                "hpk,phe->khe",
                shares_rows.astype(jnp.bfloat16),
                rows_grad,
                preferred_element_type=jnp.float32,
            )
            return (query_part, keys_part, values_part)

        def global_none():
            return (
                jnp.zeros((BLOCK, heads, head_size), jnp.float32),
                jnp.zeros((seq_len, heads, head_size), jnp.float32),
                jnp.zeros((seq_len, heads, head_size), jnp.float32),
            )

        query_part, keys_part, values_part = lax.cond(owned, global_backward, global_none)
        current = lax.dynamic_index_in_dim(query_grad, clipped, 0, keepdims=False)
        query_grad = lax.dynamic_update_index_in_dim(query_grad, current + query_part, clipped, 0)
        keys_grad = keys_grad + keys_part
        values_grad = values_grad + values_part
    keys_local, values_local = (
        lax.psum_scatter(
            keys_grad.reshape(seq_len, width).astype(jnp.bfloat16),
            "ctx",
            scatter_dimension=0,
            tiled=True,
        ).astype(jnp.float32),
        lax.psum_scatter(
            values_grad.reshape(seq_len, width).astype(jnp.bfloat16),
            "ctx",
            scatter_dimension=0,
            tiled=True,
        ).astype(jnp.float32),
    )
    projected_grad = jnp.concatenate(
        [
            query_grad.reshape(local_len, width).astype(jnp.bfloat16),
            keys_local.astype(jnp.bfloat16),
            values_local.astype(jnp.bfloat16),
        ],
        axis=1,
    )
    joint_weight_grad = contract_rows(normed_one, projected_grad)
    normed_one_grad = contract_cols(projected_grad, attn_back[2])
    first_pull = jax.vjp(
        normalize, residual_in, attn_back[0].astype(jnp.float32), attn_back[1].astype(jnp.float32)
    )[1]
    input_part, first_gain_grad, first_bias_grad = first_pull(normed_one_grad)
    tokens_grad = middle_grad + input_part
    owner_sums = (
        lax.psum_scatter(
            first_gain_grad.astype(jnp.bfloat16), "fsdp", scatter_dimension=0, tiled=True
        ).astype(jnp.float32),
        lax.psum_scatter(
            first_bias_grad.astype(jnp.bfloat16), "fsdp", scatter_dimension=0, tiled=True
        ).astype(jnp.float32),
        lax.psum_scatter(
            joint_weight_grad.astype(jnp.bfloat16), "fsdp", scatter_dimension=0, tiled=True
        ).astype(jnp.float32),
        lax.psum_scatter(
            output_weight_grad.astype(jnp.bfloat16), "fsdp", scatter_dimension=0, tiled=True
        ).astype(jnp.float32),
        lax.psum_scatter(
            second_gain_grad.astype(jnp.bfloat16), "fsdp", scatter_dimension=0, tiled=True
        ).astype(jnp.float32),
        lax.psum_scatter(
            second_bias_grad.astype(jnp.bfloat16), "fsdp", scatter_dimension=0, tiled=True
        ).astype(jnp.float32),
        lax.psum_scatter(
            up_weight_grad.astype(jnp.bfloat16), "fsdp", scatter_dimension=0, tiled=True
        ).astype(jnp.float32),
        lax.psum_scatter(
            up_bias_grad.astype(jnp.bfloat16), "fsdp", scatter_dimension=0, tiled=True
        ).astype(jnp.float32),
        lax.psum_scatter(
            down_weight_grad.astype(jnp.bfloat16), "fsdp", scatter_dimension=0, tiled=True
        ).astype(jnp.float32),
        lax.psum_scatter(
            down_bias_grad.astype(jnp.bfloat16), "fsdp", scatter_dimension=0, tiled=True
        ).astype(jnp.float32),
    )
    totals = jax.tree.map(
        lambda part: part.astype(jnp.float32), lax.psum(for_sending(tuple(owner_sums)), "ctx")
    )
    return (
        layer_out[None],
        tokens_grad[None],
        totals[0],
        totals[1],
        totals[2],
        totals[3],
        totals[4],
        totals[5],
        totals[6],
        totals[7],
        totals[8],
        totals[9],
    )


def solution(mesh):
    in_specs = (
        P("fsdp", "ctx", None),
        P("fsdp", "ctx"),
        P("fsdp", "ctx", None, None),
        P("fsdp", None),
        P("fsdp"),
        P("fsdp"),
        P("fsdp", None),
        P("fsdp", None),
        P("fsdp"),
        P("fsdp"),
        P("fsdp", None),
        P("fsdp"),
        P("fsdp", None),
        P("fsdp"),
        P("fsdp", "ctx", None),
    )
    out_specs = (
        P("fsdp", "ctx", None),
        P("fsdp", "ctx", None),
        P("fsdp"),
        P("fsdp"),
        P("fsdp", None),
        P("fsdp", None),
        P("fsdp"),
        P("fsdp"),
        P("fsdp", None),
        P("fsdp"),
        P("fsdp", None),
        P("fsdp"),
    )
    return jax.shard_map(shards, mesh=mesh, in_specs=in_specs, out_specs=out_specs, check_vma=False)
```

profile of v0, /device:TPU:0, one launch (start us, length us, event | category | flops | bytes accessed | tf_op | source)
XLA Modules:
  0.0 1844.3 jit_solution(5466574009499495229)
XLA Ops:
  8.6 12.6 all-gather.2
  32.0 95.7 %all-gather.18.cloned.1.call-done = bf16[1024,3072]{1,0:T(8,128)(2,1)} async-done(((bf16[256,3072]{1,0:T(8,128)(2,1)}), bf16[1024,3072]{1,0:T(8,128)(2,1)}) %all-gather.18.cloned.1.call-update) | async-done | bytes 6291472 | tf_op jit(solution)/shard_map/all_gather | solution.py:103
  139.2 11.9 all_gather.63
  267.1 98.0 %all-gather.24.cloned.1.call-done = bf16[1024,4096]{1,0:T(8,128)(2,1)} async-done(((bf16[256,4096]{1,0:T(8,128)(2,1)}), bf16[1024,4096]{1,0:T(8,128)(2,1)}) %all-gather.24.cloned.1.call-update) | async-done | bytes 8388624 | tf_op jit(solution)/shard_map/all_gather | solution.py:109
  374.6 139.9 %all-gather.28.cloned.1.call-done = bf16[4096,1024]{1,0:T(8,128)(2,1)} async-done(((bf16[1024,1024]{1,0:T(8,128)(2,1)}), bf16[4096,1024]{1,0:T(8,128)(2,1)}) %all-gather.28.cloned.1.call-update) | async-done | bytes 8388624 | tf_op jit(solution)/shard_map/all_gather | solution.py:220
  514.4 11.2 fusion.91
  525.6 138.2 %all-gather.30.cloned.1.call-done = bf16[1024,4096]{1,0:T(8,128)(2,1)} async-done(((bf16[256,4096]{1,0:T(8,128)(2,1)}), bf16[1024,4096]{1,0:T(8,128)(2,1)}) %all-gather.30.cloned.1.call-update) | async-done | bytes 8388624 | tf_op jit(solution)/shard_map/all_gather | solution.py:218
  672.7 36.8 %all-gather.32.cloned.1.call-done = bf16[1024,1024]{1,0:T(8,128)(2,1)} async-done(((bf16[256,1024]{1,0:T(8,128)(2,1)}), bf16[1024,1024]{1,0:T(8,128)(2,1)}) %all-gather.32.cloned.1.call-update) | async-done | bytes 2097168 | tf_op jit(solution)/shard_map/all_gather | solution.py:230
  714.0 10.7 multiply_reduce_fusion.2
  737.8 41.1 %scatter_fusion.1 = f32[16,64,16,64]{3,1,2,0:T(8,128)} fusion(f32[16,64,16,64]{3,1,2,0:T(8,128)} %broadcast.510.clone, s32[256]{0:T(256)S(1)} %reshape.446, f32[256,64,64]{2,1,0:T(8,128)} %bitcast.243), kind=kCustom, calls=%fused_computation.4 | custom fusion | flops 1048576 | bytes 12584960 | tf_op jit(solution)/shard_map/scatter-add | solution.py:287
  812.7 41.0 %scatter_fusion = f32[16,64,16,64]{3,1,2,0:T(8,128)} fusion(f32[16,64,16,64]{3,1,2,0:T(8,128)} %broadcast.510.clone.1, s32[256]{0:T(256)S(1)} %reshape.446, f32[256,64,64]{2,1,0:T(8,128)} %bitcast.246), kind=kCustom, calls=%fused_computation.3 | custom fusion | flops 1048576 | bytes 12584960 | tf_op jit(solution)/shard_map/scatter-add | solution.py:281
  884.2 12.1 add_convert_fusion
  914.6 39.7 %reduce-scatter.7.cloned.1.call-done = bf16[128,1024]{1,0:T(8,128)(2,1)} async-done(((bf16[1024,1024]{1,0:T(8,128)(2,1)}), bf16[128,1024]{1,0:T(8,128)(2,1)}) %reduce-scatter.7.cloned.1.call-update) | async-done | bytes 262160 | tf_op jit(solution)/shard_map/reduce_scatter | solution.py:337
  955.3 44.5 %reduce-scatter.9.cloned.1.call-done = bf16[128,1024]{1,0:T(8,128)(2,1)} async-done(((bf16[1024,1024]{1,0:T(8,128)(2,1)}), bf16[128,1024]{1,0:T(8,128)(2,1)}) %reduce-scatter.9.cloned.1.call-update) | async-done | bytes 262160 | tf_op jit(solution)/shard_map/reduce_scatter | solution.py:343
  1020.6 25.3 %reduce-scatter.13.cloned.1.call-done = bf16[256,1024]{1,0:T(8,128)(2,1)} async-done(((bf16[1024,1024]{1,0:T(8,128)(2,1)}), bf16[256,1024]{1,0:T(8,128)(2,1)}) %reduce-scatter.13.cloned.1.call-update) | async-done | bytes 524304 | tf_op jit(solution)/shard_map/reduce_scatter | solution.py:375
  1045.9 112.5 %reduce-scatter.11.cloned.1.call-done = bf16[256,3072]{1,0:T(8,128)(2,1)} async-done(((bf16[1024,3072]{1,0:T(8,128)(2,1)}), bf16[256,3072]{1,0:T(8,128)(2,1)}) %reduce-scatter.11.cloned.1.call-update) | async-done | bytes 1572880 | tf_op jit(solution)/shard_map/reduce_scatter | solution.py:372
  1158.4 147.4 %reduce-scatter.15.cloned.1.call-done = bf16[256,4096]{1,0:T(8,128)(2,1)} async-done(((bf16[1024,4096]{1,0:T(8,128)(2,1)}), bf16[256,4096]{1,0:T(8,128)(2,1)}) %reduce-scatter.15.cloned.1.call-update) | async-done | bytes 2097168 | tf_op jit(solution)/shard_map/reduce_scatter | solution.py:384
  1305.8 147.7 %reduce-scatter.17.cloned.1.call-done = bf16[1024,1024]{1,0:T(8,128)(2,1)} async-done(((bf16[4096,1024]{1,0:T(8,128)(2,1)}), bf16[1024,1024]{1,0:T(8,128)(2,1)}) %reduce-scatter.17.cloned.1.call-update) | async-done | bytes 2097168 | tf_op jit(solution)/shard_map/reduce_scatter | solution.py:390
  1454.1 10.3 all-gather.5
  1474.2 131.1 %all-gather.26.cloned.1.call-done = bf16[4096,1024]{1,0:T(8,128)(2,1)} async-done(((bf16[1024,1024]{1,0:T(8,128)(2,1)}), bf16[4096,1024]{1,0:T(8,128)(2,1)}) %all-gather.26.cloned.1.call-update) | async-done | bytes 8388624 | tf_op jit(solution)/shard_map/all_gather | solution.py:111
  1610.7 109.8 %all-gather.34.cloned.1.call-done = bf16[1024,3072]{1,0:T(8,128)(2,1)} async-done(((bf16[256,3072]{1,0:T(8,128)(2,1)}), bf16[1024,3072]{1,0:T(8,128)(2,1)}) %all-gather.34.cloned.1.call-update) | async-done | bytes 6291472 | tf_op jit(solution)/shard_map/all_gather | solution.py:229
  1726.0 15.9 all-reduce.8
  1742.2 13.4 all-reduce.6
  1760.1 67.7 %all-reduce.11.cloned.1.call-done = (bf16[256,3072]{1,0:T(8,128)(2,1)}, bf16[256,1024]{1,0:T(8,128)(2,1)}, bf16[256,4096]{1,0:T(8,128)(2,1)}, bf16[1024,1024]{1,0:T(8,128)(2,1)}) async-done(((bf16[256,3072]{1,0:T(8,128)(2,1)}, bf16[256,1024]{1,0:T(8,128)(2,1)}, bf16[256,4096]{1,0:T(8,128)(2,1)}, bf16[1024,1024]{1,0:T(8,128)(2,1)}), (bf16[256,3072]{1,0:T(8,128)(2,1)}, bf16[256,1024]{1,0:T(8,128)(2,1)}, ...) | async-done | bytes 6291472 | tf_op jit(solution)/shard_map/psum | solution.py:398
  (338 shorter events, 324.9 us)
Async XLA Ops:
  7.2 120.5 %copy-start.3 = (bf16[1,128,1024]{2,1,0:T(8,128)(2,1)S(1)}, bf16[1,128,1024]{2,1,0:T(8,128)(2,1)}, u32[]{:S(2)}) copy-start(bf16[1,128,1024]{2,1,0:T(8,128)(2,1)} %param.23) | copy-start | bytes 786436
  7.2 120.5 %all-gather.18.cloned.1.call-start = ((), (), s32[]{:S(2)}) async-start(), calls=%async_computation.6 | async-start | bytes 7864320 | tf_op jit(solution)/shard_map/all_gather | solution.py:103
  7.9 184.3 %all-gather.20.cloned.1.call-start = ((), (), s32[]{:S(2)}) async-start(), calls=%async_computation.7 | async-start | bytes 4718592 | tf_op jit(solution)/shard_map/all_gather | solution.py:122
  21.2 110.3 %copy-start.32 = (f32[4,1,256]{2,1,0:T(1,128)}, f32[4,1,256]{2,1,0:T(1,128)S(1)}, u32[]{:S(2)}) copy-start(f32[4,1,256]{2,1,0:T(1,128)S(1)} %convert_element_type.255) | copy-start | bytes 12292
  132.4 132.2 %all-gather.22.cloned.1.call-start = ((), (), s32[]{:S(2)}) async-start(), calls=%async_computation.8 | async-start | bytes 2621440 | tf_op jit(solution)/shard_map/all_gather | solution.py:104
  133.2 231.9 %all-gather.24.cloned.1.call-start = ((), (), s32[]{:S(2)}) async-start(), calls=%async_computation.9 | async-start | bytes 10485760 | tf_op jit(solution)/shard_map/all_gather | solution.py:109
  133.8 380.7 %all-gather.28.cloned.1.call-start = ((), (), s32[]{:S(2)}) async-start(), calls=%async_computation.11 | async-start | bytes 10485760 | tf_op jit(solution)/shard_map/all_gather | solution.py:220
  134.7 529.0 %all-gather.30.cloned.1.call-start = ((), (), s32[]{:S(2)}) async-start(), calls=%async_computation.12 | async-start | bytes 10485760 | tf_op jit(solution)/shard_map/all_gather | solution.py:218
  135.3 574.2 %all-gather.32.cloned.1.call-start = ((), (), s32[]{:S(2)}) async-start(), calls=%async_computation.13 | async-start | bytes 2621440 | tf_op jit(solution)/shard_map/all_gather | solution.py:230
  136.1 818.3 %reduce-scatter.7.cloned.1.call-start = ((), (), s32[]{:S(2)}) async-start(), calls=%async_computation.14 | async-start | bytes 2359296 | tf_op jit(solution)/shard_map/reduce_scatter | solution.py:337
  262.4 102.6 %copy-start.36 = (f32[4,1,256]{2,1,0:T(1,128)S(1)}, f32[4,1,256]{2,1,0:T(1,128)}, u32[]{:S(2)}) copy-start(f32[4,1,256]{2,1,0:T(1,128)} %convert_element_type.256) | copy-start | bytes 12292
  262.4 102.7 %copy-start.52 = (f32[4096]{0:T(1024)S(1)}, f32[4096]{0:T(1024)}, u32[]{:S(2)}) copy-start(f32[4096]{0:T(1024)} %convert_element_type.217) | copy-start | bytes 49156
  266.9 107.7 %copy-start.53 = (f32[128]{0:T(128)}, f32[128]{0:T(128)S(1)}, u32[]{:S(2)}) copy-start(f32[128]{0:T(128)S(1)} %broadcast_multiply_fusion.1) | copy-start | bytes 1540
  267.1 107.5 %copy-start.69 = (f32[128]{0:T(128)}, f32[128]{0:T(128)S(1)}, u32[]{:S(2)}) copy-start(f32[128]{0:T(128)S(1)} %multiply_reduce_fusion.5) | copy-start | bytes 1540
  267.1 107.5 %copy-start.56 = (f32[128]{0:T(128)}, f32[128]{0:T(128)S(1)}, u32[]{:S(2)}) copy-start(f32[128]{0:T(128)S(1)} %fusion.76) | copy-start | bytes 1540
  365.1 149.3 %copy-start.28 = (bf16[1,128,1024]{2,1,0:T(8,128)(2,1)S(1)}, bf16[1,128,1024]{2,1,0:T(8,128)(2,1)}, u32[]{:S(2)}) copy-start(bf16[1,128,1024]{2,1,0:T(8,128)(2,1)} %param.37) | copy-start | bytes 786436
  900.3 99.6 %reduce-scatter.9.cloned.1.call-start = ((), (), s32[]{:S(2)}) async-start(), calls=%async_computation.15 | async-start | bytes 2359296 | tf_op jit(solution)/shard_map/reduce_scatter | solution.py:343
  902.9 143.0 %reduce-scatter.13.cloned.1.call-start = ((), (), s32[]{:S(2)}) async-start(), calls=%async_computation.18 | async-start | bytes 2621440 | tf_op jit(solution)/shard_map/reduce_scatter | solution.py:375
  906.1 252.3 %reduce-scatter.11.cloned.1.call-start = ((), (), s32[]{:S(2)}) async-start(), calls=%async_computation.17 | async-start | bytes 7864320 | tf_op jit(solution)/shard_map/reduce_scatter | solution.py:372
  1005.5 300.2 %reduce-scatter.15.cloned.1.call-start = ((), (), s32[]{:S(2)}) async-start(), calls=%async_computation.19 | async-start | bytes 10485760 | tf_op jit(solution)/shard_map/reduce_scatter | solution.py:384
  1012.5 441.0 %reduce-scatter.17.cloned.1.call-start = ((), (), s32[]{:S(2)}) async-start(), calls=%async_computation.20 | async-start | bytes 10485760 | tf_op jit(solution)/shard_map/reduce_scatter | solution.py:390
  1019.4 586.0 %all-gather.26.cloned.1.call-start = ((), (), s32[]{:S(2)}) async-start(), calls=%async_computation.10 | async-start | bytes 10485760 | tf_op jit(solution)/shard_map/all_gather | solution.py:111
  1020.0 700.5 %all-gather.34.cloned.1.call-start = ((), (), s32[]{:S(2)}) async-start(), calls=%async_computation.16 | async-start | bytes 7864320 | tf_op jit(solution)/shard_map/all_gather | solution.py:229
  1020.5 807.3 %all-reduce.11.cloned.1.call-start = ((), (), s32[]{:S(2)}) async-start(), calls=%async_computation.21 | async-start | bytes 12582912 | tf_op jit(solution)/shard_map/psum | solution.py:398
  (65 other events, 1340.3 us)
Sparse Core Ops, SparseCore 0:
  9.6 118.0 all-gather.17
  132.6 35.0 all-gather.19
  169.3 45.9 all-gather.21
  216.7 148.3 all-gather.23
  366.5 147.8 all-gather.27
  515.8 147.8 all-gather.29
  665.3 44.1 all-gather.31
  900.4 53.9 reduce-scatter.6
  958.6 41.2 reduce-scatter.8
  1002.0 43.8 reduce-scatter.12
  1048.3 110.0 reduce-scatter.10
  1160.7 144.9 reduce-scatter.14
  1308.2 145.1 reduce-scatter.16
  1455.0 150.3 all-gather.25
  1606.9 113.5 all-gather.33
  1724.4 103.4 all-reduce.10
where the time goes:
time: 1850 us; the launch traced here: 1840 us
  waiting for transfers between devices  1340 us (72%)
  other arithmetic  134 us (7%)
  local copies, waits for them, and re-layouts  130 us (7%)
  blocking collectives  114 us (6%)
  matrix products  109 us (6%)
    reduce_scatter x1, waiting for transfers between devices, shards(): lax.psum_scatter(down_weight_grad.astype(jnp.bfloat16), 'fsdp', scatter_d...  148 us
    reduce_scatter x1, waiting for transfers between devices, shards(): lax.psum_scatter(up_weight_grad.astype(jnp.bfloat16), 'fsdp', scatter_dim...  147 us
    all_gather x1, waiting for transfers between devices, shards(): lax.all_gather(feed_local[4], 'fsdp', axis=0, tiled=True)  140 us
    all_gather x1, waiting for transfers between devices, shards(): lax.all_gather(feed_local[2], 'fsdp', axis=0, tiled=True)  138 us
    all_gather x1, waiting for transfers between devices, shards(): lax.all_gather(down_weight, 'fsdp', axis=0, tiled=True)  131 us
    reduce_scatter x1, waiting for transfers between devices, shards(): lax.psum_scatter(joint_weight_grad.astype(jnp.bfloat16), 'fsdp', scatter_...  113 us
    all_gather x1, waiting for transfers between devices, shards(): lax.all_gather(attn_local[2], 'fsdp', axis=0, tiled=True)  110 us
    all_gather x1, waiting for transfers between devices, shards(): lax.all_gather(up_weight, 'fsdp', axis=0, tiled=True)  98 us
  transfers between devices with their start and end apart: 16, of which 14 were waited for; matrix products, arithmetic and copies ran while one was open for 9% of the time, Pallas kernels for 0%

commit v1 on v0

v1 whole, which is shorter than its diff:
```python
import types

import jax
import jax.numpy as jnp
from jax import lax
from jax.experimental import pallas as pl
from jax.experimental.pallas import tpu as pltpu
from jax.sharding import PartitionSpec as P

BLOCK = 64
LANES = 128
CTX = 8
SEGMENTS = 4
EPS = 1e-05
BIG = 1e30
MESH = pl.DeviceIdType.MESH
BF16 = jnp.bfloat16
F32 = jnp.float32


def dot(a, b):
    return lax.dot_general(a, b, (((1,), (0,)), ((), ())), preferred_element_type=F32)


def dot_nt(a, b):
    return lax.dot_general(a, b, (((1,), (1,)), ((), ())), preferred_element_type=F32)


def dot_tn(a, b):
    return lax.dot_general(a, b, (((0,), (0,)), ((), ())), preferred_element_type=F32)


def loop(lower, upper, body):
    lax.fori_loop(lower, upper, lambda i, carry: (body(i), carry)[1], jnp.int32(0))


def rows_of(index, size):
    return pl.ds(pl.multiple_of(index * size, size), size)


def remote(src, dst, send, recv, device):
    return pltpu.make_async_remote_copy(
        src_ref=src,
        dst_ref=dst,
        send_sem=send,
        recv_sem=recv,
        device_id=device,
        device_id_type=MESH,
    )


class Place:
    def __init__(self, planes):
        self.c = lax.axis_index("ctx")
        self.f = lax.axis_index("fsdp")
        self.planes = planes
        self.parity = lax.rem(self.c, 2)
        self.chip = lax.div(self.c, 2)
        self.partner = 2 * self.chip + 1 - self.parity

    def chip_at(self, g):
        low = lax.rem(lax.rem(self.chip, 2) + lax.rem(g, 2), 2)
        high = lax.rem(lax.div(self.chip, 2) + lax.div(g, 2), 2)
        return low + 2 * high

    def same(self, g):
        return 2 * self.chip_at(g) + self.parity

    def other(self, g):
        return 2 * self.chip_at(g) + 1 - self.parity

    def ctx_at(self, d):
        return lax.rem(self.c + d, CTX)

    def plane_at(self, d):
        return lax.rem(self.f + d, self.planes)


class Gather:
    def __init__(self, at, src, slot, send, recv):
        self.at, self.src, self.slot, self.send, self.recv = at, src, slot, send, recv

    def direct(self, i):
        at = self.at
        to = at.partner if i == 0 else at.same(jnp.int32(i))
        return remote(self.src, self.slot(at.c), self.send.at[i], self.recv.at[at.c], (to, at.f))

    def passed(self, g):
        at = self.at
        block = self.slot(at.same(g))
        return remote(
            block, block, self.send.at[3 + g], self.recv.at[at.same(g)], (at.partner, at.f)
        )

    def start(self):
        for i in range(4):
            self.direct(i).start()

    def wait(self, c):
        at = self.at
        block = self.slot(c)
        remote(block, block, self.send.at[0], self.recv.at[c], (at.partner, at.f)).wait_recv()

    def relay(self, g):
        self.wait(self.at.same(g))
        self.passed(g).start()

    def relays(self):
        loop(1, 4, self.relay)

    def waits(self):
        loop(0, 4, lambda g: self.wait(self.at.other(g)))

    def finish(self):
        for i in range(4):
            self.direct(i).wait_send()
        loop(1, 4, lambda g: self.passed(g).wait_send())


class Exchange:
    def __init__(self, at, src, slot, send, recv):
        self.at, self.src, self.slot, self.send, self.recv = at, src, slot, send, recv

    def copy(self, d):
        at = self.at
        to = at.ctx_at(d)
        return remote(
            self.src(to), self.slot(at.c), self.send.at[d - 1], self.recv.at[at.c], (to, at.f)
        )

    def start(self):
        loop(1, CTX, lambda d: self.copy(d).start())

    def wait(self, d):
        at = self.at
        c = at.ctx_at(d)
        block = self.slot(c)
        remote(block, block, self.send.at[0], self.recv.at[c], (c, at.f)).wait_recv()

    def waits(self):
        loop(1, CTX, self.wait)

    def finish(self):
        loop(1, CTX, lambda d: self.copy(d).wait_send())


class Planes:
    def __init__(self, at, src, slot, send, recv):
        self.at, self.src, self.slot, self.send, self.recv = at, src, slot, send, recv

    def copy(self, d):
        at = self.at
        to = at.plane_at(d)
        return remote(
            self.src(to), self.slot(at.f), self.send.at[d - 1], self.recv.at[at.f], (at.c, to)
        )

    def start(self):
        loop(1, self.at.planes, lambda d: self.copy(d).start())

    def wait(self, d):
        at = self.at
        f = at.plane_at(d)
        block = self.slot(f)
        remote(block, block, self.send.at[0], self.recv.at[f], (at.c, f)).wait_recv()

    def waits(self):
        loop(1, self.at.planes, self.wait)

    def finish(self):
        loop(1, self.at.planes, lambda d: self.copy(d).wait_send())


class Scatter:
    def __init__(self, at, part, pair, far, pair_send, pair_recv, far_send, far_recv):
        self.at, self.part, self.pair, self.far = at, part, pair, far
        self.pair_send, self.pair_recv = pair_send, pair_recv
        self.far_send, self.far_recv = far_send, far_recv

    def to_partner(self, g):
        at = self.at
        return remote(
            self.part.at[at.other(g)],
            self.pair.at[g],
            self.pair_send.at[g],
            self.pair_recv.at[g],
            (at.partner, at.f),
        )

    def to_chip(self, g):
        at = self.at
        return remote(
            self.part.at[at.same(g)],
            self.far.at[g - 1],
            self.far_send.at[g - 1],
            self.far_recv.at[g - 1],
            (at.same(g), at.f),
        )

    def forward(self, g):
        self.to_partner(g).wait_recv()
        own = self.at.same(g)
        both = self.part[own].astype(F32) + self.pair[g].astype(F32)
        self.part[own] = both.astype(BF16)
        self.to_chip(g).start()

    def forwards(self):
        loop(1, 4, self.forward)

    def total(self):
        zero = jnp.int32(0)
        self.to_partner(zero).wait_recv()
        loop(1, 4, lambda g: self.to_chip(g).wait_recv())
        both = self.part[self.at.c].astype(F32) + self.pair[0].astype(F32)
        return (both + self.far[0].astype(F32)) + (
            self.far[1].astype(F32) + self.far[2].astype(F32)
        )

    def finish(self):
        loop(0, 4, lambda g: self.to_partner(g).wait_send())
        loop(1, 4, lambda g: self.to_chip(g).wait_send())


def standard(values):
    centre = jnp.mean(values, axis=-1, keepdims=True)
    offset = values - centre
    spread = jnp.mean(offset * offset, axis=-1, keepdims=True)
    rate = lax.rsqrt(spread + EPS)
    return offset * rate, rate


def standard_grad(e, normal, rate):
    return rate * (
        e - jnp.mean(e, axis=-1, keepdims=True) - normal * jnp.mean(e * normal, axis=-1, keepdims=True)
    )


def layer_kernel(r, planes):
    at = Place(planes)
    me, f = at.c, at.f
    tokens, cotangent, extras, small = r.tokens, r.cotangent, r.extras, r.small
    local, width = tokens.shape
    seq = local * CTX
    part_rows = width // planes
    columns = width // CTX
    ff = planes * r.down.shape[0]
    ff_blocks = ff // LANES // CTX
    shard_blocks = ff // LANES // planes
    k_own = lax.div(f * shard_blocks, CTX)
    has_down = lax.div(me, shard_blocks) == lax.rem(f, CTX // shard_blocks)
    down_place = lax.rem(me, shard_blocks)

    def down_owner(k):
        return lax.div(CTX * k + me, shard_blocks)

    my_rows = rows_of(f, part_rows)
    my_columns = rows_of(me, columns)
    my_tokens = rows_of(me, local)

    stage = []
    for j in range(3):
        stage.append(
            pltpu.make_async_copy(
                r.joint.at[:, pl.ds(pl.multiple_of(width * j + columns * me, LANES), columns)],
                r.wj.at[my_rows, pl.ds(columns * j, columns)],
                r.stage.at[j],
            )
        )
    stage.append(
        pltpu.make_async_copy(
            r.outw.at[:, my_columns], r.wo.at[my_rows, my_columns], r.stage.at[3]
        )
    )
    for k in range(ff_blocks):
        stage.append(
            pltpu.make_async_copy(
                r.up.at[:, pl.ds(pl.multiple_of(CTX * LANES * k + LANES * me, LANES), LANES)],
                r.wu.at[my_rows, pl.ds(LANES * k, LANES)],
                r.stage.at[4 + k],
            )
        )
    down_copy = pltpu.make_async_copy(
        r.down.at[rows_of(down_place, LANES), :],
        r.wd.at[rows_of(k_own, LANES), :],
        r.stage.at[4 + ff_blocks],
    )
    for copy in stage:
        copy.start()

    @pl.when(has_down)
    def _():
        down_copy.start()

    barrier = pltpu.get_barrier_semaphore()
    loop(
        1,
        CTX,
        lambda d: pl.semaphore_signal(
            barrier, inc=1, device_id=(at.ctx_at(d), f), device_id_type=MESH
        ),
    )
    loop(
        1,
        planes,
        lambda d: pl.semaphore_signal(
            barrier, inc=1, device_id=(me, at.plane_at(d)), device_id_type=MESH
        ),
    )
    pl.semaphore_wait(barrier, CTX - 1 + planes - 1)

    tok_gather = Gather(
        at, tokens, lambda c: r.tokg.at[rows_of(c, local)], *r.tok_sem
    )
    cot_gather = Gather(
        at, cotangent, lambda c: r.cotg.at[rows_of(c, local)], *r.cot_sem
    )
    ext_swap = Exchange(
        at,
        lambda c: extras.at[c],
        lambda c: r.extg.at[rows_of(c, local)],
        *r.ext_sem,
    )
    small_planes = Planes(
        at, lambda to: small, lambda p: r.smallg.at[p], *r.small_sem
    )

    def weight_planes(ref, sems, width_ds):
        view = lambda p: ref.at[rows_of(p, part_rows), width_ds]
        return Planes(at, lambda to: view(f), view, *sems)

    wj_planes = weight_planes(r.wj, r.wj_sem, slice(None))
    wo_planes = weight_planes(r.wo, r.wo_sem, my_columns)
    wu_planes = weight_planes(r.wu, r.wu_sem, slice(None))
    wo_block = r.wo.at[:, my_columns]
    wo_gather = Gather(
        at, wo_block, lambda c: r.wo.at[:, rows_of(c, columns)], *r.wog_sem
    )

    def wd_copy(d):
        to = at.plane_at(d)
        block = r.wd.at[rows_of(k_own, LANES), :]
        return remote(block, block, r.wd_sem[0].at[d - 1], r.wd_sem[1].at[k_own], (me, to))

    small_planes.start()
    tok_gather.start()
    ext_swap.start()
    for copy in stage[:3]:
        copy.wait()
    wj_planes.start()
    stage[3].wait()
    wo_planes.start()

    r.tokg[my_tokens, :] = tokens[...]
    r.cotg[my_tokens, :] = cotangent[...]
    r.extg[my_tokens, :] = extras[me]
    r.smallg[f] = small[...]
    small_planes.waits()
    params = r.params
    params[...] = jnp.zeros_like(params)

    def add_params(p):
        params[...] += r.smallg[p].astype(F32)

    loop(0, planes, add_params)
    for k in range(ff_blocks):
        r.ub[0:1, k * LANES : (k + 1) * LANES] = params[5 + k : 6 + k, my_columns]

    def norm_tokens(g):
        @pl.when(g > 0)
        def _():
            tok_gather.relay(g)

        tok_gather.wait(at.other(g))
        rows = rows_of(at.chip_at(g), 2 * local)
        normal, _ = standard(r.tokg[rows, :].astype(F32))
        r.x1[rows, :] = (normal * params[0:1, :] + params[1:2, :]).astype(BF16)

    loop(0, 4, norm_tokens)
    cot_gather.start()
    for copy in stage[4:]:
        copy.wait()
    wu_planes.start()

    @pl.when(has_down)
    def _():
        down_copy.wait()
        loop(1, planes, lambda d: wd_copy(d).start())

    ext_swap.waits()
    wj_planes.waits()

    tile = 2 * local
    lane = lax.broadcasted_iota(jnp.int32, (tile, columns), 1)
    low = lane < columns // 2
    zero_tile = jnp.zeros((tile, columns), BF16)

    def project(i):
        rows = rows_of(i, tile)
        projected = dot(r.x1[rows, :], r.wj[...]).astype(BF16)
        q = projected[:, :columns] * jnp.array(0.125, BF16)
        k = projected[:, columns : 2 * columns]
        v = projected[:, 2 * columns :]
        ext = r.extg[rows, :]
        half = lax.rem(lane, columns // 2)
        token = lax.broadcasted_iota(jnp.int32, (tile, columns), 0) + i * tile
        hot = jnp.where(half == lax.div(token, BLOCK), 1.0, 0.0)
        blocks = seq // BLOCK
        k_ext = jnp.where(
            half < blocks,
            hot,
            jnp.where(half < blocks + SEGMENTS, (1.0 - ext.astype(F32)) * -BIG, 0.0),
        ).astype(BF16)
        r.q[rows, :] = q
        r.qa[0, rows, :] = jnp.where(low, q, ext)
        r.qa[1, rows, :] = jnp.where(low, ext, q)
        r.ka[0, rows, :] = jnp.where(low, k, k_ext)
        r.ka[1, rows, :] = jnp.where(low, k_ext, k)
        r.km[0, rows, :] = jnp.where(low, k, zero_tile)
        r.km[1, rows, :] = jnp.where(low, zero_tile, k)
        r.vm[0, rows, :] = jnp.where(low, v, zero_tile)
        r.vm[1, rows, :] = jnp.where(low, zero_tile, v)

    loop(0, seq // tile, project)
    wo_planes.waits()
    wo_gather.start()

    def attend(i):
        rows = rows_of(i, tile)
        out = None
        for h in range(2):
            scores = dot_nt(r.qa[h, rows, :], r.ka[h])
            weights = jnp.exp(scores - jnp.max(scores, axis=1, keepdims=True))
            shares = (weights / jnp.sum(weights, axis=1, keepdims=True)).astype(BF16)
            r.probs[h, rows, :] = shares
            term = dot(shares, r.vm[h])
            out = term if out is None else out + term
        r.att[rows, :] = out.astype(BF16)

    loop(0, seq // tile, attend)

    att_swap = Exchange(
        at,
        lambda c: r.att.at[rows_of(c, local)],
        lambda c: r.attx.at[c],
        *r.att_sem,
    )
    att_swap.start()
    cot_gather.relays()
    wo_gather.relays()
    r.attx[me] = r.att[my_tokens, :]
    att_swap.waits()
    for c in range(CTX):
        r.attg[my_tokens, c * columns : (c + 1) * columns] = r.attx[c]
    wo_gather.waits()
    middle = tokens[...].astype(F32) + dot(r.attg[my_tokens, :], r.wo[...])
    normal, rate = standard(middle)
    r.middle[...] = middle
    r.n2[...] = normal
    r.rate2[...] = jnp.broadcast_to(rate, r.rate2.shape)
    r.x2[my_tokens, :] = (normal * params[2:3, :] + params[3:4, :]).astype(BF16)
    x2_view = lambda c: r.x2.at[rows_of(c, local)]
    x2_gather = Gather(at, x2_view(me), x2_view, *r.x2_sem)
    x2_gather.start()
    attg_view = lambda c: r.attg.at[rows_of(c, local)]
    att_gather = Gather(at, attg_view(me), attg_view, *r.attg_sem)
    wu_planes.waits()

    def wd_wait(k):
        @pl.when(down_owner(k) != f)
        def _():
            block = r.wd.at[rows_of(k, LANES), :]
            remote(block, block, r.wd_sem[0].at[0], r.wd_sem[1].at[k], (me, down_owner(k))).wait_recv()

    loop(0, ff_blocks, wd_wait)

    back = Scatter(at, *r.back)
    feed = Scatter(at, *r.feed)
    first = Scatter(at, *r.first)
    r.ubg[...] = jnp.zeros_like(r.ubg)

    def feed_forward(g):
        @pl.when(g > 0)
        def _():
            x2_gather.relay(g)

        x2_gather.wait(at.other(g))
        cot_gather.wait(at.other(g))
        chip = at.chip_at(g)
        rows = rows_of(chip, tile)
        up_sum = dot(r.x2[rows, :], r.wu[...]) + r.ub[...]
        share = 0.5 * (1.0 + lax.erf(up_sum * 0.7071067811865476))
        hidden = (up_sum * share).astype(BF16)
        slope = share + up_sum * jnp.exp(-0.5 * up_sum * up_sum) * 0.3989422804014327
        r.hidden[rows, :] = hidden
        up_grad = (dot_nt(r.cotg[rows, :], r.wd[...]) * slope).astype(BF16)
        r.upg[rows, :] = up_grad
        r.ubg[...] += jnp.sum(up_grad.astype(F32), axis=0, keepdims=True)
        back_part = dot_nt(up_grad, r.wu[...]).astype(BF16)
        r.back[0][2 * chip] = back_part[:local]
        r.back[0][2 * chip + 1] = back_part[local:]
        back.to_partner(g).start()
        feed_part = dot(hidden, r.wd[...]).astype(BF16)
        r.feed[0][2 * chip] = feed_part[:local]
        r.feed[0][2 * chip + 1] = feed_part[local:]

    loop(0, 4, feed_forward)
    back.forwards()
    att_gather.start()

    def down_grad(k):
        r.dwd[k] = dot_tn(r.hidden[:, rows_of(k, LANES)], r.cotg[...]).astype(BF16)

    def dwd_copy(k):
        return remote(
            r.dwd.at[k], r.rd.at[f], r.dwd_sem[0].at[k], r.dwd_sem[1].at[f], (me, down_owner(k))
        )

    def dwd_send(k):
        down_grad(k)

        @pl.when(down_owner(k) != f)
        def _():
            dwd_copy(k).start()

    loop(0, ff_blocks, dwd_send)
    rows_tile = min(tile, width)

    def weight_grad(out, left, right):
        def body(i):
            out[rows_of(i, rows_tile), :] = dot_tn(
                left[:, rows_of(i, rows_tile)], right[...]
            ).astype(BF16)

        loop(0, width // rows_tile, body)

    def grad_planes(grad, taken, sems):
        return Planes(
            at,
            lambda to: grad.at[rows_of(to, part_rows), :],
            lambda p: taken.at[p],
            *sems,
        )

    du_planes = grad_planes(r.du, r.ru, r.du_sem)
    do_planes = grad_planes(r.do, r.ro, r.do_sem)
    dj_planes = grad_planes(r.dj, r.rj, r.dj_sem)
    weight_grad(r.du, r.x2, r.upg)
    du_planes.start()

    normed_two_grad = back.total()
    normal = r.n2[...]
    cot_own = cotangent[...].astype(F32)
    sums = r.sums
    sums[...] = jnp.zeros_like(sums)
    sums[2:3, :] = jnp.sum(normed_two_grad * normal, axis=0, keepdims=True)
    sums[3:4, :] = jnp.sum(normed_two_grad, axis=0, keepdims=True)
    sums[4:5, :] = jnp.sum(cot_own, axis=0, keepdims=True)
    for k in range(ff_blocks):
        sums[5 + k : 6 + k, my_columns] = r.ubg[0:1, k * LANES : (k + 1) * LANES]
    middle_grad = cot_own + standard_grad(
        normed_two_grad * params[2:3, :], normal, r.rate2[:, 0:1]
    )
    r.tokens_grad[...] = middle_grad
    branch = middle_grad.astype(BF16)
    attended_grad = dot_nt(branch, r.wo[...]).astype(BF16)
    for c in range(CTX):
        r.dat[c] = attended_grad[:, c * columns : (c + 1) * columns]
        r.brs[c] = branch[:, c * columns : (c + 1) * columns]

    def token_swap(src, dst, sems):
        return Exchange(at, lambda c: src.at[c], lambda c: dst.at[rows_of(c, local)], *sems)

    dat_swap = token_swap(r.dat, r.datg, r.dat_sem)
    br_swap = token_swap(r.brs, r.brg, r.br_sem)
    dat_swap.start()
    br_swap.start()
    r.datg[my_tokens, :] = r.dat[me]
    r.brg[my_tokens, :] = r.brs[me]
    att_gather.relays()
    loop(0, 4, lambda g: feed.to_partner(g).start())
    r.dk[...] = jnp.zeros_like(r.dk)
    r.dv[...] = jnp.zeros_like(r.dv)
    dat_swap.waits()

    def attend_back(i):
        rows = rows_of(i, tile)
        grad = r.datg[rows, :]
        both = grad.astype(F32) * r.att[rows, :].astype(F32)
        q = r.q[rows, :]
        query_grad = None
        for h in range(2):
            keep = low if h == 0 else ~low
            delta = jnp.sum(jnp.where(keep, both, 0.0), axis=1, keepdims=True)
            probs = r.probs[h, rows, :]
            prob_grad = dot_nt(grad, r.vm[h])
            score_grad = (probs.astype(F32) * (prob_grad - delta)).astype(BF16)
            term = dot(score_grad, r.km[h])
            query_grad = term if query_grad is None else query_grad + term
            r.dk[...] += dot_tn(score_grad, jnp.where(keep, q, zero_tile))
            r.dv[...] += dot_tn(probs, jnp.where(keep, grad, zero_tile))
        r.pg[rows, :columns] = (query_grad * 0.125).astype(BF16)

    loop(0, seq // tile, attend_back)
    r.pg[:, columns : 2 * columns] = r.dk[...].astype(BF16)
    r.pg[:, 2 * columns :] = r.dv[...].astype(BF16)
    weight_grad(r.dj, r.x1, r.pg)
    dj_planes.start()

    def first_part(g):
        chip = at.chip_at(g)
        part = dot_nt(r.pg[rows_of(chip, tile), :], r.wj[...]).astype(BF16)
        r.first[0][2 * chip] = part[:local]
        r.first[0][2 * chip + 1] = part[local:]
        first.to_partner(g).start()

    loop(0, 4, first_part)
    feed.forwards()
    first.forwards()
    att_gather.waits()
    br_swap.waits()
    weight_grad(r.do, r.attg, r.brg)
    do_planes.start()

    class Owned:
        def __init__(self, number, copies, grad, taken, acc, total, out, sems):
            self.copies, self.grad, self.taken, self.acc, self.total = copies, grad, taken, acc, total
            self.gather = Gather(at, total, lambda c: out.at[c], *sems)
            self.own = pltpu.make_async_copy(total, out.at[me], r.own.at[number])

        def reduce(self):
            self.copies.waits()
            self.acc[...] = self.grad[my_rows, :].astype(F32)

            def add(d):
                self.acc[...] += self.taken[at.plane_at(d)].astype(F32)

            loop(1, planes, add)
            self.total[...] = self.acc[...].astype(BF16)
            self.gather.start()
            self.own.start()

    owned_u = Owned(0, du_planes, r.du, r.ru, r.au, r.tu, r.gu, r.gu_sem)
    owned_o = Owned(1, do_planes, r.do, r.ro, r.ao, r.to, r.go, r.go_sem)
    owned_j = Owned(2, dj_planes, r.dj, r.rj, r.aj, r.tj, r.gj, r.gj_sem)

    full_shard = shard_blocks == CTX
    gd_gather = Gather(
        at, r.td, lambda c: r.gd.at[c], *r.gd_sem
    )
    gd_own = pltpu.make_async_copy(r.td, r.gd.at[down_place], r.own.at[3])

    def gd_copy(d):
        return remote(
            r.td, r.gd.at[down_place], r.gd_sem[0].at[d - 1], r.gd_sem[1].at[down_place], (at.ctx_at(d), f)
        )

    @pl.when(has_down)
    def _():
        def take(d):
            p = at.plane_at(d)
            block = r.rd.at[p]
            remote(block, block, r.dwd_sem[0].at[0], r.dwd_sem[1].at[p], (me, p)).wait_recv()

        loop(1, planes, take)
        total = r.n2
        total[...] = r.dwd[k_own].astype(F32)

        def add(d):
            total[...] += r.rd[at.plane_at(d)].astype(F32)

        loop(1, planes, add)
        r.td[...] = total[...].astype(BF16)
        gd_own.start()
        if not full_shard:
            loop(1, CTX, lambda d: gd_copy(d).start())

    if full_shard:
        gd_gather.start()
    owned_u.reduce()

    feed_total = feed.total()
    r.layer_out[...] = (r.middle[...] + feed_total + params[4:5, :]).astype(BF16)
    owned_j.reduce()

    normed_one_grad = first.total()
    normal, rate = standard(tokens[...].astype(F32))
    sums[0:1, :] = jnp.sum(normed_one_grad * normal, axis=0, keepdims=True)
    sums[1:2, :] = jnp.sum(normed_one_grad, axis=0, keepdims=True)
    r.tokens_grad[...] += standard_grad(
        normed_one_grad * params[0:1, :], normal, rate
    )
    r.sum_s[...] = sums[...].astype(BF16)
    sum_swap = Exchange(
        at, lambda c: r.sum_s, lambda c: r.sum_c.at[c], *r.sumc_sem
    )
    sum_swap.start()
    owned_o.reduce()
    if full_shard:
        gd_gather.relays()
    owned_u.gather.relays()
    sum_swap.waits()

    def add_ctx(d):
        sums[...] += r.sum_c[at.ctx_at(d)].astype(F32)

    loop(1, CTX, add_ctx)
    r.sum_p[...] = sums[...].astype(BF16)
    sum_planes = Planes(
        at, lambda to: r.sum_p, lambda p: r.sum_z.at[p], *r.sumz_sem
    )
    sum_planes.start()
    owned_j.gather.relays()
    owned_o.gather.relays()
    sum_planes.waits()

    def add_planes(d):
        sums[...] += r.sum_z[at.plane_at(d)].astype(F32)

    loop(1, planes, add_planes)
    r.totals[...] = sums[...]

    for each in (owned_u, owned_o, owned_j):
        each.gather.waits()
        each.own.wait()
    if full_shard:
        gd_own.wait()
        gd_gather.waits()
        gd_gather.finish()
    else:

        @pl.when(has_down)
        def _():
            gd_own.wait()
            loop(1, CTX, lambda d: gd_copy(d).wait_send())

        def gd_take(b):
            @pl.when(me != lax.rem(f * shard_blocks + b, CTX))
            def _():
                block = r.gd.at[b]
                remote(
                    block, block, r.gd_sem[0].at[0], r.gd_sem[1].at[b], (at.ctx_at(jnp.int32(1)), f)
                ).wait_recv()

        loop(0, shard_blocks, gd_take)

    @pl.when(has_down)
    def _():
        loop(1, planes, lambda d: wd_copy(d).wait_send())

    def dwd_sent(k):
        @pl.when(down_owner(k) != f)
        def _():
            dwd_copy(k).wait_send()

    loop(0, ff_blocks, dwd_sent)
    for each in (
        tok_gather, cot_gather, wo_gather, x2_gather, att_gather, owned_u.gather, owned_o.gather,
        owned_j.gather, ext_swap, att_swap, dat_swap, br_swap, sum_swap, small_planes, wj_planes,
        wo_planes, wu_planes, du_planes, do_planes, dj_planes, sum_planes, back, feed, first,
    ):
        each.finish()


def shards(
    tokens,
    segment_ids,
    random_blocks,
    global_blocks,
    first_gain,
    first_bias,
    joint_weight,
    output_weight,
    second_gain,
    second_bias,
    up_weight,
    up_bias,
    down_weight,
    down_bias,
    cotangent,
):
    local, width = tokens.shape[1:]
    ctx, planes = lax.axis_size("ctx"), lax.axis_size("fsdp")
    plane = lax.axis_index("fsdp")
    heads = random_blocks.shape[2]
    seq = local * ctx
    blocks = seq // BLOCK
    part_rows = width // planes
    columns = width // ctx
    ff_shard = up_bias.shape[0]
    ff = ff_shard * planes
    ff_blocks = ff // LANES // ctx
    shard_blocks = ff_shard // LANES
    ff_part = ff // ctx
    assert ctx == CTX and columns == LANES and heads == 2 * ctx and blocks + SEGMENTS <= 64
    assert CTX % shard_blocks == 0 and ff // width == ff_blocks

    local_blocks = local // BLOCK
    block_ids = lax.axis_index("ctx") * local_blocks + jnp.arange(local_blocks, dtype=jnp.int32)
    key_ids = jnp.arange(blocks, dtype=jnp.int32)
    window = jnp.abs(key_ids[None, :] - block_ids[:, None]) <= 1
    chosen = jnp.any(key_ids[:, None] == global_blocks[0][None, :], axis=1)
    whole = jnp.any(block_ids[:, None] == global_blocks[0][None, :], axis=1)
    drawn = jnp.any(random_blocks[0][:, :, :, None] == key_ids, axis=2)
    counted = drawn | (window | chosen[None, :] | whole[:, None])[:, None, :]
    code = jnp.where(counted, 0.0, -BIG).astype(BF16)
    code = jnp.broadcast_to(
        code.transpose(1, 0, 2)[:, :, None, :], (heads, local_blocks, BLOCK, blocks)
    ).reshape(heads, local, blocks)
    segment = (
        segment_ids[0][:, None] == jnp.arange(SEGMENTS, dtype=jnp.int32)[None, :]
    ).astype(BF16)
    segment = jnp.broadcast_to(segment[None], (heads, local, SEGMENTS))
    rest = jnp.zeros((heads, local, 64 - blocks - SEGMENTS), BF16)
    extras = jnp.concatenate([code, segment, rest], axis=2).reshape(ctx, 2, local, 64)
    extras = jnp.concatenate([extras[:, 1], extras[:, 0]], axis=2)

    vectors = jnp.stack([first_gain, first_bias, second_gain, second_bias, down_bias])
    small = jnp.zeros((16, width), BF16)
    small = lax.dynamic_update_slice(small, vectors, (0, plane * part_rows))
    flat = lax.dynamic_update_slice(jnp.zeros((ff,), BF16), up_bias, (plane * ff_shard,))
    small = lax.dynamic_update_slice(small, flat.reshape(ff_blocks, width), (5, 0))

    vmem, hbm = pl.BlockSpec(memory_space=pltpu.VMEM), pl.BlockSpec(memory_space=pl.ANY)
    inputs = dict(
        tokens=(tokens[0], vmem),
        cotangent=(cotangent[0], vmem),
        extras=(extras, vmem),
        small=(small, vmem),
        joint=(joint_weight, hbm),
        outw=(output_weight, hbm),
        up=(up_weight, hbm),
        down=(down_weight, hbm),
    )
    outputs = dict(
        layer_out=((local, width), BF16, vmem),
        tokens_grad=((local, width), F32, vmem),
        totals=((16, width), F32, vmem),
        gj=((ctx, part_rows, 3 * columns), BF16, hbm),
        go=((ctx, part_rows, columns), BF16, hbm),
        gu=((ctx, part_rows, ff_part), BF16, hbm),
        gd=((shard_blocks, LANES, width), BF16, hbm),
    )
    dma = lambda n: pltpu.SemaphoreType.DMA((n,))
    v16 = lambda *shape: pltpu.VMEM(shape, BF16)
    v32 = lambda *shape: pltpu.VMEM(shape, F32)
    others = max(planes - 1, 1)
    scatter = (
        v16(ctx, local, width), v16(4, local, width), v16(3, local, width),
        dma(4), dma(4), dma(3), dma(3),
    )
    gather, swap, plane_sems = (dma(7), dma(ctx)), (dma(ctx - 1), dma(ctx)), (dma(others), dma(planes))
    scratch = dict(
        wj=v16(width, 3 * columns), wo=v16(width, width), wu=v16(width, ff_part),
        wd=v16(ff_part, width), tokg=v16(seq, width), cotg=v16(seq, width),
        x1=v16(seq, width), x2=v16(seq, width), attg=v16(seq, width),
        extg=v16(seq, columns), smallg=v16(planes, 16, width), params=v32(16, width),
        ub=v32(1, ff_part), ubg=v32(1, ff_part), q=v16(seq, columns),
        qa=v16(2, seq, columns), ka=v16(2, seq, columns), km=v16(2, seq, columns),
        vm=v16(2, seq, columns), probs=v16(2, seq, seq), att=v16(seq, columns),
        attx=v16(ctx, local, columns), middle=v32(local, width), n2=v32(local, width),
        rate2=v32(local, LANES), hidden=v16(seq, ff_part),
        upg=v16(seq, ff_part), dat=v16(ctx, local, columns), brs=v16(ctx, local, columns),
        datg=v16(seq, columns), brg=v16(seq, columns), dk=v32(seq, columns),
        dv=v32(seq, columns), pg=v16(seq, 3 * columns), sums=v32(16, width),
        sum_s=v16(16, width), sum_p=v16(16, width), sum_c=v16(ctx, 16, width),
        sum_z=v16(planes, 16, width),
        dj=v16(width, 3 * columns), do=v16(width, columns), du=v16(width, ff_part),
        dwd=v16(ff_blocks, LANES, width),
        rj=v16(planes, part_rows, 3 * columns), ro=v16(planes, part_rows, columns),
        ru=v16(planes, part_rows, ff_part), rd=v16(planes, LANES, width),
        aj=v32(part_rows, 3 * columns), ao=v32(part_rows, columns), au=v32(part_rows, ff_part),
        tj=v16(part_rows, 3 * columns), to=v16(part_rows, columns),
        tu=v16(part_rows, ff_part), td=v16(LANES, width),
        stage=dma(5 + ff_blocks), own=dma(4), wd_sem=(dma(others), dma(ff_blocks)),
        dwd_sem=(dma(ff_blocks), dma(planes)), back=scatter, feed=scatter, first=scatter,
        tok_sem=gather, cot_sem=gather, wog_sem=gather, x2_sem=gather, attg_sem=gather,
        gj_sem=gather, go_sem=gather, gu_sem=gather, gd_sem=gather,
        ext_sem=swap, att_sem=swap, dat_sem=swap, br_sem=swap, sumc_sem=swap,
        small_sem=plane_sems, wj_sem=plane_sems, wo_sem=plane_sems, wu_sem=plane_sems,
        dj_sem=plane_sems, do_sem=plane_sems, du_sem=plane_sems, sumz_sem=plane_sems,
    )
    shapes, scratch_tree = jax.tree.flatten(scratch)
    ins, outs = len(inputs), len(outputs)

    def kernel(*refs):
        held = dict(zip([*inputs, *outputs], refs, strict=False))
        held |= jax.tree.unflatten(scratch_tree, refs[ins + outs :])
        layer_kernel(types.SimpleNamespace(**held), planes)

    layer_out, tokens_grad, totals, gj, go, gu, gd = pl.pallas_call(
        kernel,
        out_shape=[jax.ShapeDtypeStruct(shape, dtype) for shape, dtype, _ in outputs.values()],
        in_specs=[spec for _, spec in inputs.values()],
        out_specs=[spec for *_, spec in outputs.values()],
        scratch_shapes=shapes,
        compiler_params=pltpu.CompilerParams(
            collective_id=0, has_side_effects=True, vmem_limit_bytes=60 * 1024 * 1024
        ),
    )(*(value for value, _ in inputs.values()))

    def spread(blocks_of, groups):
        parts = blocks_of.astype(F32).reshape(ctx, part_rows, groups, columns)
        return parts.transpose(1, 2, 0, 3).reshape(part_rows, groups * ctx * columns)

    mine = lax.dynamic_slice(totals[:5], (0, plane * part_rows), (5, part_rows))
    bias = lax.dynamic_slice(totals[5 : 5 + ff_blocks].reshape(ff), (plane * ff_shard,), (ff_shard,))
    return (
        layer_out[None],
        tokens_grad[None],
        mine[0],
        mine[1],
        spread(gj, 3),
        spread(go, 1),
        mine[2],
        mine[3],
        spread(gu, ff_blocks),
        bias,
        gd.astype(F32).reshape(ff_shard, width),
        mine[4],
    )


def solution(mesh):
    in_specs = (
        P("fsdp", "ctx", None),
        P("fsdp", "ctx"),
        P("fsdp", "ctx", None, None),
        P("fsdp", None),
        P("fsdp"),
        P("fsdp"),
        P("fsdp", None),
        P("fsdp", None),
        P("fsdp"),
        P("fsdp"),
        P("fsdp", None),
        P("fsdp"),
        P("fsdp", None),
        P("fsdp"),
        P("fsdp", "ctx", None),
    )
    out_specs = (
        P("fsdp", "ctx", None),
        P("fsdp", "ctx", None),
        P("fsdp"),
        P("fsdp"),
        P("fsdp", None),
        P("fsdp", None),
        P("fsdp"),
        P("fsdp"),
        P("fsdp", None),
        P("fsdp"),
        P("fsdp", None),
        P("fsdp"),
    )
    return jax.shard_map(shards, mesh=mesh, in_specs=in_specs, out_specs=out_specs, check_vma=False)
```

time: 1850 us -> 236 us (0.13)
  waiting for transfers between devices: 1340 us -> 0 us
  Pallas kernels: 0 us -> 193 us
  other arithmetic: 134 us -> 6.36 us
  blocking collectives: 114 us -> 0 us
  matrix products: 109 us -> 0 us
  local copies, waits for them, and re-layouts: 130 us -> 35.2 us
    all_gather x9 -> x0, waiting for transfers between devices: 749 us -> none  [the longest x1 140 us: shards(): lax.all_gather(feed_local[4], 'fsdp', axis=0, tiled=True)]
    reduce_scatter x6 -> x0, waiting for transfers between devices: 517 us -> none  [the longest x1 148 us: shards(): lax.psum_scatter(down_weight_grad.astype(jnp.bfloat16), 'fsdp', scatter_d...]
    pallas_call x0 -> x1, Pallas kernels: none -> 193 us  [shards(): pl.pallas_call(kernel, out_shape=[jax.ShapeDtypeStruct(shape, dtype) for...]
    dot_general x18 -> x0, matrix products: 109 us -> none  [the longest x4 26.7 us: contract_cols(): lax.dot_general(left, right, (((1,), (1,)), ((), ())), preferred_element_...]
    all_gather x9 -> x0, blocking collectives: 84.4 us -> none  [the longest x1 12.6 us: shards(): lax.all_gather(first_bias, 'fsdp', axis=0, tiled=True)]
    scatter-add x2 -> x0, other arithmetic: 82.1 us -> none  [the longest x1 41.1 us: shards(): values_grad = jnp.zeros((block_count, BLOCK, heads, head_size), jnp.float...]
    psum x1 -> x0, waiting for transfers between devices: 67.7 us -> none  [shards(): lax.psum(for_sending(tuple(owner_sums)), 'ctx')]
    another operation x16 -> x6, local copies, waits for them, and re-layouts: 40.2 us -> 3.32 us  [shards(): jnp.stack([first_gain, first_bias, second_gain, second_bias, down_bias])]
  transfers between devices with their start and end apart: 16 -> 0, of which waited for: 14 -> 0; matrix products, arithmetic and copies ran while one was open for 9% -> 0% of each run, Pallas kernels for 0% -> 0%
where the time goes in v1:
time: 236 us
  Pallas kernels  193 us (82%)
  local copies, waits for them, and re-layouts  35.2 us (15%)
  other arithmetic  6.36 us (3%)
    pallas_call x1, Pallas kernels, shards(): pl.pallas_call(kernel, out_shape=[jax.ShapeDtypeStruct(shape, dtype) for...  193 us
    reshape x5, local copies, waits for them, and re-layouts, spread(): parts.transpose(1, 2, 0, 3).reshape(part_rows, groups * ctx * columns)  13.3 us
    unnamed x17, local copies, waits for them, and re-layouts  13.2 us

profile of v1, /device:TPU:0, one launch (start us, length us, event | category | flops | bytes accessed | tf_op | source)
XLA Modules:
  0.0 235.6 jit_solution(9059435509812175072)
XLA Ops:
  0.6 0.7 stack.18
  1.3 0.7 stack.19
  2.0 0.7 stack.20
  2.6 0.7 stack.21
  3.3 0.7 stack.22
  4.5 0.9 dynamic_update_slice.10
  5.6 0.8 compare_reduce_fusion
  6.5 0.7 compare_reduce_fusion.1
  7.3 0.7 copy.45
  9.0 0.7 fusion
  10.3 0.9 pad_maximum_fusion.refs_2_
  11.2 193.2 %shard_map.238 = (bf16[128,1024]{1,0:T(8,128)(2,1)}, f32[128,1024]{1,0:T(8,128)}, f32[16,1024]{1,0:T(8,128)}, bf16[8,256,384]{2,1,0:T(8,128)(2,1)}, bf16[8,256,1...) custom-call(bf16[128,1024]{1,0:T(8,128)(2,1)} %bitcast.51, ...), custom_call_target="tpu_custom_call" | custom-call | tf_op jit(solution)/shard_map/pallas_call | solution.py:890
  204.4 0.8 slice.29
  205.8 0.8 slice_bitcast_fusion.2
  207.3 4.7 %reshape.171 = f32[8,256,4,128]{3,2,1,0:T(4,128)} reshape(bf16[8,256,512]{2,1,0:T(8,128)(2,1)} %get-tuple-element.24) | data formatting | bytes 6291456 | tf_op jit(solution)/shard_map/reshape | solution.py:903
  212.0 4.6 %copy.51 = f32[256,4,8,128]{3,2,1,0:T(8,128)S(1)} copy(f32[256,4,8,128]{3,1,0,2:T(4,128)} %bitcast.44) | data formatting | bytes 8388608 | tf_op jit(solution)/shard_map/reshape | solution.py:903
  216.6 5.8 %copy.58 = f32[32,8,32,128]{3,1,2,0:T(8,128)} copy(f32[32,8,32,128]{3,2,1,0:T(8,128)S(1)} %bitcast.45) | data formatting | bytes 8388608
  222.4 1.7 copy.48
  224.1 1.9 copy.49
  226.1 3.7 %copy.52 = f32[256,3072]{1,0:T(8,128)} copy(f32[256,3072]{0,1:T(8,128)} %bitcast.47) | data formatting | bytes 6291456
  229.7 2.6 %bitcast_convert_fusion = f32[1024,1024]{1,0:T(8,128)} fusion(bf16[8,128,1024]{2,1,0:T(8,128)(2,1)S(1)} %copy-done), kind=kLoop, calls=%fused_computation.1 | loop fusion | flops 1048576 | bytes 6291456 | tf_op jit(solution)/shard_map/reshape | solution.py:918
  232.8 1.3 copy.53
  234.1 0.7 copy.65
  234.8 0.8 copy.66
  (34 shorter events, 4.0 us)
Async XLA Ops:
  5.6 5.6 %copy-start.4 = (bf16[16,1024]{1,0:T(8,128)(2,1)}, bf16[16,1024]{1,0:T(8,128)(2,1)S(1)}, u32[]{:S(2)}) copy-start(bf16[16,1024]{1,0:T(8,128)(2,1)S(1)} %dynamic_update_slice.11.refs_3_) | copy-start | bytes 98308
  226.0 3.7 %copy-start = (bf16[8,128,1024]{2,1,0:T(8,128)(2,1)S(1)}, bf16[8,128,1024]{2,1,0:T(8,128)(2,1)}, u32[]{:S(2)}) copy-start(bf16[8,128,1024]{2,1,0:T(8,128)(2,1)} %get-tuple-element.25) | copy-start | bytes 6291460
  229.7 2.6 %copy-start.1 = (bf16[8,256,128]{2,1,0:T(8,128)(2,1)S(1)}, bf16[8,256,128]{2,1,0:T(8,128)(2,1)}, u32[]{:S(2)}) copy-start(bf16[8,256,128]{2,1,0:T(8,128)(2,1)} %get-tuple-element.23) | copy-start | bytes 1572868
  232.4 1.7 copy-start.3
  232.4 2.4 %copy-start.2 = (f32[128,1024]{1,0:T(8,128)S(1)}, f32[128,1024]{1,0:T(8,128)}, u32[]{:S(2)}) copy-start(f32[128,1024]{1,0:T(8,128)} %get-tuple-element.20) | copy-start | bytes 1572868

commit v2 on v1

--- a/solution.py
+++ b/solution.py
@@ -235,10 +235,37 @@
     )
 
 
+def write_extras(r, at, seq):
+    local = r.segments.shape[1]
+    blocks, local_blocks = seq // BLOCK, local // BLOCK
+    heads = r.random.shape[1]
+    half = LANES // 2
+    key = lax.rem(lax.broadcasted_iota(jnp.int32, (heads, LANES), 1), half)
+    lower = lax.broadcasted_iota(jnp.int32, (1, LANES), 1) < half
+    place = lax.rem(lax.broadcasted_iota(jnp.int32, (LANES, local), 0), half)
+    hot = jnp.where(r.segments[...] == place - blocks, 1.0, 0.0).T
+    hot = jnp.where(key[0:1] >= blocks + SEGMENTS, 0.0, hot)
+    pair = r.globals[...]
+    for b in range(local_blocks):
+        block = at.c * local_blocks + b
+        drawn = r.random[b]
+        counted = jnp.abs(key - block) <= 1
+        for j in range(drawn.shape[1]):
+            counted = counted | (key == drawn[:, j : j + 1])
+        for j in range(pair.shape[1]):
+            chosen = pair[:, j : j + 1]
+            counted = counted | (key == chosen) | (chosen == block)
+        code = jnp.where(counted | (key >= blocks), 0.0, -BIG)
+        rows = slice(b * BLOCK, (b + 1) * BLOCK)
+        for d in range(heads // 2):
+            both = jnp.where(lower, code[2 * d + 1 : 2 * d + 2], code[2 * d : 2 * d + 1])
+            r.extras[d, rows, :] = (both + hot[rows]).astype(BF16)
+
+
 def layer_kernel(r, planes):
     at = Place(planes)
     me, f = at.c, at.f
-    tokens, cotangent, extras, small = r.tokens, r.cotangent, r.extras, r.small
+    tokens, cotangent = r.tokens, r.cotangent
     local, width = tokens.shape
     seq = local * CTX
     part_rows = width // planes
@@ -291,6 +318,19 @@
     def _():
         down_copy.start()
 
+    small, wide, shard = r.small, r.sums, ff // planes
+    wide[...] = jnp.zeros_like(wide)
+    for i, vector in enumerate((r.gain_one, r.bias_one, r.gain_two, r.bias_two, r.bias_down)):
+        wide[i : i + 1, 0:part_rows] = vector[...].astype(F32).reshape(1, part_rows)
+    wide[8:9, 0:shard] = r.bias_up[...].astype(F32).reshape(1, shard)
+    vectors = pltpu.roll(wide[0:8, :], f * part_rows, axis=1)
+    bias_row = lax.div(f * shard, width)
+    bias = pltpu.roll(wide[8:16, :], lax.rem(f * shard, width), axis=1)[0:1]
+    row = lax.broadcasted_iota(jnp.int32, (16, width), 0)
+    small[...] = jnp.where(
+        row == 5 + bias_row, bias, jnp.concatenate([vectors, jnp.zeros_like(vectors)], axis=0)
+    ).astype(BF16)
+
     barrier = pltpu.get_barrier_semaphore()
     loop(
         1,
@@ -316,7 +356,7 @@
     )
     ext_swap = Exchange(
         at,
-        lambda c: extras.at[c],
+        lambda c: r.extras.at[c],
         lambda c: r.extg.at[rows_of(c, local)],
         *r.ext_sem,
     )
@@ -343,6 +383,7 @@
 
     small_planes.start()
     tok_gather.start()
+    write_extras(r, at, seq)
     ext_swap.start()
     for copy in stage[:3]:
         copy.wait()
@@ -352,7 +393,7 @@
 
     r.tokg[my_tokens, :] = tokens[...]
     r.cotg[my_tokens, :] = cotangent[...]
-    r.extg[my_tokens, :] = extras[me]
+    r.extg[my_tokens, :] = r.extras[me]
     r.smallg[f] = small[...]
     small_planes.waits()
     params = r.params
@@ -717,7 +758,15 @@
         sums[...] += r.sum_z[at.plane_at(d)].astype(F32)
 
     loop(1, planes, add_planes)
-    r.totals[...] = sums[...]
+    r.totals[0:8, :] = pltpu.roll(
+        sums[0:8, :], lax.rem((planes - f) * part_rows, width), axis=1
+    )
+    bias_total = jnp.sum(
+        jnp.where(row == 5 + bias_row, sums[...], 0.0), axis=0, keepdims=True
+    )
+    r.totals[8:16, :] = pltpu.roll(
+        jnp.broadcast_to(bias_total, (8, width)), width - lax.rem(f * shard, width), axis=1
+    )
 
     for each in (owned_u, owned_o, owned_j):
         each.gather.waits()
@@ -780,7 +829,6 @@
 ):
     local, width = tokens.shape[1:]
     ctx, planes = lax.axis_size("ctx"), lax.axis_size("fsdp")
-    plane = lax.axis_index("fsdp")
     heads = random_blocks.shape[2]
     seq = local * ctx
     blocks = seq // BLOCK
@@ -794,38 +842,19 @@
     assert ctx == CTX and columns == LANES and heads == 2 * ctx and blocks + SEGMENTS <= 64
     assert CTX % shard_blocks == 0 and ff // width == ff_blocks
 
-    local_blocks = local // BLOCK
-    block_ids = lax.axis_index("ctx") * local_blocks + jnp.arange(local_blocks, dtype=jnp.int32)
-    key_ids = jnp.arange(blocks, dtype=jnp.int32)
-    window = jnp.abs(key_ids[None, :] - block_ids[:, None]) <= 1
-    chosen = jnp.any(key_ids[:, None] == global_blocks[0][None, :], axis=1)
-    whole = jnp.any(block_ids[:, None] == global_blocks[0][None, :], axis=1)
-    drawn = jnp.any(random_blocks[0][:, :, :, None] == key_ids, axis=2)
-    counted = drawn | (window | chosen[None, :] | whole[:, None])[:, None, :]
-    code = jnp.where(counted, 0.0, -BIG).astype(BF16)
-    code = jnp.broadcast_to(
-        code.transpose(1, 0, 2)[:, :, None, :], (heads, local_blocks, BLOCK, blocks)
-    ).reshape(heads, local, blocks)
-    segment = (
-        segment_ids[0][:, None] == jnp.arange(SEGMENTS, dtype=jnp.int32)[None, :]
-    ).astype(BF16)
-    segment = jnp.broadcast_to(segment[None], (heads, local, SEGMENTS))
-    rest = jnp.zeros((heads, local, 64 - blocks - SEGMENTS), BF16)
-    extras = jnp.concatenate([code, segment, rest], axis=2).reshape(ctx, 2, local, 64)
-    extras = jnp.concatenate([extras[:, 1], extras[:, 0]], axis=2)
-
-    vectors = jnp.stack([first_gain, first_bias, second_gain, second_bias, down_bias])
-    small = jnp.zeros((16, width), BF16)
-    small = lax.dynamic_update_slice(small, vectors, (0, plane * part_rows))
-    flat = lax.dynamic_update_slice(jnp.zeros((ff,), BF16), up_bias, (plane * ff_shard,))
-    small = lax.dynamic_update_slice(small, flat.reshape(ff_blocks, width), (5, 0))
-
     vmem, hbm = pl.BlockSpec(memory_space=pltpu.VMEM), pl.BlockSpec(memory_space=pl.ANY)
     inputs = dict(
         tokens=(tokens[0], vmem),
         cotangent=(cotangent[0], vmem),
-        extras=(extras, vmem),
-        small=(small, vmem),
+        segments=(segment_ids, vmem),
+        random=(random_blocks[0], vmem),
+        globals=(global_blocks, vmem),
+        gain_one=(first_gain, vmem),
+        bias_one=(first_bias, vmem),
+        gain_two=(second_gain, vmem),
+        bias_two=(second_bias, vmem),
+        bias_up=(up_bias, vmem),
+        bias_down=(down_bias, vmem),
         joint=(joint_weight, hbm),
         outw=(output_weight, hbm),
         up=(up_weight, hbm),
@@ -853,7 +882,7 @@
         wj=v16(width, 3 * columns), wo=v16(width, width), wu=v16(width, ff_part),
         wd=v16(ff_part, width), tokg=v16(seq, width), cotg=v16(seq, width),
         x1=v16(seq, width), x2=v16(seq, width), attg=v16(seq, width),
-        extg=v16(seq, columns), smallg=v16(planes, 16, width), params=v32(16, width),
+        extras=v16(ctx, local, columns), small=v16(16, width), extg=v16(seq, columns), smallg=v16(planes, 16, width), params=v32(16, width),
         ub=v32(1, ff_part), ubg=v32(1, ff_part), q=v16(seq, columns),
         qa=v16(2, seq, columns), ka=v16(2, seq, columns), km=v16(2, seq, columns),
         vm=v16(2, seq, columns), probs=v16(2, seq, seq), att=v16(seq, columns),
@@ -898,25 +927,70 @@
         ),
     )(*(value for value, _ in inputs.values()))
 
-    def spread(blocks_of, groups):
-        parts = blocks_of.astype(F32).reshape(ctx, part_rows, groups, columns)
-        return parts.transpose(1, 2, 0, 3).reshape(part_rows, groups * ctx * columns)
-
-    mine = lax.dynamic_slice(totals[:5], (0, plane * part_rows), (5, part_rows))
-    bias = lax.dynamic_slice(totals[5 : 5 + ff_blocks].reshape(ff), (plane * ff_shard,), (ff_shard,))
+    group = 4
+
+    def spread(ref, out):
+        for q in range(group):
+            out[:, q * columns : (q + 1) * columns] = ref[q].astype(F32)
+
+    def finish(totals, gj, go, gu, gd, joint, outw, up, down, *vectors):
+        for ref, out in ((gj, joint), (go, outw), (gu, up)):
+            spread(ref, out)
+        down[...] = gd[0].astype(F32)
+        for i, out in enumerate(vectors[:5]):
+            out[...] = totals[i : i + 1, 0:part_rows].reshape(part_rows)
+        vectors[5][...] = totals[8:9, 0:ff_shard].reshape(ff_shard)
+
+    quads = ctx // group
+    steps = ff_blocks * quads
+
+    def spec_pair(groups):
+        last = groups * quads - 1
+        place = lambda i: jnp.minimum(i, last)
+        return (
+            pl.BlockSpec(
+                (group, part_rows, columns), lambda i: (place(i) % quads, 0, place(i) // quads)
+            ),
+            pl.BlockSpec((part_rows, group * columns), lambda i: (0, place(i))),
+        )
+
+    pairs = [spec_pair(3), spec_pair(1), spec_pair(ff_blocks)]
+    down_place = lambda i: jnp.minimum(i, shard_blocks - 1)
+    whole = pl.BlockSpec(memory_space=pltpu.VMEM)
+    made = pl.pallas_call(
+        finish,
+        grid=(steps,),
+        out_shape=[
+            jax.ShapeDtypeStruct(shape, F32)
+            for shape in (
+                (part_rows, 3 * width), (part_rows, width), (part_rows, ff), (ff_shard, width),
+                *([(part_rows,)] * 5), (ff_shard,),
+            )
+        ],
+        in_specs=[
+            whole,
+            *(pair[0] for pair in pairs),
+            pl.BlockSpec((1, LANES, width), lambda i: (down_place(i), 0, 0)),
+        ],
+        out_specs=[
+            *(pair[1] for pair in pairs),
+            pl.BlockSpec((LANES, width), lambda i: (down_place(i), 0)),
+            *([whole] * 6),
+        ],
+    )(totals, gj, go, gu, gd)
     return (
         layer_out[None],
         tokens_grad[None],
-        mine[0],
-        mine[1],
-        spread(gj, 3),
-        spread(go, 1),
-        mine[2],
-        mine[3],
-        spread(gu, ff_blocks),
-        bias,
-        gd.astype(F32).reshape(ff_shard, width),
-        mine[4],
+        made[4],
+        made[5],
+        made[0],
+        made[1],
+        made[6],
+        made[7],
+        made[2],
+        made[9],
+        made[3],
+        made[8],
     )
 
 

time: 236 us -> 206 us (0.87)
  local copies, waits for them, and re-layouts: 35.2 us -> 2.88 us
  Pallas kernels: 193 us -> 202 us
  other arithmetic: 6.36 us -> 0 us
    reshape x6 -> x0, local copies, waits for them, and re-layouts: 13.3 us -> none  [the longest x5 13.3 us: spread(): parts.transpose(1, 2, 0, 3).reshape(part_rows, groups * ctx * columns)]
    unnamed x17 -> x6, local copies, waits for them, and re-layouts: 13.2 us -> 1.51 us
    pallas_call x0 -> x1, Pallas kernels: none -> 9.25 us  [shards(): pl.pallas_call(finish, grid=(steps,), out_shape=[jax.ShapeDtypeStruct(sha...]
    another operation x6 -> x0, local copies, waits for them, and re-layouts: 3.32 us -> none  [shards(): jnp.stack([first_gain, first_bias, second_gain, second_bias, down_bias])]
    reshape x2 -> x0, other arithmetic: 2.68 us -> none  [the longest x1 2.61 us: shards(): gd.astype(F32).reshape(ff_shard, width)]
where the time goes in v2:
time: 206 us
  Pallas kernels  202 us (98%)
  local copies, waits for them, and re-layouts  2.88 us (1%)
    pallas_call x1, Pallas kernels, shards(): pl.pallas_call(kernel, out_shape=[jax.ShapeDtypeStruct(shape, dtype) for...  193 us
    pallas_call x1, Pallas kernels, shards(): pl.pallas_call(finish, grid=(steps,), out_shape=[jax.ShapeDtypeStruct(sha...  9.25 us

profile of v2, /device:TPU:0, one launch (start us, length us, event | category | flops | bytes accessed | tf_op | source)
XLA Modules:
  0.0 205.9 jit_solution(10458004083375295017)
XLA Ops:
  0.6 1.4 copy.27.refs_3_
  2.0 193.1 %shard_map.238 = (bf16[128,1024]{1,0:T(8,128)(2,1)}, f32[128,1024]{1,0:T(8,128)}, f32[16,1024]{1,0:T(8,128)}, bf16[8,256,384]{2,1,0:T(8,128)(2,1)}, bf16[8,256,1...) custom-call(bf16[128,1024]{1,0:T(8,128)(2,1)} %bitcast.7, ...), custom_call_target="tpu_custom_call" | custom-call | tf_op jit(solution)/shard_map/pallas_call | solution.py:919
  195.1 0.0 copy-start.1
  195.1 0.0 copy-start
  195.1 9.2 %shard_map.239 = (f32[256,3072]{1,0:T(8,128)}, f32[256,1024]{1,0:T(8,128)}, f32[256,4096]{1,0:T(8,128)}, f32[1024,1024]{1,0:T(8,128)}, f32[256]{0:T(256)}, /*ind...) custom-call(f32[16,1024]{1,0:T(8,128)} %get-tuple-element.31.totals, ...), custom_call_target="tpu_custom_call" | custom-call | tf_op jit(solution)/shard_map/pallas_call | solution.py:960
  204.4 0.0 copy-done.1
  204.4 0.7 copy.30
  205.1 0.0 copy-done
  205.1 0.8 copy.31
Async XLA Ops:
  195.1 9.3 %copy-start.1 = (bf16[128,1024]{1,0:T(8,128)(2,1)S(1)}, bf16[128,1024]{1,0:T(8,128)(2,1)}, u32[]{:S(2)}) copy-start(bf16[128,1024]{1,0:T(8,128)(2,1)} %get-tuple-element.29) | copy-start | bytes 786436
  195.1 10.0 %copy-start = (f32[128,1024]{1,0:T(8,128)S(1)}, f32[128,1024]{1,0:T(8,128)}, u32[]{:S(2)}) copy-start(f32[128,1024]{1,0:T(8,128)} %get-tuple-element.30) | copy-start | bytes 1572868

commit v3 on v2

--- a/solution.py
+++ b/solution.py
@@ -80,20 +80,31 @@
     def __init__(self, at, src, slot, send, recv):
         self.at, self.src, self.slot, self.send, self.recv = at, src, slot, send, recv
 
+    def half(self, c, i):
+        block = self.slot(c)
+        size = block.shape[0] // 2
+        return block.at[pl.ds(i * size, size)]
+
     def direct(self, i):
         at = self.at
         to = at.partner if i == 0 else at.same(jnp.int32(i))
         return remote(self.src, self.slot(at.c), self.send.at[i], self.recv.at[at.c], (to, at.f))
 
+    def across(self, i):
+        at = self.at
+        c, to = at.same(jnp.int32(1 + i)), at.same(jnp.int32(2 - i))
+        block = self.half(c, i)
+        recv = self.recv.at[c] if i == 0 else self.recv.at[CTX]
+        return remote(block, block, self.send.at[3 + i], recv, (to, at.f))
+
     def passed(self, g):
         at = self.at
-        block = self.slot(at.same(g))
-        return remote(
-            block, block, self.send.at[3 + g], self.recv.at[at.same(g)], (at.partner, at.f)
-        )
+        c = at.same(jnp.int32(g))
+        block = self.slot(c)
+        return remote(block, block, self.send.at[4 + g], self.recv.at[c], (at.partner, at.f))
 
     def start(self):
-        for i in range(4):
+        for i in (1, 2, 0):
             self.direct(i).start()
 
     def wait(self, c):
@@ -101,20 +112,32 @@
         block = self.slot(c)
         remote(block, block, self.send.at[0], self.recv.at[c], (at.partner, at.f)).wait_recv()
 
-    def relay(self, g):
-        self.wait(self.at.same(g))
-        self.passed(g).start()
-
-    def relays(self):
-        loop(1, 4, self.relay)
+    def near(self):
+        for i in range(2):
+            self.wait(self.at.same(jnp.int32(1 + i)))
+            self.across(i).start()
+        for g in (1, 2):
+            self.passed(g).start()
+
+    def far(self):
+        at = self.at
+        for i in range(2):
+            c = at.same(jnp.int32(3))
+            block = self.half(c, i)
+            recv = self.recv.at[c] if i == 0 else self.recv.at[CTX]
+            remote(block, block, self.send.at[0], recv, (at.partner, at.f)).wait_recv()
+        self.passed(3).start()
 
     def waits(self):
         loop(0, 4, lambda g: self.wait(self.at.other(g)))
 
     def finish(self):
-        for i in range(4):
+        for i in range(3):
             self.direct(i).wait_send()
-        loop(1, 4, lambda g: self.passed(g).wait_send())
+        for i in range(2):
+            self.across(i).wait_send()
+        for g in (1, 2, 3):
+            self.passed(g).wait_send()
 
 
 class Exchange:
@@ -171,11 +194,134 @@
         loop(1, self.at.planes, lambda d: self.copy(d).wait_send())
 
 
+class Line:
+    def __init__(self, at, items, owner, view, send, recv):
+        self.at, self.items, self.owner, self.view = at, items, owner, view
+        self.send, self.recv = send, recv
+
+    def hop(self, i, up):
+        at, block = self.at, self.view(i)
+        to = jnp.minimum(at.f + 1, at.planes - 1) if up else jnp.maximum(at.f - 1, 0)
+        return remote(
+            block, block, self.send.at[2 * i + (1 if up else 0)], self.recv.at[i], (at.c, to)
+        )
+
+    def outward(self, i, act):
+        at, owner = self.at, self.owner(i)
+
+        @pl.when((owner <= at.f) & (at.f < at.planes - 1))
+        def _():
+            act(self.hop(i, True))
+
+        @pl.when((owner >= at.f) & (at.f > 0))
+        def _():
+            act(self.hop(i, False))
+
+    def start(self):
+        def each(i):
+            @pl.when(self.owner(i) == self.at.f)
+            def _():
+                self.outward(i, lambda copy: copy.start())
+
+        loop(0, self.items, each)
+
+    def arrive(self, i):
+        self.hop(i, True).wait_recv()
+        self.outward(i, lambda copy: copy.start())
+
+    def passes(self, d):
+        def each(i):
+            owner = self.owner(i)
+
+            @pl.when((owner == self.at.f + d) | (owner == self.at.f - d))
+            def _():
+                self.arrive(i)
+
+        loop(0, self.items, each)
+
+    def passes_at(self, d):
+        if d < self.at.planes:
+            self.passes(d)
+
+    def rest(self, d):
+        loop(d, self.at.planes, self.passes)
+
+    def finish(self):
+        loop(0, self.items, lambda i: self.outward(i, lambda copy: copy.wait_send()))
+
+
+class Toward:
+    def __init__(self, at, items, owner, part, taken, send, recv):
+        self.at, self.items, self.owner, self.part, self.taken = at, items, owner, part, taken
+        self.send, self.recv = send, recv
+
+    def hop(self, i, up):
+        at = self.at
+        to = jnp.minimum(at.f + 1, at.planes - 1) if up else jnp.maximum(at.f - 1, 0)
+        slot = i + 1 if up else i
+        return remote(
+            self.part(i), self.taken.at[slot], self.send.at[i], self.recv.at[slot], (at.c, to)
+        )
+
+    def step(self, d):
+        at = self.at
+
+        def one(i, up, comes):
+            @pl.when(comes)
+            def _():
+                self.hop(i, up).wait_recv()
+                block = self.part(i)
+                come = self.taken[i + 1 if up else i].astype(F32)
+                block[...] = (block[...].astype(F32) + come).astype(BF16)
+
+            self.hop(i, up).start()
+
+        def each(i):
+            @pl.when(self.owner(i) == at.f + d)
+            def _():
+                one(i, True, at.f > 0)
+
+            @pl.when(self.owner(i) == at.f - d)
+            def _():
+                one(i, False, at.f < at.planes - 1)
+
+        loop(0, self.items, each)
+
+    def first(self, d):
+        loop(d, self.at.planes, lambda j: self.step(self.at.planes - 1 + d - j))
+
+    def total(self, i, acc):
+        at = self.at
+        acc[...] = self.part(i)[...].astype(F32)
+
+        @pl.when(at.f > 0)
+        def _():
+            self.hop(i, True).wait_recv()
+            acc[...] += self.taken[i + 1].astype(F32)
+
+        @pl.when(at.f < at.planes - 1)
+        def _():
+            self.hop(i, False).wait_recv()
+            acc[...] += self.taken[i].astype(F32)
+
+    def finish(self):
+        def each(i):
+            @pl.when(self.owner(i) > self.at.f)
+            def _():
+                self.hop(i, True).wait_send()
+
+            @pl.when(self.owner(i) < self.at.f)
+            def _():
+                self.hop(i, False).wait_send()
+
+        loop(0, self.items, each)
+
+
 class Scatter:
-    def __init__(self, at, part, pair, far, pair_send, pair_recv, far_send, far_recv):
-        self.at, self.part, self.pair, self.far = at, part, pair, far
-        self.pair_send, self.pair_recv = pair_send, pair_recv
-        self.far_send, self.far_recv = far_send, far_recv
+    def __init__(self, at, part, pair, halves, far, pair_send, pair_recv, send, recv):
+        self.at, self.part, self.pair, self.halves, self.far = at, part, pair, halves, far
+        self.pair_send, self.pair_recv, self.send, self.recv = pair_send, pair_recv, send, recv
+        self.size = part.shape[1] // 2
 
     def to_partner(self, g):
         at = self.at
@@ -187,38 +333,57 @@
             (at.partner, at.f),
         )
 
-    def to_chip(self, g):
+    def across(self, i):
         at = self.at
         return remote(
-            self.part.at[at.same(g)],
-            self.far.at[g - 1],
-            self.far_send.at[g - 1],
-            self.far_recv.at[g - 1],
-            (at.same(g), at.f),
+            self.part.at[at.same(jnp.int32(3)), pl.ds(i * self.size, self.size)],
+            self.halves.at[i],
+            self.send.at[i],
+            self.recv.at[i],
+            (at.same(jnp.int32(1 + i)), at.f),
         )
 
-    def forward(self, g):
-        self.to_partner(g).wait_recv()
-        own = self.at.same(g)
+    def beside(self, i):
+        at = self.at
+        to = at.same(jnp.int32(1 + i))
+        return remote(
+            self.part.at[to], self.far.at[i], self.send.at[2 + i], self.recv.at[2 + i], (to, at.f)
+        )
+
+    def add_pair(self, g):
+        self.to_partner(jnp.int32(g)).wait_recv()
+        own = self.at.same(jnp.int32(g))
         both = self.part[own].astype(F32) + self.pair[g].astype(F32)
         self.part[own] = both.astype(BF16)
-        self.to_chip(g).start()
-
-    def forwards(self):
-        loop(1, 4, self.forward)
+
+    def first(self):
+        self.add_pair(3)
+        for i in range(2):
+            self.across(i).start()
+
+    def second(self):
+        for i in range(2):
+            self.add_pair(1 + i)
+        for i in range(2):
+            self.across(i).wait_recv()
+            to = self.at.same(jnp.int32(2 - i))
+            rows = pl.ds(i * self.size, self.size)
+            both = self.part[to, rows].astype(F32) + self.halves[i].astype(F32)
+            self.part[to, rows] = both.astype(BF16)
+            self.beside(1 - i).start()
 
     def total(self):
-        zero = jnp.int32(0)
-        self.to_partner(zero).wait_recv()
-        loop(1, 4, lambda g: self.to_chip(g).wait_recv())
+        self.to_partner(jnp.int32(0)).wait_recv()
+        for i in range(2):
+            self.beside(i).wait_recv()
         both = self.part[self.at.c].astype(F32) + self.pair[0].astype(F32)
-        return (both + self.far[0].astype(F32)) + (
-            self.far[1].astype(F32) + self.far[2].astype(F32)
-        )
+        return both + (self.far[0].astype(F32) + self.far[1].astype(F32))
 
     def finish(self):
         loop(0, 4, lambda g: self.to_partner(g).wait_send())
-        loop(1, 4, lambda g: self.to_chip(g).wait_send())
+        for i in range(2):
+            self.across(i).wait_send()
+            self.beside(i).wait_send()
 
 
 def standard(values):
@@ -366,7 +531,7 @@
 
     def weight_planes(ref, sems, width_ds):
         view = lambda p: ref.at[rows_of(p, part_rows), width_ds]
-        return Planes(at, lambda to: view(f), view, *sems)
+        return Line(at, planes, lambda i: i, view, *sems)
 
     wj_planes = weight_planes(r.wj, r.wj_sem, slice(None))
     wo_planes = weight_planes(r.wo, r.wo_sem, my_columns)
@@ -376,21 +541,16 @@
         at, wo_block, lambda c: r.wo.at[:, rows_of(c, columns)], *r.wog_sem
     )
 
-    def wd_copy(d):
-        to = at.plane_at(d)
-        block = r.wd.at[rows_of(k_own, LANES), :]
-        return remote(block, block, r.wd_sem[0].at[d - 1], r.wd_sem[1].at[k_own], (me, to))
+    wd_planes = Line(
+        at, ff_blocks, down_owner, lambda k: r.wd.at[rows_of(k, LANES), :], *r.wd_sem
+    )
 
     small_planes.start()
     tok_gather.start()
-    write_extras(r, at, seq)
-    ext_swap.start()
     for copy in stage[:3]:
         copy.wait()
     wj_planes.start()
-    stage[3].wait()
-    wo_planes.start()
-
+    write_extras(r, at, seq)
     r.tokg[my_tokens, :] = tokens[...]
     r.cotg[my_tokens, :] = cotangent[...]
     r.extg[my_tokens, :] = r.extras[me]
@@ -407,9 +567,18 @@
         r.ub[0:1, k * LANES : (k + 1) * LANES] = params[5 + k : 6 + k, my_columns]
 
     def norm_tokens(g):
-        @pl.when(g > 0)
-        def _():
-            tok_gather.relay(g)
+        @pl.when(g == 1)
+        def _():
+            tok_gather.near()
+            ext_swap.start()
+
+        @pl.when(g == 2)
+        def _():
+            wj_planes.passes_at(1)
+
+        @pl.when(g == 3)
+        def _():
+            tok_gather.far()
 
         tok_gather.wait(at.other(g))
         rows = rows_of(at.chip_at(g), 2 * local)
@@ -418,17 +587,17 @@
 
     loop(0, 4, norm_tokens)
     cot_gather.start()
+    wj_planes.passes_at(2)
+    stage[3].wait()
+    wo_planes.start()
+    wj_planes.rest(3)
+    ext_swap.waits()
     for copy in stage[4:]:
         copy.wait()
-    wu_planes.start()
 
     @pl.when(has_down)
     def _():
         down_copy.wait()
-        loop(1, planes, lambda d: wd_copy(d).start())
-
-    ext_swap.waits()
-    wj_planes.waits()
 
     tile = 2 * local
     lane = lax.broadcasted_iota(jnp.int32, (tile, columns), 1)
@@ -462,10 +631,24 @@
         r.vm[1, rows, :] = jnp.where(low, zero_tile, v)
 
     loop(0, seq // tile, project)
-    wo_planes.waits()
-    wo_gather.start()
+    wo_planes.passes_at(1)
 
     def attend(i):
+        @pl.when(i == 1)
+        def _():
+            wo_planes.passes_at(2)
+            wu_planes.start()
+
+        @pl.when(i == 2)
+        def _():
+            wo_planes.rest(3)
+            cot_gather.near()
+
+        @pl.when(i == 3)
+        def _():
+            wo_gather.start()
+            cot_gather.far()
+
         rows = rows_of(i, tile)
         out = None
         for h in range(2):
@@ -486,9 +669,12 @@
         *r.att_sem,
     )
     att_swap.start()
-    cot_gather.relays()
-    wo_gather.relays()
+    wu_planes.passes_at(1)
     r.attx[me] = r.att[my_tokens, :]
+    wo_gather.near()
+    wu_planes.passes_at(2)
+    wd_planes.start()
+    wo_gather.far()
     att_swap.waits()
     for c in range(CTX):
         r.attg[my_tokens, c * columns : (c + 1) * columns] = r.attx[c]
@@ -504,66 +690,67 @@
     x2_gather.start()
     attg_view = lambda c: r.attg.at[rows_of(c, local)]
     att_gather = Gather(at, attg_view(me), attg_view, *r.attg_sem)
-    wu_planes.waits()
-
-    def wd_wait(k):
-        @pl.when(down_owner(k) != f)
-        def _():
-            block = r.wd.at[rows_of(k, LANES), :]
-            remote(block, block, r.wd_sem[0].at[0], r.wd_sem[1].at[k], (me, down_owner(k))).wait_recv()
-
-    loop(0, ff_blocks, wd_wait)
+    wu_planes.rest(3)
 
     back = Scatter(at, *r.back)
     feed = Scatter(at, *r.feed)
     first = Scatter(at, *r.first)
     r.ubg[...] = jnp.zeros_like(r.ubg)
 
-    def feed_forward(g):
-        @pl.when(g > 0)
-        def _():
-            x2_gather.relay(g)
+    def hidden_units(g):
+        @pl.when(g == 1)
+        def _():
+            x2_gather.near()
+
+        @pl.when(g == 3)
+        def _():
+            x2_gather.far()
 
         x2_gather.wait(at.other(g))
         cot_gather.wait(at.other(g))
+        rows = rows_of(at.chip_at(g), tile)
+        up_sum = dot(r.x2[rows, :], r.wu[...]) + r.ub[...]
+        share = 0.5 * (1.0 + lax.erf(up_sum * 0.7071067811865476))
+        r.hidden[rows, :] = (up_sum * share).astype(BF16)
+        r.slope[rows, :] = share + up_sum * jnp.exp(-0.5 * up_sum * up_sum) * 0.3989422804014327
+
+    loop(0, 4, hidden_units)
+    att_gather.start()
+
+    def down_grad(k):
+        r.dwd[k] = dot_tn(r.hidden[:, rows_of(k, LANES)], r.cotg[...]).astype(BF16)
+
+    loop(0, ff_blocks, down_grad)
+    dd_planes = Toward(at, ff_blocks, down_owner, lambda k: r.dwd.at[k], r.rd, *r.dwd_sem)
+    wd_planes.passes_at(1)
+    dd_planes.first(3)
+    wd_planes.passes_at(2)
+    if planes > 2:
+        dd_planes.step(2)
+    att_gather.near()
+    wd_planes.rest(3)
+
+    def feed_back(j):
+        g = jnp.where(j == 0, 3, jnp.where(j == 3, 0, j))
+
+        @pl.when(j == 2)
+        def _():
+            back.first()
+
         chip = at.chip_at(g)
         rows = rows_of(chip, tile)
-        up_sum = dot(r.x2[rows, :], r.wu[...]) + r.ub[...]
-        share = 0.5 * (1.0 + lax.erf(up_sum * 0.7071067811865476))
-        hidden = (up_sum * share).astype(BF16)
-        slope = share + up_sum * jnp.exp(-0.5 * up_sum * up_sum) * 0.3989422804014327
-        r.hidden[rows, :] = hidden
-        up_grad = (dot_nt(r.cotg[rows, :], r.wd[...]) * slope).astype(BF16)
+        up_grad = (dot_nt(r.cotg[rows, :], r.wd[...]) * r.slope[rows, :]).astype(BF16)
         r.upg[rows, :] = up_grad
         r.ubg[...] += jnp.sum(up_grad.astype(F32), axis=0, keepdims=True)
-        back_part = dot_nt(up_grad, r.wu[...]).astype(BF16)
-        r.back[0][2 * chip] = back_part[:local]
-        r.back[0][2 * chip + 1] = back_part[local:]
+        part = dot_nt(up_grad, r.wu[...]).astype(BF16)
+        r.back[0][2 * chip] = part[:local]
+        r.back[0][2 * chip + 1] = part[local:]
         back.to_partner(g).start()
-        feed_part = dot(hidden, r.wd[...]).astype(BF16)
-        r.feed[0][2 * chip] = feed_part[:local]
-        r.feed[0][2 * chip + 1] = feed_part[local:]
-
-    loop(0, 4, feed_forward)
-    back.forwards()
-    att_gather.start()
-
-    def down_grad(k):
-        r.dwd[k] = dot_tn(r.hidden[:, rows_of(k, LANES)], r.cotg[...]).astype(BF16)
-
-    def dwd_copy(k):
-        return remote(
-            r.dwd.at[k], r.rd.at[f], r.dwd_sem[0].at[k], r.dwd_sem[1].at[f], (me, down_owner(k))
-        )
-
-    def dwd_send(k):
-        down_grad(k)
-
-        @pl.when(down_owner(k) != f)
-        def _():
-            dwd_copy(k).start()
-
-    loop(0, ff_blocks, dwd_send)
+
+    loop(0, 4, feed_back)
+    back.second()
+    if planes > 1:
+        dd_planes.step(1)
     rows_tile = min(tile, width)
 
     def weight_grad(out, left, right):
@@ -575,10 +762,12 @@
         loop(0, width // rows_tile, body)
 
     def grad_planes(grad, taken, sems):
-        return Planes(
+        return Toward(
             at,
-            lambda to: grad.at[rows_of(to, part_rows), :],
-            lambda p: taken.at[p],
+            planes,
+            lambda i: i,
+            lambda i: grad.at[rows_of(i, part_rows), :],
+            taken,
             *sems,
         )
 
@@ -586,7 +775,17 @@
     do_planes = grad_planes(r.do, r.ro, r.do_sem)
     dj_planes = grad_planes(r.dj, r.rj, r.dj_sem)
     weight_grad(r.du, r.x2, r.upg)
-    du_planes.start()
+    du_planes.first(3)
+
+    def feed_part(g):
+        chip = at.chip_at(g)
+        part = dot(r.hidden[rows_of(chip, tile), :], r.wd[...]).astype(BF16)
+        r.feed[0][2 * chip] = part[:local]
+        r.feed[0][2 * chip + 1] = part[local:]
+        feed.to_partner(g).start()
+
+    loop(0, 4, feed_part)
+    att_gather.far()
 
     normed_two_grad = back.total()
     normal = r.n2[...]
@@ -617,13 +816,71 @@
     br_swap.start()
     r.datg[my_tokens, :] = r.dat[me]
     r.brg[my_tokens, :] = r.brs[me]
-    att_gather.relays()
-    loop(0, 4, lambda g: feed.to_partner(g).start())
+    if planes > 2:
+        du_planes.step(2)
+    feed.first()
     r.dk[...] = jnp.zeros_like(r.dk)
     r.dv[...] = jnp.zeros_like(r.dv)
+
+    class Owned:
+        def __init__(self, number, copies, acc, total, out, sems):
+            self.copies, self.acc, self.total = copies, acc, total
+            self.gather = Gather(at, total, lambda c: out.at[c], *sems)
+            self.own = pltpu.make_async_copy(total, out.at[me], r.own.at[number])
+
+        def reduce(self):
+            self.copies.total(f, self.acc)
+            self.total[...] = self.acc[...].astype(BF16)
+            self.gather.start()
+            self.own.start()
+
+    owned_u = Owned(0, du_planes, r.au, r.tu, r.gu, r.gu_sem)
+    owned_o = Owned(1, do_planes, r.ao, r.to, r.go, r.go_sem)
+    owned_j = Owned(2, dj_planes, r.aj, r.tj, r.gj, r.gj_sem)
+
+    full_shard = shard_blocks == CTX
+    gd_gather = Gather(
+        at, r.td, lambda c: r.gd.at[c], *r.gd_sem
+    )
+    gd_own = pltpu.make_async_copy(r.td, r.gd.at[down_place], r.own.at[3])
+
+    def gd_copy(d):
+        return remote(
+            r.td, r.gd.at[down_place], r.gd_sem[0].at[d - 1], r.gd_sem[1].at[down_place], (at.ctx_at(d), f)
+        )
+
+    def reduce_down():
+        @pl.when(has_down)
+        def _():
+            dd_planes.total(k_own, r.ad)
+            r.td[...] = r.ad[...].astype(BF16)
+            gd_own.start()
+            if not full_shard:
+                loop(1, CTX, lambda d: gd_copy(d).start())
+
+        if full_shard:
+            gd_gather.start()
+
+    reduce_down()
     dat_swap.waits()
 
     def attend_back(i):
+        @pl.when(i == 1)
+        def _():
+            feed.second()
+
+        @pl.when(i == 2)
+        def _():
+            if planes > 1:
+                du_planes.step(1)
+            if full_shard:
+                gd_gather.near()
+
+        @pl.when(i == 3)
+        def _():
+            if full_shard:
+                gd_gather.far()
+
         rows = rows_of(i, tile)
         grad = r.datg[rows, :]
         both = grad.astype(F32) * r.att[rows, :].astype(F32)
@@ -644,10 +901,12 @@
     loop(0, seq // tile, attend_back)
     r.pg[:, columns : 2 * columns] = r.dk[...].astype(BF16)
     r.pg[:, 2 * columns :] = r.dv[...].astype(BF16)
+    owned_u.reduce()
     weight_grad(r.dj, r.x1, r.pg)
-    dj_planes.start()
-
-    def first_part(g):
+    dj_planes.first(3)
+
+    def first_part(j):
+        g = jnp.where(j == 0, 3, jnp.where(j == 3, 0, j))
         chip = at.chip_at(g)
         part = dot_nt(r.pg[rows_of(chip, tile), :], r.wj[...]).astype(BF16)
         r.first[0][2 * chip] = part[:local]
@@ -655,90 +914,33 @@
         first.to_partner(g).start()
 
     loop(0, 4, first_part)
-    feed.forwards()
-    first.forwards()
+    first.first()
+    if planes > 2:
+        dj_planes.step(2)
+    first.second()
     att_gather.waits()
     br_swap.waits()
     weight_grad(r.do, r.attg, r.brg)
-    do_planes.start()
-
-    class Owned:
-        def __init__(self, number, copies, grad, taken, acc, total, out, sems):
-            self.copies, self.grad, self.taken, self.acc, self.total = copies, grad, taken, acc, total
-            self.gather = Gather(at, total, lambda c: out.at[c], *sems)
-            self.own = pltpu.make_async_copy(total, out.at[me], r.own.at[number])
-
-        def reduce(self):
-            self.copies.waits()
-            self.acc[...] = self.grad[my_rows, :].astype(F32)
-
-            def add(d):
-                self.acc[...] += self.taken[at.plane_at(d)].astype(F32)
-
-            loop(1, planes, add)
-            self.total[...] = self.acc[...].astype(BF16)
-            self.gather.start()
-            self.own.start()
-
-    owned_u = Owned(0, du_planes, r.du, r.ru, r.au, r.tu, r.gu, r.gu_sem)
-    owned_o = Owned(1, do_planes, r.do, r.ro, r.ao, r.to, r.go, r.go_sem)
-    owned_j = Owned(2, dj_planes, r.dj, r.rj, r.aj, r.tj, r.gj, r.gj_sem)
-
-    full_shard = shard_blocks == CTX
-    gd_gather = Gather(
-        at, r.td, lambda c: r.gd.at[c], *r.gd_sem
-    )
-    gd_own = pltpu.make_async_copy(r.td, r.gd.at[down_place], r.own.at[3])
-
-    def gd_copy(d):
-        return remote(
-            r.td, r.gd.at[down_place], r.gd_sem[0].at[d - 1], r.gd_sem[1].at[down_place], (at.ctx_at(d), f)
-        )
-
-    @pl.when(has_down)
-    def _():
-        def take(d):
-            p = at.plane_at(d)
-            block = r.rd.at[p]
-            remote(block, block, r.dwd_sem[0].at[0], r.dwd_sem[1].at[p], (me, p)).wait_recv()
-
-        loop(1, planes, take)
-        total = r.n2
-        total[...] = r.dwd[k_own].astype(F32)
-
-        def add(d):
-            total[...] += r.rd[at.plane_at(d)].astype(F32)
-
-        loop(1, planes, add)
-        r.td[...] = total[...].astype(BF16)
-        gd_own.start()
-        if not full_shard:
-            loop(1, CTX, lambda d: gd_copy(d).start())
-
-    if full_shard:
-        gd_gather.start()
-    owned_u.reduce()
-
+    if planes > 1:
+        dj_planes.step(1)
+    do_planes.first(1)
+    owned_u.gather.near()
     feed_total = feed.total()
     r.layer_out[...] = (r.middle[...] + feed_total + params[4:5, :]).astype(BF16)
     owned_j.reduce()
-
     normed_one_grad = first.total()
     normal, rate = standard(tokens[...].astype(F32))
     sums[0:1, :] = jnp.sum(normed_one_grad * normal, axis=0, keepdims=True)
     sums[1:2, :] = jnp.sum(normed_one_grad, axis=0, keepdims=True)
-    r.tokens_grad[...] += standard_grad(
-        normed_one_grad * params[0:1, :], normal, rate
-    )
+    r.tokens_grad[...] += standard_grad(normed_one_grad * params[0:1, :], normal, rate)
     r.sum_s[...] = sums[...].astype(BF16)
     sum_swap = Exchange(
         at, lambda c: r.sum_s, lambda c: r.sum_c.at[c], *r.sumc_sem
     )
     sum_swap.start()
     owned_o.reduce()
-    if full_shard:
-        gd_gather.relays()
-    owned_u.gather.relays()
+    owned_u.gather.far()
+    owned_j.gather.near()
     sum_swap.waits()
 
     def add_ctx(d):
@@ -750,8 +952,9 @@
         at, lambda to: r.sum_p, lambda p: r.sum_z.at[p], *r.sumz_sem
     )
     sum_planes.start()
-    owned_j.gather.relays()
-    owned_o.gather.relays()
+    owned_o.gather.near()
+    owned_j.gather.far()
+    owned_o.gather.far()
     sum_planes.waits()
 
     def add_planes(d):
@@ -792,20 +995,11 @@
 
         loop(0, shard_blocks, gd_take)
 
-    @pl.when(has_down)
-    def _():
-        loop(1, planes, lambda d: wd_copy(d).wait_send())
-
-    def dwd_sent(k):
-        @pl.when(down_owner(k) != f)
-        def _():
-            dwd_copy(k).wait_send()
-
-    loop(0, ff_blocks, dwd_sent)
     for each in (
         tok_gather, cot_gather, wo_gather, x2_gather, att_gather, owned_u.gather, owned_o.gather,
         owned_j.gather, ext_swap, att_swap, dat_swap, br_swap, sum_swap, small_planes, wj_planes,
-        wo_planes, wu_planes, du_planes, do_planes, dj_planes, sum_planes, back, feed, first,
+        wo_planes, wu_planes, wd_planes, dd_planes, du_planes, do_planes, dj_planes, sum_planes, back, feed,
+        first,
     ):
         each.finish()
 
@@ -874,10 +1068,11 @@
     v32 = lambda *shape: pltpu.VMEM(shape, F32)
     others = max(planes - 1, 1)
     scatter = (
-        v16(ctx, local, width), v16(4, local, width), v16(3, local, width),
-        dma(4), dma(4), dma(3), dma(3),
-    )
-    gather, swap, plane_sems = (dma(7), dma(ctx)), (dma(ctx - 1), dma(ctx)), (dma(others), dma(planes))
+        v16(ctx, local, width), v16(4, local, width), v16(2, local // 2, width), v16(2, local, width),
+        dma(4), dma(4), dma(4), dma(4),
+    )
+    gather, swap, plane_sems = (dma(8), dma(ctx + 1)), (dma(ctx - 1), dma(ctx)), (dma(others), dma(planes))
+    line, toward = (dma(2 * planes), dma(planes)), (dma(planes), dma(planes + 1))
     scratch = dict(
         wj=v16(width, 3 * columns), wo=v16(width, width), wu=v16(width, ff_part),
         wd=v16(ff_part, width), tokg=v16(seq, width), cotg=v16(seq, width),
@@ -895,18 +1090,18 @@
         sum_z=v16(planes, 16, width),
         dj=v16(width, 3 * columns), do=v16(width, columns), du=v16(width, ff_part),
         dwd=v16(ff_blocks, LANES, width),
-        rj=v16(planes, part_rows, 3 * columns), ro=v16(planes, part_rows, columns),
-        ru=v16(planes, part_rows, ff_part), rd=v16(planes, LANES, width),
-        aj=v32(part_rows, 3 * columns), ao=v32(part_rows, columns), au=v32(part_rows, ff_part),
+        rj=v16(planes + 1, part_rows, 3 * columns), ro=v16(planes + 1, part_rows, columns),
+        ru=v16(planes + 1, part_rows, ff_part), rd=v16(ff_blocks + 1, LANES, width),
+        aj=v32(part_rows, 3 * columns), ao=v32(part_rows, columns), au=v32(part_rows, ff_part), ad=v32(LANES, width), slope=v32(seq, ff_part),
         tj=v16(part_rows, 3 * columns), to=v16(part_rows, columns),
         tu=v16(part_rows, ff_part), td=v16(LANES, width),
-        stage=dma(5 + ff_blocks), own=dma(4), wd_sem=(dma(others), dma(ff_blocks)),
-        dwd_sem=(dma(ff_blocks), dma(planes)), back=scatter, feed=scatter, first=scatter,
+        stage=dma(5 + ff_blocks), own=dma(4), wd_sem=(dma(2 * ff_blocks), dma(ff_blocks)),
+        dwd_sem=(dma(ff_blocks), dma(ff_blocks + 1)), back=scatter, feed=scatter, first=scatter,
         tok_sem=gather, cot_sem=gather, wog_sem=gather, x2_sem=gather, attg_sem=gather,
         gj_sem=gather, go_sem=gather, gu_sem=gather, gd_sem=gather,
         ext_sem=swap, att_sem=swap, dat_sem=swap, br_sem=swap, sumc_sem=swap,
-        small_sem=plane_sems, wj_sem=plane_sems, wo_sem=plane_sems, wu_sem=plane_sems,
-        dj_sem=plane_sems, do_sem=plane_sems, du_sem=plane_sems, sumz_sem=plane_sems,
+        small_sem=plane_sems, wj_sem=line, wo_sem=line, wu_sem=line,
+        dj_sem=toward, do_sem=toward, du_sem=toward, sumz_sem=plane_sems,
     )
     shapes, scratch_tree = jax.tree.flatten(scratch)
     ins, outs = len(inputs), len(outputs)

time: 206 us -> 176 us (0.85)
  Pallas kernels: 202 us -> 172 us
    pallas_call x1, Pallas kernels: 193 us -> 163 us  [shards(): pl.pallas_call(kernel, out_shape=[jax.ShapeDtypeStruct(shape, dtype) for...]
where the time goes in v3:
time: 176 us; the launch traced here: 175 us
  Pallas kernels  172 us (98%)
  local copies, waits for them, and re-layouts  2.88 us (2%)
    pallas_call x1, Pallas kernels, shards(): pl.pallas_call(kernel, out_shape=[jax.ShapeDtypeStruct(shape, dtype) for...  163 us
    pallas_call x1, Pallas kernels, shards(): pl.pallas_call(finish, grid=(steps,), out_shape=[jax.ShapeDtypeStruct(sha...  9.25 us

profile of v3, /device:TPU:0, one launch (start us, length us, event | category | flops | bytes accessed | tf_op | source)
XLA Modules:
  0.0 175.5 jit_solution(15748699943141936449)
XLA Ops:
  0.6 1.4 copy.27.refs_3_
  2.0 162.7 %shard_map.238 = (bf16[128,1024]{1,0:T(8,128)(2,1)}, f32[128,1024]{1,0:T(8,128)}, f32[16,1024]{1,0:T(8,128)}, bf16[8,256,384]{2,1,0:T(8,128)(2,1)}, bf16[8,256,1...) custom-call(bf16[128,1024]{1,0:T(8,128)(2,1)} %bitcast.7, ...), custom_call_target="tpu_custom_call" | custom-call | tf_op jit(solution)/shard_map/pallas_call | solution.py:1114
  164.7 0.0 copy-start.1
  164.7 0.0 copy-start
  164.7 9.2 %shard_map.239 = (f32[256,3072]{1,0:T(8,128)}, f32[256,1024]{1,0:T(8,128)}, f32[256,4096]{1,0:T(8,128)}, f32[1024,1024]{1,0:T(8,128)}, f32[256]{0:T(256)}, /*ind...) custom-call(f32[16,1024]{1,0:T(8,128)} %get-tuple-element.31.totals, ...), custom_call_target="tpu_custom_call" | custom-call | tf_op jit(solution)/shard_map/pallas_call | solution.py:1155
  174.0 0.0 copy-done.1
  174.0 0.7 copy.30
  174.7 0.0 copy-done
  174.7 0.8 copy.31
Async XLA Ops:
  164.7 9.3 %copy-start.1 = (bf16[128,1024]{1,0:T(8,128)(2,1)S(1)}, bf16[128,1024]{1,0:T(8,128)(2,1)}, u32[]{:S(2)}) copy-start(bf16[128,1024]{1,0:T(8,128)(2,1)} %get-tuple-element.29) | copy-start | bytes 786436
  164.7 10.0 %copy-start = (f32[128,1024]{1,0:T(8,128)S(1)}, f32[128,1024]{1,0:T(8,128)}, u32[]{:S(2)}) copy-start(f32[128,1024]{1,0:T(8,128)} %get-tuple-element.30) | copy-start | bytes 1572868

commit v4 on v3

v4 whole, which is shorter than its diff:
```python
import types

import jax
import jax.numpy as jnp
from jax import lax
from jax.experimental import pallas as pl
from jax.experimental.pallas import tpu as pltpu
from jax.sharding import PartitionSpec as P

BLOCK = 64
LANES = 128
CTX = 8
SEGMENTS = 4
EPS = 1e-05
BIG = 1e30
MESH = pl.DeviceIdType.MESH
BF16 = jnp.bfloat16
F32 = jnp.float32


def dot(a, b):
    return lax.dot_general(a, b, (((1,), (0,)), ((), ())), preferred_element_type=F32)


def dot_nt(a, b):
    return lax.dot_general(a, b, (((1,), (1,)), ((), ())), preferred_element_type=F32)


def dot_tn(a, b):
    return lax.dot_general(a, b, (((0,), (0,)), ((), ())), preferred_element_type=F32)


def loop(lower, upper, body):
    lax.fori_loop(lower, upper, lambda i, carry: (body(i), carry)[1], jnp.int32(0))


def rows_of(index, size):
    return pl.ds(pl.multiple_of(index * size, size), size)


def remote(src, dst, send, recv, device):
    return pltpu.make_async_remote_copy(
        src_ref=src,
        dst_ref=dst,
        send_sem=send,
        recv_sem=recv,
        device_id=device,
        device_id_type=MESH,
    )


class Place:
    def __init__(self, planes):
        self.c = lax.axis_index("ctx")
        self.f = lax.axis_index("fsdp")
        self.planes = planes
        self.parity = lax.rem(self.c, 2)
        self.chip = lax.div(self.c, 2)
        self.partner = 2 * self.chip + 1 - self.parity

    def chip_at(self, g):
        low = lax.rem(lax.rem(self.chip, 2) + lax.rem(g, 2), 2)
        high = lax.rem(lax.div(self.chip, 2) + lax.div(g, 2), 2)
        return low + 2 * high

    def same(self, g):
        return 2 * self.chip_at(g) + self.parity

    def other(self, g):
        return 2 * self.chip_at(g) + 1 - self.parity

    def ctx_at(self, d):
        return lax.rem(self.c + d, CTX)

    def plane_at(self, d):
        return lax.rem(self.f + d, self.planes)


class Gather:
    def __init__(self, at, src, slot, send, recv):
        self.at, self.src, self.slot, self.send, self.recv = at, src, slot, send, recv

    def half(self, c, i):
        block = self.slot(c)
        size = block.shape[0] // 2
        return block.at[pl.ds(i * size, size)]

    def direct(self, i):
        at = self.at
        to = at.partner if i == 0 else at.same(jnp.int32(i))
        return remote(self.src, self.slot(at.c), self.send.at[i], self.recv.at[at.c], (to, at.f))

    def across(self, i):
        at = self.at
        c, to = at.same(jnp.int32(1 + i)), at.same(jnp.int32(2 - i))
        block = self.half(c, i)
        recv = self.recv.at[c] if i == 0 else self.recv.at[CTX]
        return remote(block, block, self.send.at[3 + i], recv, (to, at.f))

    def passed(self, g):
        at = self.at
        c = at.same(jnp.int32(g))
        block = self.slot(c)
        return remote(block, block, self.send.at[4 + g], self.recv.at[c], (at.partner, at.f))

    def start(self):
        for i in (1, 2, 0):
            self.direct(i).start()

    def wait(self, c):
        at = self.at
        block = self.slot(c)
        remote(block, block, self.send.at[0], self.recv.at[c], (at.partner, at.f)).wait_recv()

    def near(self, i):
        self.wait(self.at.same(jnp.int32(1 + i)))
        self.across(i).start()
        self.passed(1 + i).start()

    def far(self):
        at = self.at
        for i in range(2):
            c = at.same(jnp.int32(3))
            block = self.half(c, i)
            recv = self.recv.at[c] if i == 0 else self.recv.at[CTX]
            remote(block, block, self.send.at[0], recv, (at.partner, at.f)).wait_recv()
        self.passed(3).start()

    def waits(self):
        loop(0, 4, lambda g: self.wait(self.at.other(g)))

    def finish(self):
        for i in range(3):
            self.direct(i).wait_send()
        for i in range(2):
            self.across(i).wait_send()
        for g in (1, 2, 3):
            self.passed(g).wait_send()


class Exchange:
    def __init__(self, at, src, slot, send, recv):
        self.at, self.src, self.slot, self.send, self.recv = at, src, slot, send, recv

    def copy(self, d):
        at = self.at
        to = at.ctx_at(d)
        return remote(
            self.src(to), self.slot(at.c), self.send.at[d - 1], self.recv.at[at.c], (to, at.f)
        )

    def start(self):
        loop(1, CTX, lambda d: self.copy(d).start())

    def wait(self, d):
        at = self.at
        c = at.ctx_at(d)
        block = self.slot(c)
        remote(block, block, self.send.at[0], self.recv.at[c], (c, at.f)).wait_recv()

    def waits(self):
        loop(1, CTX, self.wait)

    def finish(self):
        loop(1, CTX, lambda d: self.copy(d).wait_send())


class Planes:
    def __init__(self, at, src, slot, send, recv):
        self.at, self.src, self.slot, self.send, self.recv = at, src, slot, send, recv

    def copy(self, d):
        at = self.at
        to = at.plane_at(d)
        return remote(
            self.src(to), self.slot(at.f), self.send.at[d - 1], self.recv.at[at.f], (at.c, to)
        )

    def start(self):
        loop(1, self.at.planes, lambda d: self.copy(d).start())

    def wait(self, d):
        at = self.at
        f = at.plane_at(d)
        block = self.slot(f)
        remote(block, block, self.send.at[0], self.recv.at[f], (at.c, f)).wait_recv()

    def waits(self):
        loop(1, self.at.planes, self.wait)

    def finish(self):
        loop(1, self.at.planes, lambda d: self.copy(d).wait_send())


class Line:
    def __init__(self, at, items, owner, view, send, recv):
        self.at, self.items, self.owner, self.view = at, items, owner, view
        self.send, self.recv = send, recv

    def hop(self, i, up):
        at, block = self.at, self.view(i)
        to = jnp.minimum(at.f + 1, at.planes - 1) if up else jnp.maximum(at.f - 1, 0)
        return remote(
            block, block, self.send.at[2 * i + (1 if up else 0)], self.recv.at[i], (at.c, to)
        )

    def outward(self, i, act):
        at, owner = self.at, self.owner(i)

        @pl.when((owner <= at.f) & (at.f < at.planes - 1))
        def _():
            act(self.hop(i, True))

        @pl.when((owner >= at.f) & (at.f > 0))
        def _():
            act(self.hop(i, False))

    def start(self):
        def each(i):
            @pl.when(self.owner(i) == self.at.f)
            def _():
                self.outward(i, lambda copy: copy.start())

        loop(0, self.items, each)

    def arrive(self, i):
        self.hop(i, True).wait_recv()
        self.outward(i, lambda copy: copy.start())

    def passes(self, d):
        if d == 3:
            loop(3, self.at.planes, self.passes_from)
        elif d < self.at.planes:
            self.passes_from(d)

    def passes_from(self, d):
        def each(i):
            owner = self.owner(i)

            @pl.when((owner == self.at.f + d) | (owner == self.at.f - d))
            def _():
                self.arrive(i)

        loop(0, self.items, each)

    def finish(self):
        loop(0, self.items, lambda i: self.outward(i, lambda copy: copy.wait_send()))


class Toward:
    def __init__(self, at, items, owner, part, taken, send, recv):
        self.at, self.items, self.owner, self.part, self.taken = at, items, owner, part, taken
        self.send, self.recv = send, recv

    def hop(self, i, up):
        at = self.at
        to = jnp.minimum(at.f + 1, at.planes - 1) if up else jnp.maximum(at.f - 1, 0)
        slot = i + 1 if up else i
        return remote(
            self.part(i), self.taken.at[slot], self.send.at[i], self.recv.at[slot], (at.c, to)
        )

    def step(self, d):
        at = self.at
        if d == 3:
            loop(3, at.planes, lambda j: self.step_to(at.planes + 2 - j))
        elif d < at.planes:
            self.step_to(d)

    def step_to(self, d):
        at = self.at

        def one(i, up, comes):
            @pl.when(comes)
            def _():
                self.hop(i, up).wait_recv()
                block = self.part(i)
                come = self.taken[i + 1 if up else i].astype(F32)
                block[...] = (block[...].astype(F32) + come).astype(BF16)

            self.hop(i, up).start()

        def each(i):
            @pl.when(self.owner(i) == at.f + d)
            def _():
                one(i, True, at.f > 0)

            @pl.when(self.owner(i) == at.f - d)
            def _():
                one(i, False, at.f < at.planes - 1)

        loop(0, self.items, each)

    def total(self, i, acc):
        at = self.at
        acc[...] = self.part(i)[...].astype(F32)

        @pl.when(at.f > 0)
        def _():
            self.hop(i, True).wait_recv()
            acc[...] += self.taken[i + 1].astype(F32)

        @pl.when(at.f < at.planes - 1)
        def _():
            self.hop(i, False).wait_recv()
            acc[...] += self.taken[i].astype(F32)

    def finish(self):
        def each(i):
            @pl.when(self.owner(i) > self.at.f)
            def _():
                self.hop(i, True).wait_send()

            @pl.when(self.owner(i) < self.at.f)
            def _():
                self.hop(i, False).wait_send()

        loop(0, self.items, each)


class Scatter:
    def __init__(self, at, part, pair, halves, far, pair_send, pair_recv, send, recv):
        self.at, self.part, self.pair, self.halves, self.far = at, part, pair, halves, far
        self.pair_send, self.pair_recv, self.send, self.recv = pair_send, pair_recv, send, recv
        self.size = part.shape[1] // 2

    def to_partner(self, g):
        at = self.at
        return remote(
            self.part.at[at.other(g)],
            self.pair.at[g],
            self.pair_send.at[g],
            self.pair_recv.at[g],
            (at.partner, at.f),
        )

    def across(self, i):
        at = self.at
        return remote(
            self.part.at[at.same(jnp.int32(3)), pl.ds(i * self.size, self.size)],
            self.halves.at[i],
            self.send.at[i],
            self.recv.at[i],
            (at.same(jnp.int32(1 + i)), at.f),
        )

    def beside(self, i):
        at = self.at
        to = at.same(jnp.int32(1 + i))
        return remote(
            self.part.at[to], self.far.at[i], self.send.at[2 + i], self.recv.at[2 + i], (to, at.f)
        )

    def add_pair(self, g):
        self.to_partner(jnp.int32(g)).wait_recv()
        own = self.at.same(jnp.int32(g))
        both = self.part[own].astype(F32) + self.pair[g].astype(F32)
        self.part[own] = both.astype(BF16)

    def first(self):
        self.add_pair(3)
        for i in range(2):
            self.across(i).start()

    def second(self):
        for i in range(2):
            self.add_pair(1 + i)
        for i in range(2):
            self.across(i).wait_recv()
            to = self.at.same(jnp.int32(2 - i))
            rows = pl.ds(i * self.size, self.size)
            both = self.part[to, rows].astype(F32) + self.halves[i].astype(F32)
            self.part[to, rows] = both.astype(BF16)
            self.beside(1 - i).start()

    def total(self):
        self.to_partner(jnp.int32(0)).wait_recv()
        for i in range(2):
            self.beside(i).wait_recv()
        both = self.part[self.at.c].astype(F32) + self.pair[0].astype(F32)
        return both + (self.far[0].astype(F32) + self.far[1].astype(F32))

    def finish(self):
        loop(0, 4, lambda g: self.to_partner(g).wait_send())
        for i in range(2):
            self.across(i).wait_send()
            self.beside(i).wait_send()


def standard(values):
    centre = jnp.mean(values, axis=-1, keepdims=True)
    offset = values - centre
    spread = jnp.mean(offset * offset, axis=-1, keepdims=True)
    rate = lax.rsqrt(spread + EPS)
    return offset * rate, rate


def standard_grad(e, normal, rate):
    return rate * (
        e - jnp.mean(e, axis=-1, keepdims=True) - normal * jnp.mean(e * normal, axis=-1, keepdims=True)
    )


def write_codes(r, at, seq):
    local = r.segments.shape[1]
    blocks, local_blocks = seq // BLOCK, local // BLOCK
    draws, _, heads = r.random.shape
    half = LANES // 2
    key = lax.rem(lax.broadcasted_iota(jnp.int32, (heads, LANES), 1), half)
    lower = lax.broadcasted_iota(jnp.int32, (1, LANES), 1) < half
    diagonal = lax.broadcasted_iota(jnp.int32, (heads, heads), 0) == lax.broadcasted_iota(
        jnp.int32, (heads, heads), 1
    )
    pair = r.globals[...]
    for b in range(local_blocks):
        block = at.c * local_blocks + b
        counted = jnp.abs(key - block) <= 1
        for j in range(draws):
            row = jnp.broadcast_to(r.random[j, b : b + 1, :].astype(F32), (heads, heads))
            drawn = jnp.sum(jnp.where(diagonal, row, 0.0), axis=1, keepdims=True)
            counted = counted | (key.astype(F32) == drawn)
        for j in range(pair.shape[1]):
            chosen = pair[:, j : j + 1]
            counted = counted | (key == chosen) | (chosen == block)
        code = jnp.where(counted | (key >= blocks), 0.0, -BIG)
        for d in range(heads // 2):
            both = jnp.where(lower, code[2 * d + 1 : 2 * d + 2], code[2 * d : 2 * d + 1])
            r.codes[d, b : b + 1, :] = both
    segments = r.segments[...].astype(F32)
    for d in range(heads // 2):
        r.codes[d, local_blocks : local_blocks + 1, :] = segments


def layer_kernel(r, planes):
    at = Place(planes)
    me, f = at.c, at.f
    tokens, cotangent = r.tokens, r.cotangent
    local, width = tokens.shape
    seq = local * CTX
    blocks, local_blocks = seq // BLOCK, local // BLOCK
    part_rows = width // planes
    columns = width // CTX
    shard = r.down.shape[0]
    ff = planes * shard
    ff_blocks = ff // LANES // CTX
    shard_blocks = shard // LANES
    full_shard = shard_blocks == CTX
    tile = 2 * local
    k_own = lax.div(f * shard_blocks, CTX)
    has_down = lax.div(me, shard_blocks) == lax.rem(f, CTX // shard_blocks)
    down_place = lax.rem(me, shard_blocks)

    def down_owner(k):
        return lax.div(CTX * k + me, shard_blocks)

    my_rows = rows_of(f, part_rows)
    my_columns = rows_of(me, columns)
    my_tokens = rows_of(me, local)

    barrier = pltpu.get_barrier_semaphore()
    loop(
        1,
        CTX,
        lambda d: pl.semaphore_signal(
            barrier, inc=1, device_id=(at.ctx_at(d), f), device_id_type=MESH
        ),
    )
    loop(
        1,
        planes,
        lambda d: pl.semaphore_signal(
            barrier, inc=1, device_id=(me, at.plane_at(d)), device_id_type=MESH
        ),
    )

    stage_j = [
        pltpu.make_async_copy(
            r.joint.at[:, pl.ds(pl.multiple_of(width * j + columns * me, LANES), columns)],
            r.wj.at[my_rows, pl.ds(columns * j, columns)],
            r.stage.at[j],
        )
        for j in range(3)
    ]
    stage_o = pltpu.make_async_copy(
        r.outw.at[:, my_columns], r.wo.at[my_rows, my_columns], r.stage.at[3]
    )
    stage_u = [
        pltpu.make_async_copy(
            r.up.at[:, pl.ds(pl.multiple_of(CTX * LANES * k + LANES * me, LANES), LANES)],
            r.wu.at[my_rows, pl.ds(LANES * k, LANES)],
            r.stage.at[4 + k],
        )
        for k in range(ff_blocks)
    ]
    stage_d = pltpu.make_async_copy(
        r.down.at[rows_of(down_place, LANES), :],
        r.wd.at[rows_of(k_own, LANES), :],
        r.stage.at[4 + ff_blocks],
    )
    for copy in [*stage_j, stage_o, *stage_u]:
        copy.start()

    @pl.when(has_down)
    def _():
        stage_d.start()

    small, short = r.small, r.small.shape[1]
    small[...] = jnp.zeros_like(small)
    for i, vector in enumerate((r.gain_one, r.bias_one, r.gain_two, r.bias_two, r.bias_down)):
        small[i : i + 1, 0:part_rows] = vector[...].astype(F32).reshape(1, part_rows)
    for i in range(shard // short):
        piece = r.bias_up[i * short : (i + 1) * short]
        small[5 + i : 6 + i, :] = piece.astype(F32).reshape(1, short)

    def token_gather(src, dst, sems):
        return Gather(at, src, lambda c: dst.at[rows_of(c, local)], *sems)

    tok = token_gather(tokens, r.tokg, r.tok_sem)
    cot = token_gather(cotangent, r.cotg, r.cot_sem)
    x2 = token_gather(r.x2.at[my_tokens], r.x2, r.x2_sem)
    attg = token_gather(r.attg.at[my_tokens], r.attg, r.attg_sem)
    wog = Gather(
        at, r.wo.at[:, my_columns], lambda c: r.wo.at[:, rows_of(c, columns)], *r.wog_sem
    )
    codes = Exchange(at, lambda c: r.codes.at[c], lambda c: r.codeg.at[c], *r.code_sem)
    att_swap = Exchange(
        at, lambda c: r.att.at[rows_of(c, local)], lambda c: r.attx.at[c], *r.att_sem
    )

    def token_swap(src, dst, sems):
        return Exchange(at, lambda c: src.at[c], lambda c: dst.at[rows_of(c, local)], *sems)

    dat_swap = token_swap(r.dat, r.datg, r.dat_sem)
    br_swap = token_swap(r.brs, r.brg, r.br_sem)
    small_planes = Planes(at, lambda to: small, lambda p: r.smallg.at[p], *r.small_sem)

    def weight_line(ref, sems, width_ds):
        return Line(
            at, planes, lambda i: i, lambda i: ref.at[rows_of(i, part_rows), width_ds], *sems
        )

    wj = weight_line(r.wj, r.wj_sem, slice(None))
    wo = weight_line(r.wo, r.wo_sem, my_columns)
    wu = weight_line(r.wu, r.wu_sem, slice(None))
    wd = Line(at, ff_blocks, down_owner, lambda k: r.wd.at[rows_of(k, LANES), :], *r.wd_sem)
    back, feed, first = (Scatter(at, *group) for group in (r.back, r.feed, r.first))

    def grad_line(grad, taken, sems):
        return Toward(
            at, planes, lambda i: i, lambda i: grad.at[rows_of(i, part_rows), :], taken, *sems
        )

    dd = Toward(at, ff_blocks, down_owner, lambda k: r.dwd.at[k], r.rd, *r.dwd_sem)
    du = grad_line(r.du, r.ru, r.du_sem)
    do = grad_line(r.do, r.ro, r.do_sem)
    dk = grad_line(r.dk, r.rk, r.dk_sem)
    dq = grad_line(r.dq, r.rq, r.dq_sem)

    class Owned:
        def __init__(self, number, line, acc, total, out, sems):
            self.line, self.acc, self.sum = line, acc, total
            self.gather = Gather(at, total, lambda c: out.at[c], *sems)
            self.own = pltpu.make_async_copy(total, out.at[me], r.own.at[number])

        def total(self):
            self.line.total(f, self.acc)
            self.sum[...] = self.acc[...].astype(BF16)
            self.gather.start()
            self.own.start()

        def near(self, i):
            self.gather.near(i)

        def far(self):
            self.gather.far()

        def waits(self):
            self.gather.waits()
            self.own.wait()

        def finish(self):
            self.gather.finish()

    gu = Owned(0, du, r.au, r.tu, r.gu, r.gu_sem)
    go = Owned(1, do, r.ao, r.to, r.go, r.go_sem)
    gk = Owned(2, dk, r.ak, r.tk, r.gk, r.gk_sem)
    gq = Owned(3, dq, r.aq, r.tq, r.gq, r.gq_sem)

    class OwnedDown:
        def __init__(self):
            self.gather = Gather(at, r.td, lambda c: r.gd.at[c], *r.gd_sem)
            self.own = pltpu.make_async_copy(r.td, r.gd.at[down_place], r.own.at[4])

        def copy(self, d):
            send, recv = r.gd_sem
            block = r.gd.at[down_place]
            return remote(r.td, block, send.at[d - 1], recv.at[down_place], (at.ctx_at(d), f))

        def total(self):
            @pl.when(has_down)
            def _():
                dd.total(k_own, r.ad)
                r.td[...] = r.ad[...].astype(BF16)
                self.own.start()
                if not full_shard:
                    loop(1, CTX, lambda d: self.copy(d).start())

            if full_shard:
                self.gather.start()

        def near(self, i):
            if full_shard:
                self.gather.near(i)

        def far(self):
            if full_shard:
                self.gather.far()

        def waits(self):
            @pl.when(has_down)
            def _():
                self.own.wait()

            if full_shard:
                self.gather.waits()
                return

            def take(b):
                @pl.when(me != lax.rem(f * shard_blocks + b, CTX))
                def _():
                    block, (send, recv) = r.gd.at[b], r.gd_sem
                    to = (at.ctx_at(jnp.int32(1)), f)
                    remote(block, block, send.at[0], recv.at[b], to).wait_recv()

            loop(0, shard_blocks, take)

        def finish(self):
            if full_shard:
                self.gather.finish()
                return

            @pl.when(has_down)
            def _():
                loop(1, CTX, lambda d: self.copy(d).wait_send())

    gd = OwnedDown()

    class Sums:
        def __init__(self, own, acc, sent, ctx_in, plane_in, ctx_sems, plane_sems):
            self.own, self.acc, self.sent, self.ctx_in, self.plane_in = own, acc, sent, ctx_in, plane_in
            self.swap = Exchange(at, lambda c: own, lambda c: ctx_in.at[c], *ctx_sems)
            self.planes = Planes(at, lambda to: sent, lambda p: plane_in.at[p], *plane_sems)

        def put(self, row, vector):
            for k in range(width // LANES):
                self.acc[row + k : row + k + 1, :] = vector[:, k * LANES : (k + 1) * LANES]

        def start(self):
            self.own[...] = self.acc[...].astype(BF16)
            self.swap.start()

        def middle(self):
            self.swap.waits()

            def add(d):
                self.acc[...] += self.ctx_in[at.ctx_at(d)].astype(F32)

            loop(1, CTX, add)
            self.sent[...] = self.acc[...].astype(BF16)
            self.planes.start()

        def end(self):
            self.planes.waits()

            def add(d):
                self.acc[...] += self.plane_in[at.plane_at(d)].astype(F32)

            loop(1, planes, add)

        def row(self, row):
            for k in range(width // LANES):
                r.wide[0:1, k * LANES : (k + 1) * LANES] = self.acc[row + k : row + k + 1, :]
            return r.wide[0:1, :]

        def finish(self):
            self.swap.finish()
            self.planes.finish()

    early, late = Sums(*r.early), Sums(*r.late)
    params = r.params

    def open_devices():
        pl.semaphore_wait(barrier, CTX - 1 + planes - 1)
        r.tokg[my_tokens, :] = tokens[...]
        r.cotg[my_tokens, :] = cotangent[...]

    def wj_start():
        for copy in stage_j:
            copy.wait()
        wj.start()

    def wo_start():
        stage_o.wait()
        wo.start()

    def wu_start():
        for copy in stage_u:
            copy.wait()
        wu.start()

    def wd_start():
        @pl.when(has_down)
        def _():
            stage_d.wait()

        wd.start()

    def make_codes():
        write_codes(r, at, seq)
        r.codeg[me] = r.codes[me]

    def take_params():
        r.smallg[f] = small[...]
        small_planes.waits()
        params[...] = jnp.zeros_like(params)
        r.wide[...] = jnp.zeros_like(r.wide)

        def add(p):
            r.wide[:, 0:short] = r.smallg[p, 0:8, :]
            params[...] += pltpu.roll(r.wide[...], p * part_rows, axis=1)

        loop(0, planes, add)
        for k in range(ff_blocks):
            block = CTX * k + me
            place = lax.rem(block, shard_blocks) * LANES
            lanes = pl.ds(pl.multiple_of(lax.rem(place, short), LANES), LANES)
            rows = r.smallg[down_owner(k), :, lanes]
            number = lax.broadcasted_iota(jnp.int32, rows.shape, 0)
            r.ub[0:1, k * LANES : (k + 1) * LANES] = jnp.sum(
                jnp.where(number == 5 + lax.div(place, short), rows, 0.0), axis=0, keepdims=True
            )

    def norm_tokens(g):
        tok.wait(at.other(g))
        rows = rows_of(at.chip_at(g), tile)
        normal, _ = standard(r.tokg[rows, :].astype(F32))
        r.x1[rows, :] = (normal * params[0:1, :] + params[1:2, :]).astype(BF16)

    lane = lax.broadcasted_iota(jnp.int32, (tile, columns), 1)
    low = lane < columns // 2
    zero_tile = jnp.zeros((tile, columns), BF16)

    def project(i):
        rows = rows_of(i, tile)
        projected = dot(r.x1[rows, :], r.wj[...]).astype(BF16)
        q = projected[:, :columns] * jnp.array(0.125, BF16)
        k = projected[:, columns : 2 * columns]
        v = projected[:, 2 * columns :]
        half = lax.rem(lane, columns // 2)
        segment_place = lax.rem(lax.broadcasted_iota(jnp.int32, (LANES, local), 0), LANES // 2) - blocks
        parts = []
        for e in range(2):
            code = r.codeg[2 * i + e]
            hot = jnp.where(
                code[local_blocks : local_blocks + 1] == segment_place.astype(F32), 1.0, 0.0
            ).T
            for b in range(local_blocks):
                parts.append(hot[b * BLOCK : (b + 1) * BLOCK] + code[b : b + 1])
        ext = jnp.concatenate(parts, axis=0)
        token = lax.broadcasted_iota(jnp.int32, (tile, columns), 0) + i * tile
        hot = jnp.where(half == lax.div(token, BLOCK), 1.0, 0.0)
        k_ext = jnp.where(
            half < blocks, hot, jnp.where(half < blocks + SEGMENTS, (1.0 - ext) * -BIG, 0.0)
        ).astype(BF16)
        ext = ext.astype(BF16)
        r.q[rows, :] = q
        r.qa[0, rows, :] = jnp.where(low, q, ext)
        r.qa[1, rows, :] = jnp.where(low, ext, q)
        r.ka[0, rows, :] = jnp.where(low, k, k_ext)
        r.ka[1, rows, :] = jnp.where(low, k_ext, k)
        r.km[0, rows, :] = jnp.where(low, k, zero_tile)
        r.km[1, rows, :] = jnp.where(low, zero_tile, k)
        r.vm[0, rows, :] = jnp.where(low, v, zero_tile)
        r.vm[1, rows, :] = jnp.where(low, zero_tile, v)

    def attend(i):
        rows = rows_of(i, tile)
        out = None
        for h in range(2):
            scores = dot_nt(r.qa[h, rows, :], r.ka[h])
            weights = jnp.exp(scores - jnp.max(scores, axis=1, keepdims=True))
            shares = (weights / jnp.sum(weights, axis=1, keepdims=True)).astype(BF16)
            r.probs[h, rows, :] = shares
            term = dot(shares, r.vm[h])
            out = term if out is None else out + term
        r.att[rows, :] = out.astype(BF16)

    def att_swap_start():
        att_swap.start()
        r.attx[me] = r.att[my_tokens, :]

    def project_out():
        att_swap.waits()
        for c in range(CTX):
            r.attg[my_tokens, c * columns : (c + 1) * columns] = r.attx[c]
        wog.waits()
        middle = tokens[...].astype(F32) + dot(r.attg[my_tokens, :], r.wo[...])
        normal, rate = standard(middle)
        r.middle[...] = middle
        r.n2[...] = normal
        r.rate2[...] = jnp.broadcast_to(rate, r.rate2.shape)
        r.x2[my_tokens, :] = (normal * params[2:3, :] + params[3:4, :]).astype(BF16)

    r.ubg[...] = jnp.zeros_like(r.ubg)

    def hidden_units(g):
        x2.wait(at.other(g))
        rows = rows_of(at.chip_at(g), tile)
        up_sum = dot(r.x2[rows, :], r.wu[...]) + r.ub[...]
        share = 0.5 * (1.0 + lax.erf(up_sum * 0.7071067811865476))
        r.hidden[rows, :] = (up_sum * share).astype(BF16)
        r.slope[rows, :] = share + up_sum * jnp.exp(-0.5 * up_sum * up_sum) * 0.3989422804014327

    def down_grad():
        def one(k):
            r.dwd[k] = dot_tn(r.hidden[:, rows_of(k, LANES)], r.cotg[...]).astype(BF16)

        loop(0, ff_blocks, one)

    def far_first(j):
        return jnp.where(j == 0, 3, jnp.where(j == 3, 0, j))

    def put_part(scatter, g, part):
        chip = at.chip_at(g)
        part = part.astype(BF16)
        scatter.part[2 * chip] = part[:local]
        scatter.part[2 * chip + 1] = part[local:]
        scatter.to_partner(g).start()

    def feed_back(j):
        g = far_first(j)
        rows = rows_of(at.chip_at(g), tile)
        up_grad = (dot_nt(r.cotg[rows, :], r.wd[...]) * r.slope[rows, :]).astype(BF16)
        r.upg[rows, :] = up_grad
        r.ubg[...] += jnp.sum(up_grad.astype(F32), axis=0, keepdims=True)
        put_part(back, g, dot_nt(up_grad, r.wu[...]))

    def feed_part(j):
        g = far_first(j)
        put_part(feed, g, dot(r.hidden[rows_of(at.chip_at(g), tile), :], r.wd[...]))

    def first_part(j):
        g = far_first(j)
        put_part(first, g, dot_nt(r.pg[rows_of(at.chip_at(g), tile), :], r.wj[...]))

    rows_tile = min(tile, width)

    def weight_grad(out, left, right, lanes=slice(None)):
        def body(i):
            out[rows_of(i, rows_tile), :] = dot_tn(
                left[:, rows_of(i, rows_tile)], right[:, lanes]
            ).astype(BF16)

        loop(0, width // rows_tile, body)

    def up_weight_grad():
        weight_grad(r.du, r.x2, r.upg)

    def middle_back():
        normed_two_grad = back.total()
        normal = r.n2[...]
        cot_own = cotangent[...].astype(F32)
        early.acc[...] = jnp.zeros_like(early.acc)
        early.put(0, jnp.sum(normed_two_grad * normal, axis=0, keepdims=True))
        early.put(8, jnp.sum(normed_two_grad, axis=0, keepdims=True))
        early.put(16, jnp.sum(cot_own, axis=0, keepdims=True))
        for k in range(ff_blocks):
            early.acc[pl.ds(24 + CTX * k + me, 1), :] = r.ubg[0:1, k * LANES : (k + 1) * LANES]
        middle_grad = cot_own + standard_grad(
            normed_two_grad * params[2:3, :], normal, r.rate2[:, 0:1]
        )
        r.tokens_grad[...] = middle_grad
        branch = middle_grad.astype(BF16)
        attended_grad = dot_nt(branch, r.wo[...]).astype(BF16)
        for c in range(CTX):
            r.dat[c] = attended_grad[:, c * columns : (c + 1) * columns]
            r.brs[c] = branch[:, c * columns : (c + 1) * columns]
        r.acc_k[...] = jnp.zeros_like(r.acc_k)
        r.acc_v[...] = jnp.zeros_like(r.acc_v)

    def dat_start():
        dat_swap.start()
        r.datg[my_tokens, :] = r.dat[me]

    def br_start():
        br_swap.start()
        r.brg[my_tokens, :] = r.brs[me]

    def attend_back(i):
        rows = rows_of(i, tile)
        grad = r.datg[rows, :]
        both = grad.astype(F32) * r.att[rows, :].astype(F32)
        q = r.q[rows, :]
        query_grad = None
        for h in range(2):
            keep = low if h == 0 else ~low
            delta = jnp.sum(jnp.where(keep, both, 0.0), axis=1, keepdims=True)
            probs = r.probs[h, rows, :]
            prob_grad = dot_nt(grad, r.vm[h])
            score_grad = (probs.astype(F32) * (prob_grad - delta)).astype(BF16)
            term = dot(score_grad, r.km[h])
            query_grad = term if query_grad is None else query_grad + term
            r.acc_k[...] += dot_tn(score_grad, jnp.where(keep, q, zero_tile))
            r.acc_v[...] += dot_tn(probs, jnp.where(keep, grad, zero_tile))
        r.pg[rows, :columns] = (query_grad * 0.125).astype(BF16)

    def keys_back():
        r.pg[:, columns : 2 * columns] = r.acc_k[...].astype(BF16)
        r.pg[:, 2 * columns :] = r.acc_v[...].astype(BF16)

    def key_weight_grad():
        weight_grad(r.dk, r.x1, r.pg, slice(columns, None))

    def query_weight_grad():
        weight_grad(r.dq, r.x1, r.pg, slice(0, columns))

    def out_weight_grad():
        attg.waits()
        br_swap.waits()
        weight_grad(r.do, r.attg, r.brg)

    def layer_end():
        r.layer_out[...] = (r.middle[...] + feed.total() + params[4:5, :]).astype(BF16)

    def tokens_back():
        normed_one_grad = first.total()
        normal, rate = standard(tokens[...].astype(F32))
        late.put(0, jnp.sum(normed_one_grad * normal, axis=0, keepdims=True))
        late.put(8, jnp.sum(normed_one_grad, axis=0, keepdims=True))
        r.tokens_grad[...] += standard_grad(normed_one_grad * params[0:1, :], normal, rate)

    def write_totals():
        for i, (sums, row) in enumerate(((late, 0), (late, 8), (early, 0), (early, 8), (early, 16))):
            vector = jnp.broadcast_to(sums.row(row), (8, width))
            turned = pltpu.roll(vector, lax.rem((planes - f) * part_rows, width), axis=1)
            r.totals[i : i + 1, :] = turned[0:1]
        for k in range(shard_blocks):
            r.totals[5:6, k * LANES : (k + 1) * LANES] = early.acc[
                pl.ds(24 + f * shard_blocks + k, 1), :
            ]

    open_devices()
    tok.start()
    wj_start()
    wo_start()
    wo.passes(1)
    small_planes.start()
    cot.start()
    take_params()
    wj.passes(1)
    tok.near(0)
    wo.passes(2)
    tok.near(1)
    make_codes()
    codes.start()
    wj.passes(2)

    def step_1(i):

        @pl.when(i == 2)
        def _():
            wu_start()
            tok.far()
            cot.near(0)

        @pl.when(i == 3)
        def _():
            wo.passes(3)
            wog.start()

        norm_tokens(i)

    loop(0, 4, step_1)

    codes.waits()
    wj.passes(3)

    def step_2(i):

        @pl.when(i == 1)
        def _():
            cot.near(1)

        project(i)

    loop(0, 4, step_2)


    def step_3(i):

        @pl.when(i == 2)
        def _():
            wu.passes(1)
            wog.near(1)
            cot.far()
            wog.near(0)

        attend(i)

    loop(0, 4, step_3)

    att_swap_start()
    wd_start()
    wog.far()
    wu.passes(2)
    project_out()
    x2.start()
    wd.passes(1)
    x2.near(0)
    x2.near(1)
    wu.passes(3)

    def step_4(i):

        @pl.when(i == 2)
        def _():
            attg.start()
            wd.passes(2)
            x2.far()

        hidden_units(i)

    loop(0, 4, step_4)

    cot.waits()
    down_grad()
    wd.passes(3)
    attg.near(0)
    attg.near(1)
    dd.step(3)
    feed_back(jnp.int32(0))
    feed_part(jnp.int32(0))
    back.first()

    def step_5(i):

        @pl.when(i == 3)
        def _():
            back.second()
            dd.step(2)

        feed_back(i)

    loop(1, 4, step_5)

    up_weight_grad()
    du.step(3)
    middle_back()
    dat_start()
    dd.step(1)
    loop(1, 3, feed_part)
    feed.first()
    br_start()
    dat_swap.waits()

    def step_6(i):

        @pl.when(i == 1)
        def _():
            du.step(2)
            gd.total()

        @pl.when(i == 2)
        def _():
            feed.second()

        @pl.when(i == 3)
        def _():
            du.step(1)
            early.start()

        attend_back(i)

    loop(0, 4, step_6)

    keys_back()

    def step_7(i):

        @pl.when(i == 1)
        def _():
            query_weight_grad()

        @pl.when(i == 2)
        def _():
            key_weight_grad()
            dk.step(3)
            attg.far()
            first.first()
            early.middle()
            out_weight_grad()
            dk.step(2)
            dq.step(3)
            gd.near(0)
            gd.near(1)

        first_part(i)

    loop(0, 3, step_7)

    first.second()
    dq.step(2)
    gu.total()
    dk.step(1)
    do.step(3)
    dq.step(1)
    do.step(2)
    feed_part(jnp.int32(3))
    gk.total()
    gq.total()
    first_part(jnp.int32(3))
    early.end()
    do.step(1)
    gu.near(1)
    go.total()
    gu.near(0)
    gq.near(1)
    tokens_back()
    gk.near(0)
    gk.near(1)
    late.start()
    go.near(0)
    gd.far()
    gq.near(0)
    late.middle()
    go.near(1)
    gu.far()
    gk.far()
    go.far()
    layer_end()
    gq.far()
    late.end()
    for each in (gd, gu, go, gk, gq):
        each.waits()
    write_totals()
    for each in (
        tok, cot, wog, x2, attg, gu, go, gk, gq, gd, codes, att_swap, dat_swap, br_swap, early, late,
        small_planes, wj, wo, wu, wd, dd, du, do, dk, dq, back, feed, first,
    ):
        each.finish()


def shards(
    tokens,
    segment_ids,
    random_blocks,
    global_blocks,
    first_gain,
    first_bias,
    joint_weight,
    output_weight,
    second_gain,
    second_bias,
    up_weight,
    up_bias,
    down_weight,
    down_bias,
    cotangent,
):
    local, width = tokens.shape[1:]
    ctx, planes = lax.axis_size("ctx"), lax.axis_size("fsdp")
    heads = random_blocks.shape[2]
    seq = local * ctx
    blocks = seq // BLOCK
    part_rows = width // planes
    columns = width // ctx
    ff_shard = up_bias.shape[0]
    ff = ff_shard * planes
    ff_blocks = ff // LANES // ctx
    shard_blocks = ff_shard // LANES
    ff_part = ff // ctx
    assert ctx == CTX and columns == LANES and heads == 2 * ctx and blocks + SEGMENTS <= 64
    assert CTX % shard_blocks == 0 and ff // width == ff_blocks

    vmem, hbm = pl.BlockSpec(memory_space=pltpu.VMEM), pl.BlockSpec(memory_space=pl.ANY)
    inputs = dict(
        tokens=(tokens[0], vmem),
        cotangent=(cotangent[0], vmem),
        segments=(segment_ids, vmem),
        random=(random_blocks[0].transpose(2, 0, 1), vmem),
        globals=(global_blocks, vmem),
        gain_one=(first_gain, vmem),
        bias_one=(first_bias, vmem),
        gain_two=(second_gain, vmem),
        bias_two=(second_bias, vmem),
        bias_up=(up_bias, vmem),
        bias_down=(down_bias, vmem),
        joint=(joint_weight, hbm),
        outw=(output_weight, hbm),
        up=(up_weight, hbm),
        down=(down_weight, hbm),
    )
    outputs = dict(
        layer_out=((local, width), BF16, vmem),
        tokens_grad=((local, width), F32, vmem),
        totals=((8, width), F32, vmem),
        gk=((ctx, part_rows, 2 * columns), BF16, hbm),
        gq=((ctx, part_rows, columns), BF16, hbm),
        go=((ctx, part_rows, columns), BF16, hbm),
        gu=((ctx, part_rows, ff_part), BF16, hbm),
        gd=((shard_blocks, LANES, width), BF16, hbm),
    )
    dma = lambda n: pltpu.SemaphoreType.DMA((n,))
    v16 = lambda *shape: pltpu.VMEM(shape, BF16)
    v32 = lambda *shape: pltpu.VMEM(shape, F32)
    others = max(planes - 1, 1)
    scatter = (
        v16(ctx, local, width), v16(4, local, width), v16(2, local // 2, width), v16(2, local, width),
        dma(4), dma(4), dma(4), dma(4),
    )
    gather, swap, plane_sems = (dma(8), dma(ctx + 1)), (dma(ctx - 1), dma(ctx)), (dma(others), dma(planes))
    line, toward = (dma(2 * planes), dma(planes)), (dma(planes), dma(planes + 1))
    short = max(part_rows, LANES)
    vectors = lambda rows: (
        v16(rows, LANES), v32(rows, LANES), v16(rows, LANES), v16(ctx, rows, LANES),
        v16(planes, rows, LANES), swap, plane_sems,
    )
    scratch = dict(
        wj=v16(width, 3 * columns), wo=v16(width, width), wu=v16(width, ff_part),
        wd=v16(ff_part, width), tokg=v16(seq, width), cotg=v16(seq, width),
        x1=v16(seq, width), x2=v16(seq, width), attg=v16(seq, width),
        codes=v32(ctx, 8, LANES), codeg=v32(ctx, 8, LANES), small=v32(16, short),
        smallg=v32(planes, 16, short), params=v32(8, width), wide=v32(8, width),
        ub=v32(1, ff_part), ubg=v32(1, ff_part), q=v16(seq, columns),
        qa=v16(2, seq, columns), ka=v16(2, seq, columns), km=v16(2, seq, columns),
        vm=v16(2, seq, columns), probs=v16(2, seq, seq), att=v16(seq, columns),
        attx=v16(ctx, local, columns), middle=v32(local, width), n2=v32(local, width),
        rate2=v32(local, LANES), hidden=v16(seq, ff_part), slope=v32(seq, ff_part),
        upg=v16(seq, ff_part), dat=v16(ctx, local, columns), brs=v16(ctx, local, columns),
        datg=v16(seq, columns), brg=v16(seq, columns), acc_k=v32(seq, columns),
        acc_v=v32(seq, columns), pg=v16(seq, 3 * columns), early=vectors(64), late=vectors(16),
        dk=v16(width, 2 * columns), dq=v16(width, columns), do=v16(width, columns),
        du=v16(width, ff_part), dwd=v16(ff_blocks, LANES, width),
        rk=v16(planes + 1, part_rows, 2 * columns), rq=v16(planes + 1, part_rows, columns),
        ro=v16(planes + 1, part_rows, columns), ru=v16(planes + 1, part_rows, ff_part),
        rd=v16(ff_blocks + 1, LANES, width),
        ak=v32(part_rows, 2 * columns), aq=v32(part_rows, columns), ao=v32(part_rows, columns),
        au=v32(part_rows, ff_part), ad=v32(LANES, width),
        tk=v16(part_rows, 2 * columns), tq=v16(part_rows, columns), to=v16(part_rows, columns),
        tu=v16(part_rows, ff_part), td=v16(LANES, width),
        stage=dma(5 + ff_blocks), own=dma(5), wd_sem=(dma(2 * ff_blocks), dma(ff_blocks)),
        dwd_sem=(dma(ff_blocks), dma(ff_blocks + 1)), back=scatter, feed=scatter, first=scatter,
        tok_sem=gather, cot_sem=gather, wog_sem=gather, x2_sem=gather, attg_sem=gather,
        gk_sem=gather, gq_sem=gather, go_sem=gather, gu_sem=gather, gd_sem=gather,
        code_sem=swap, att_sem=swap, dat_sem=swap, br_sem=swap,
        small_sem=plane_sems, wj_sem=line, wo_sem=line, wu_sem=line,
        dk_sem=toward, dq_sem=toward, do_sem=toward, du_sem=toward,
    )
    shapes, scratch_tree = jax.tree.flatten(scratch)
    ins, outs = len(inputs), len(outputs)

    def kernel(*refs):
        held = dict(zip([*inputs, *outputs], refs, strict=False))
        held |= jax.tree.unflatten(scratch_tree, refs[ins + outs :])
        layer_kernel(types.SimpleNamespace(**held), planes)

    layer_out, tokens_grad, totals, gk, gq, go, gu, gd = pl.pallas_call(
        kernel,
        out_shape=[jax.ShapeDtypeStruct(shape, dtype) for shape, dtype, _ in outputs.values()],
        in_specs=[spec for _, spec in inputs.values()],
        out_specs=[spec for *_, spec in outputs.values()],
        scratch_shapes=shapes,
        compiler_params=pltpu.CompilerParams(
            collective_id=0, has_side_effects=True, vmem_limit_bytes=60 * 1024 * 1024
        ),
    )(*(value for value, _ in inputs.values()))

    group = 4
    quads = ctx // group
    steps = ff_blocks * quads

    def spread(ref, out):
        for q in range(group):
            out[:, q * columns : (q + 1) * columns] = ref[q].astype(F32)

    def finish(out_in, grad_in, totals, gk, gq, go, gu, gd, joint, outw, up, down, out, grad, *vectors):
        step = pl.program_id(0)

        @pl.when(step < quads)
        def _():
            spread(gq, joint)
            spread(go, outw)

        @pl.when((step >= quads) & (step < 3 * quads))
        def _():
            spread(gk, joint)

        spread(gu, up)
        down[...] = gd[0].astype(F32)
        out[...] = out_in[...]
        grad[...] = grad_in[...]
        for i, vector in enumerate(vectors[:5]):
            vector[...] = totals[i : i + 1, 0:part_rows].reshape(part_rows)
        vectors[5][...] = totals[5:6, 0:ff_shard].reshape(ff_shard)

    def from_places(start, count):
        place = lambda i: jnp.clip(i - start, 0, count - 1)
        return pl.BlockSpec(
            (group, part_rows, columns), lambda i: (place(i) % quads, 0, place(i) // quads)
        )

    def to_columns(count):
        return pl.BlockSpec((part_rows, group * columns), lambda i: (0, jnp.minimum(i, count - 1)))

    down_place = lambda i: jnp.minimum(i, shard_blocks - 1)
    whole = pl.BlockSpec(memory_space=pltpu.VMEM)
    tokens_spec = pl.BlockSpec((local // steps, width), lambda i: (i, 0))
    made = pl.pallas_call(
        finish,
        grid=(steps,),
        out_shape=[
            jax.ShapeDtypeStruct(shape, dtype)
            for shape, dtype in (
                ((part_rows, 3 * width), F32), ((part_rows, width), F32), ((part_rows, ff), F32),
                ((ff_shard, width), F32), ((local, width), BF16), ((local, width), F32),
                *([((part_rows,), F32)] * 5), ((ff_shard,), F32),
            )
        ],
        in_specs=[
            tokens_spec,
            tokens_spec,
            whole,
            from_places(quads, 2 * quads),
            from_places(0, quads),
            from_places(0, quads),
            from_places(0, steps),
            pl.BlockSpec((1, LANES, width), lambda i: (down_place(i), 0, 0)),
        ],
        out_specs=[
            to_columns(3 * quads),
            to_columns(quads),
            to_columns(steps),
            pl.BlockSpec((LANES, width), lambda i: (down_place(i), 0)),
            tokens_spec,
            tokens_spec,
            *([whole] * 6),
        ],
    )(layer_out, tokens_grad, totals, gk, gq, go, gu, gd)
    return (
        made[4][None],
        made[5][None],
        made[6],
        made[7],
        made[0],
        made[1],
        made[8],
        made[9],
        made[2],
        made[11],
        made[3],
        made[10],
    )


def solution(mesh):
    in_specs = (
        P("fsdp", "ctx", None),
        P("fsdp", "ctx"),
        P("fsdp", "ctx", None, None),
        P("fsdp", None),
        P("fsdp"),
        P("fsdp"),
        P("fsdp", None),
        P("fsdp", None),
        P("fsdp"),
        P("fsdp"),
        P("fsdp", None),
        P("fsdp"),
        P("fsdp", None),
        P("fsdp"),
        P("fsdp", "ctx", None),
    )
    out_specs = (
        P("fsdp", "ctx", None),
        P("fsdp", "ctx", None),
        P("fsdp"),
        P("fsdp"),
        P("fsdp", None),
        P("fsdp", None),
        P("fsdp"),
        P("fsdp"),
        P("fsdp", None),
        P("fsdp"),
        P("fsdp", None),
        P("fsdp"),
    )
    return jax.shard_map(shards, mesh=mesh, in_specs=in_specs, out_specs=out_specs, check_vma=False)
```

time: 176 us -> 154 us (0.88)
  Pallas kernels: 172 us -> 153 us
  local copies, waits for them, and re-layouts: 2.88 us -> 0 us
    pallas_call x1, Pallas kernels: 163 us -> 144 us  [shards(): pl.pallas_call(kernel, out_shape=[jax.ShapeDtypeStruct(shape, dtype) for...]
where the time goes in v4:
time: 154 us
  Pallas kernels  153 us (99%)
    pallas_call x1, Pallas kernels, shards(): pl.pallas_call(kernel, out_shape=[jax.ShapeDtypeStruct(shape, dtype) for...  144 us
    pallas_call x1, Pallas kernels, shards(): pl.pallas_call(finish, grid=(steps,), out_shape=[jax.ShapeDtypeStruct(sha...  9.4 us

profile of v4, /device:TPU:0, one launch (start us, length us, event | category | flops | bytes accessed | tf_op | source)
XLA Modules:
  0.0 153.8 jit_solution(144409097594018381)
XLA Ops:
  0.7 143.6 %shard_map.238 = (bf16[128,1024]{1,0:T(8,128)(2,1)}, f32[128,1024]{1,0:T(8,128)}, f32[8,1024]{1,0:T(8,128)}, bf16[8,256,256]{2,1,0:T(8,128)(2,1)}, bf16[8,256,12...) custom-call(bf16[128,1024]{1,0:T(8,128)(2,1)} %bitcast.7, ...), custom_call_target="tpu_custom_call" | custom-call | tf_op jit(solution)/shard_map/pallas_call | solution.py:1267
  144.2 9.4 %shard_map.239 = (f32[256,3072]{1,0:T(8,128)}, f32[256,1024]{1,0:T(8,128)}, f32[256,4096]{1,0:T(8,128)}, f32[1024,1024]{1,0:T(8,128)}, bf16[128,1024]{1,0:T(8,12...) custom-call(bf16[128,1024]{1,0:T(8,128)(2,1)} %get-tuple-element.32., ...), custom_call_target="tpu_custom_call" | custom-call | tf_op jit(solution)/shard_map/pallas_call | solution.py:1318

commit v5 on v4

--- a/solution.py
+++ b/solution.py
@@ -77,8 +77,9 @@
 
 
 class Gather:
-    def __init__(self, at, src, slot, send, recv):
-        self.at, self.src, self.slot, self.send, self.recv = at, src, slot, send, recv
+    def __init__(self, at, src, slot, bulk, send, recv):
+        self.at, self.src, self.slot, self.bulk = at, src, slot, bulk
+        self.send, self.recv = send.at[0], recv
 
     def half(self, c, i):
         block = self.slot(c)
@@ -88,20 +89,20 @@
     def direct(self, i):
         at = self.at
         to = at.partner if i == 0 else at.same(jnp.int32(i))
-        return remote(self.src, self.slot(at.c), self.send.at[i], self.recv.at[at.c], (to, at.f))
+        return remote(self.src, self.slot(at.c), self.send, self.recv.at[at.c], (to, at.f))
 
     def across(self, i):
         at = self.at
         c, to = at.same(jnp.int32(1 + i)), at.same(jnp.int32(2 - i))
         block = self.half(c, i)
         recv = self.recv.at[c] if i == 0 else self.recv.at[CTX]
-        return remote(block, block, self.send.at[3 + i], recv, (to, at.f))
+        return remote(block, block, self.send, recv, (to, at.f))
 
     def passed(self, g):
         at = self.at
         c = at.same(jnp.int32(g))
         block = self.slot(c)
-        return remote(block, block, self.send.at[4 + g], self.recv.at[c], (at.partner, at.f))
+        return remote(block, block, self.send, self.recv.at[c], (at.partner, at.f))
 
     def start(self):
         for i in (1, 2, 0):
@@ -110,7 +111,7 @@
     def wait(self, c):
         at = self.at
         block = self.slot(c)
-        remote(block, block, self.send.at[0], self.recv.at[c], (at.partner, at.f)).wait_recv()
+        remote(block, block, self.send, self.recv.at[c], (at.partner, at.f)).wait_recv()
 
     def near(self, i):
         self.wait(self.at.same(jnp.int32(1 + i)))
@@ -123,73 +124,62 @@
             c = at.same(jnp.int32(3))
             block = self.half(c, i)
             recv = self.recv.at[c] if i == 0 else self.recv.at[CTX]
-            remote(block, block, self.send.at[0], recv, (at.partner, at.f)).wait_recv()
+            remote(block, block, self.send, recv, (at.partner, at.f)).wait_recv()
         self.passed(3).start()
 
     def waits(self):
         loop(0, 4, lambda g: self.wait(self.at.other(g)))
 
     def finish(self):
-        for i in range(3):
-            self.direct(i).wait_send()
-        for i in range(2):
-            self.across(i).wait_send()
-        for g in (1, 2, 3):
-            self.passed(g).wait_send()
+        remote(self.bulk, self.bulk, self.send, self.recv.at[0], (self.at.partner, self.at.f)).wait_send()
 
 
 class Exchange:
-    def __init__(self, at, src, slot, send, recv):
-        self.at, self.src, self.slot, self.send, self.recv = at, src, slot, send, recv
+    def __init__(self, at, src, slot, bulk, send, recv):
+        self.at, self.src, self.slot, self.bulk = at, src, slot, bulk
+        self.send, self.recv = send.at[0], recv.at[0]
 
     def copy(self, d):
         at = self.at
         to = at.ctx_at(d)
-        return remote(
-            self.src(to), self.slot(at.c), self.send.at[d - 1], self.recv.at[at.c], (to, at.f)
-        )
+        return remote(self.src(to), self.slot(at.c), self.send, self.recv, (to, at.f))
 
     def start(self):
         loop(1, CTX, lambda d: self.copy(d).start())
 
-    def wait(self, d):
-        at = self.at
-        c = at.ctx_at(d)
-        block = self.slot(c)
-        remote(block, block, self.send.at[0], self.recv.at[c], (c, at.f)).wait_recv()
+    def whole(self):
+        return remote(self.bulk, self.bulk, self.send, self.recv, (self.at.partner, self.at.f))
 
     def waits(self):
-        loop(1, CTX, self.wait)
+        self.whole().wait_recv()
 
     def finish(self):
-        loop(1, CTX, lambda d: self.copy(d).wait_send())
+        self.whole().wait_send()
 
 
 class Planes:
-    def __init__(self, at, src, slot, send, recv):
-        self.at, self.src, self.slot, self.send, self.recv = at, src, slot, send, recv
+    def __init__(self, at, src, slot, bulk, send, recv):
+        self.at, self.src, self.slot, self.bulk = at, src, slot, bulk
+        self.send, self.recv = send.at[0], recv.at[0]
 
     def copy(self, d):
         at = self.at
         to = at.plane_at(d)
-        return remote(
-            self.src(to), self.slot(at.f), self.send.at[d - 1], self.recv.at[at.f], (at.c, to)
-        )
+        return remote(self.src(to), self.slot(at.f), self.send, self.recv, (at.c, to))
 
     def start(self):
         loop(1, self.at.planes, lambda d: self.copy(d).start())
 
-    def wait(self, d):
+    def whole(self):
         at = self.at
-        f = at.plane_at(d)
-        block = self.slot(f)
-        remote(block, block, self.send.at[0], self.recv.at[f], (at.c, f)).wait_recv()
+        to = at.plane_at(jnp.int32(1))
+        return remote(self.bulk, self.bulk, self.send, self.recv, (at.c, to))
 
     def waits(self):
-        loop(1, self.at.planes, self.wait)
+        self.whole().wait_recv()
 
     def finish(self):
-        loop(1, self.at.planes, lambda d: self.copy(d).wait_send())
+        self.whole().wait_send()
 
 
 class Line:
@@ -319,9 +309,9 @@
 
 
 class Scatter:
-    def __init__(self, at, part, pair, halves, far, pair_send, pair_recv, send, recv):
+    def __init__(self, at, part, pair, halves, far, send, pair_recv, recv):
         self.at, self.part, self.pair, self.halves, self.far = at, part, pair, halves, far
-        self.pair_send, self.pair_recv, self.send, self.recv = pair_send, pair_recv, send, recv
+        self.send, self.pair_recv, self.recv = send.at[0], pair_recv, recv
         self.size = part.shape[1] // 2
 
     def to_partner(self, g):
@@ -329,7 +319,7 @@
         return remote(
             self.part.at[at.other(g)],
             self.pair.at[g],
-            self.pair_send.at[g],
+            self.send,
             self.pair_recv.at[g],
             (at.partner, at.f),
         )
@@ -339,7 +329,7 @@
         return remote(
             self.part.at[at.same(jnp.int32(3)), pl.ds(i * self.size, self.size)],
             self.halves.at[i],
-            self.send.at[i],
+            self.send,
             self.recv.at[i],
             (at.same(jnp.int32(1 + i)), at.f),
         )
@@ -348,7 +338,7 @@
         at = self.at
         to = at.same(jnp.int32(1 + i))
         return remote(
-            self.part.at[to], self.far.at[i], self.send.at[2 + i], self.recv.at[2 + i], (to, at.f)
+            self.part.at[to], self.far.at[i], self.send, self.recv.at[2 + i], (to, at.f)
         )
 
     def add_pair(self, g):
@@ -381,10 +371,8 @@
         return both + (self.far[0].astype(F32) + self.far[1].astype(F32))
 
     def finish(self):
-        loop(0, 4, lambda g: self.to_partner(g).wait_send())
-        for i in range(2):
-            self.across(i).wait_send()
-            self.beside(i).wait_send()
+        at, blocks = self.at, self.part.at[pl.ds(0, CTX - 1)]
+        remote(blocks, blocks, self.send, self.recv.at[0], (at.partner, at.f)).wait_send()
 
 
 def standard(values):
@@ -434,8 +422,7 @@
 def layer_kernel(r, planes):
     at = Place(planes)
     me, f = at.c, at.f
-    tokens, cotangent = r.tokens, r.cotangent
-    local, width = tokens.shape
+    local, width = r.tokens_in.shape
     seq = local * CTX
     blocks, local_blocks = seq // BLOCK, local // BLOCK
     part_rows = width // planes
@@ -456,6 +443,7 @@
     my_rows = rows_of(f, part_rows)
     my_columns = rows_of(me, columns)
     my_tokens = rows_of(me, local)
+    tokens, cotangent = r.tokg.at[my_tokens], r.cotg.at[my_tokens]
 
     barrier = pltpu.get_barrier_semaphore()
     loop(
@@ -473,6 +461,20 @@
         ),
     )
 
+    fetched = (
+        (r.tokens_in, tokens), (r.gain_one_in, r.gain_one), (r.bias_one_in, r.bias_one),
+        (r.gain_two_in, r.gain_two), (r.bias_two_in, r.bias_two), (r.bias_down_in, r.bias_down),
+        (r.bias_up_in, r.bias_up), (r.segments_in, r.segments), (r.random_in, r.random),
+        (r.globals_in, r.globals), (r.cotangent_in, cotangent),
+    )
+    fetch = [
+        pltpu.make_async_copy(src, dst, r.fetch.at[i]) for i, (src, dst) in enumerate(fetched)
+    ]
+    for copy in fetch:
+        copy.start()
+    layer_copy = pltpu.make_async_copy(r.layer, r.layer_out, r.fetch.at[len(fetch)])
+    grad_copy = pltpu.make_async_copy(r.grad, r.tokens_grad, r.fetch.at[len(fetch) + 1])
+    totals_copy = pltpu.make_async_copy(r.sums, r.totals, r.fetch.at[len(fetch) + 2])
     stage_j = [
         pltpu.make_async_copy(
             r.joint.at[:, pl.ds(pl.multiple_of(width * j + columns * me, LANES), columns)],
@@ -504,6 +506,8 @@
     def _():
         stage_d.start()
 
+    for copy in fetch[1:10]:
+        copy.wait()
     small, short = r.small, r.small.shape[1]
     small[...] = jnp.zeros_like(small)
     for i, vector in enumerate((r.gain_one, r.bias_one, r.gain_two, r.bias_two, r.bias_down)):
@@ -513,26 +517,36 @@
         small[5 + i : 6 + i, :] = piece.astype(F32).reshape(1, short)
 
     def token_gather(src, dst, sems):
-        return Gather(at, src, lambda c: dst.at[rows_of(c, local)], *sems)
+        bulk = dst.at[pl.ds(0, (CTX - 1) * local)]
+        return Gather(at, src, lambda c: dst.at[rows_of(c, local)], bulk, *sems)
 
     tok = token_gather(tokens, r.tokg, r.tok_sem)
     cot = token_gather(cotangent, r.cotg, r.cot_sem)
     x2 = token_gather(r.x2.at[my_tokens], r.x2, r.x2_sem)
     attg = token_gather(r.attg.at[my_tokens], r.attg, r.attg_sem)
     wog = Gather(
-        at, r.wo.at[:, my_columns], lambda c: r.wo.at[:, rows_of(c, columns)], *r.wog_sem
-    )
-    codes = Exchange(at, lambda c: r.codes.at[c], lambda c: r.codeg.at[c], *r.code_sem)
+        at, r.wo.at[:, my_columns], lambda c: r.wo.at[:, rows_of(c, columns)],
+        r.wo.at[:, pl.ds(0, (CTX - 1) * columns)], *r.wog_sem
+    )
+    seven = pl.ds(0, CTX - 1)
+    codes = Exchange(
+        at, lambda c: r.codes.at[c], lambda c: r.codeg.at[c], r.codeg.at[seven], *r.code_sem
+    )
     att_swap = Exchange(
-        at, lambda c: r.att.at[rows_of(c, local)], lambda c: r.attx.at[c], *r.att_sem
+        at, lambda c: r.att.at[rows_of(c, local)], lambda c: r.attx.at[c], r.attx.at[seven], *r.att_sem
     )
 
     def token_swap(src, dst, sems):
-        return Exchange(at, lambda c: src.at[c], lambda c: dst.at[rows_of(c, local)], *sems)
+        return Exchange(
+            at, lambda c: src.at[c], lambda c: dst.at[rows_of(c, local)], src.at[seven], *sems
+        )
 
     dat_swap = token_swap(r.dat, r.datg, r.dat_sem)
     br_swap = token_swap(r.brs, r.brg, r.br_sem)
-    small_planes = Planes(at, lambda to: small, lambda p: r.smallg.at[p], *r.small_sem)
+    rest = pl.ds(0, planes - 1)
+    small_planes = Planes(
+        at, lambda to: small, lambda p: r.smallg.at[p], r.smallg.at[rest], *r.small_sem
+    )
 
     def weight_line(ref, sems, width_ds):
         return Line(
@@ -559,7 +573,7 @@
     class Owned:
         def __init__(self, number, line, acc, total, out, sems):
             self.line, self.acc, self.sum = line, acc, total
-            self.gather = Gather(at, total, lambda c: out.at[c], *sems)
+            self.gather = Gather(at, total, lambda c: out.at[c], out.at[seven], *sems)
             self.own = pltpu.make_async_copy(total, out.at[me], r.own.at[number])
 
         def total(self):
@@ -588,7 +602,8 @@
 
     class OwnedDown:
         def __init__(self):
-            self.gather = Gather(at, r.td, lambda c: r.gd.at[c], *r.gd_sem)
+            if full_shard:
+                self.gather = Gather(at, r.td, lambda c: r.gd.at[c], r.gd.at[seven], *r.gd_sem)
             self.own = pltpu.make_async_copy(r.td, r.gd.at[down_place], r.own.at[4])
 
         def copy(self, d):
@@ -648,8 +663,12 @@
     class Sums:
         def __init__(self, own, acc, sent, ctx_in, plane_in, ctx_sems, plane_sems):
             self.own, self.acc, self.sent, self.ctx_in, self.plane_in = own, acc, sent, ctx_in, plane_in
-            self.swap = Exchange(at, lambda c: own, lambda c: ctx_in.at[c], *ctx_sems)
-            self.planes = Planes(at, lambda to: sent, lambda p: plane_in.at[p], *plane_sems)
+            self.swap = Exchange(
+                at, lambda c: own, lambda c: ctx_in.at[c], ctx_in.at[seven], *ctx_sems
+            )
+            self.planes = Planes(
+                at, lambda to: sent, lambda p: plane_in.at[p], plane_in.at[rest], *plane_sems
+            )
 
         def put(self, row, vector):
             for k in range(width // LANES):
@@ -691,8 +710,8 @@
 
     def open_devices():
         pl.semaphore_wait(barrier, CTX - 1 + planes - 1)
-        r.tokg[my_tokens, :] = tokens[...]
-        r.cotg[my_tokens, :] = cotangent[...]
+        fetch[0].wait()
+        fetch[10].wait()
 
     def wj_start():
         for copy in stage_j:
@@ -879,7 +898,7 @@
         middle_grad = cot_own + standard_grad(
             normed_two_grad * params[2:3, :], normal, r.rate2[:, 0:1]
         )
-        r.tokens_grad[...] = middle_grad
+        r.grad[...] = middle_grad
         branch = middle_grad.astype(BF16)
         attended_grad = dot_nt(branch, r.wo[...]).astype(BF16)
         for c in range(CTX):
@@ -930,79 +949,89 @@
         weight_grad(r.do, r.attg, r.brg)
 
     def layer_end():
-        r.layer_out[...] = (r.middle[...] + feed.total() + params[4:5, :]).astype(BF16)
+        r.layer[...] = (r.middle[...] + feed.total() + params[4:5, :]).astype(BF16)
+        layer_copy.start()
 
     def tokens_back():
         normed_one_grad = first.total()
         normal, rate = standard(tokens[...].astype(F32))
         late.put(0, jnp.sum(normed_one_grad * normal, axis=0, keepdims=True))
         late.put(8, jnp.sum(normed_one_grad, axis=0, keepdims=True))
-        r.tokens_grad[...] += standard_grad(normed_one_grad * params[0:1, :], normal, rate)
+        r.grad[...] += standard_grad(normed_one_grad * params[0:1, :], normal, rate)
+        grad_copy.start()
 
     def write_totals():
         for i, (sums, row) in enumerate(((late, 0), (late, 8), (early, 0), (early, 8), (early, 16))):
             vector = jnp.broadcast_to(sums.row(row), (8, width))
             turned = pltpu.roll(vector, lax.rem((planes - f) * part_rows, width), axis=1)
-            r.totals[i : i + 1, :] = turned[0:1]
+            r.sums[i : i + 1, :] = turned[0:1]
         for k in range(shard_blocks):
-            r.totals[5:6, k * LANES : (k + 1) * LANES] = early.acc[
+            r.sums[5:6, k * LANES : (k + 1) * LANES] = early.acc[
                 pl.ds(24 + f * shard_blocks + k, 1), :
             ]
 
+    def finish(*ended):
+        for each in ended:
+            each.finish()
+
+    def finish_forward():
+        finish(tok, cot, wog, x2, codes, att_swap, small_planes, wj, wo, wu, wd)
+
+    def finish_middle():
+        finish(attg, dat_swap, br_swap, dd, back)
+
     open_devices()
-    tok.start()
-    wj_start()
     wo_start()
-    wo.passes(1)
-    small_planes.start()
-    cot.start()
-    take_params()
-    wj.passes(1)
-    tok.near(0)
-    wo.passes(2)
-    tok.near(1)
     make_codes()
     codes.start()
-    wj.passes(2)
+    wj_start()
+    small_planes.start()
+    tok.start()
+    wo.passes(1)
+    take_params()
+    wo.passes(2)
 
     def step_1(i):
 
+        @pl.when(i == 1)
+        def _():
+            wu_start()
+            cot.start()
+            tok.near(0)
+            wj.passes(1)
+            tok.near(1)
+            cot.near(0)
+            wj.passes(2)
+            tok.far()
+            cot.near(1)
+            wo.passes(3)
+
+        norm_tokens(i)
+
+    loop(0, 4, step_1)
+
+    wog.start()
+    wj.passes(3)
+    codes.waits()
+
+    def step_2(i):
+
+        @pl.when(i == 1)
+        def _():
+            wd_start()
+            wu.passes(1)
+
+        project(i)
+
+    loop(0, 4, step_2)
+
+
+    def step_3(i):
+
         @pl.when(i == 2)
         def _():
-            wu_start()
-            tok.far()
-            cot.near(0)
-
-        @pl.when(i == 3)
-        def _():
-            wo.passes(3)
-            wog.start()
-
-        norm_tokens(i)
-
-    loop(0, 4, step_1)
-
-    codes.waits()
-    wj.passes(3)
-
-    def step_2(i):
-
-        @pl.when(i == 1)
-        def _():
-            cot.near(1)
-
-        project(i)
-
-    loop(0, 4, step_2)
-
-
-    def step_3(i):
-
-        @pl.when(i == 2)
-        def _():
-            wu.passes(1)
+            cot.far()
             wog.near(1)
-            cot.far()
             wog.near(0)
 
         attend(i)
@@ -1010,7 +1039,6 @@
     loop(0, 4, step_3)
 
     att_swap_start()
-    wd_start()
     wog.far()
     wu.passes(2)
     project_out()
@@ -1024,130 +1052,126 @@
 
         @pl.when(i == 2)
         def _():
-            attg.start()
+            x2.far()
             wd.passes(2)
-            x2.far()
 
         hidden_units(i)
 
     loop(0, 4, step_4)
 
+    attg.start()
     cot.waits()
     down_grad()
     wd.passes(3)
+    dd.step(3)
+
+    def step_5(i):
+
+        @pl.when(i == 2)
+        def _():
+            back.first()
+
+        feed_back(i)
+
+    loop(0, 3, step_5)
+
+    back.second()
+    dd.step(2)
+    feed_part(jnp.int32(0))
+    feed_back(jnp.int32(3))
+    up_weight_grad()
     attg.near(0)
     attg.near(1)
-    dd.step(3)
-    feed_back(jnp.int32(0))
-    feed_part(jnp.int32(0))
-    back.first()
-
-    def step_5(i):
-
-        @pl.when(i == 3)
-        def _():
-            back.second()
-            dd.step(2)
-
-        feed_back(i)
-
-    loop(1, 4, step_5)
-
-    up_weight_grad()
     du.step(3)
     middle_back()
     dat_start()
     dd.step(1)
-    loop(1, 3, feed_part)
+    loop(1, 4, feed_part)
+    attg.far()
     feed.first()
-    br_start()
     dat_swap.waits()
 
     def step_6(i):
 
         @pl.when(i == 1)
         def _():
+            early.start()
             du.step(2)
+            br_start()
+
+        @pl.when(i == 2)
+        def _():
             gd.total()
-
-        @pl.when(i == 2)
-        def _():
             feed.second()
 
         @pl.when(i == 3)
         def _():
             du.step(1)
-            early.start()
 
         attend_back(i)
 
     loop(0, 4, step_6)
 
+    finish_forward()
     keys_back()
 
     def step_7(i):
 
         @pl.when(i == 1)
-        def _():
-            query_weight_grad()
-
-        @pl.when(i == 2)
         def _():
             key_weight_grad()
             dk.step(3)
-            attg.far()
+            query_weight_grad()
+            dq.step(3)
+            out_weight_grad()
+            finish_middle()
             first.first()
-            early.middle()
-            out_weight_grad()
-            dk.step(2)
-            dq.step(3)
-            gd.near(0)
-            gd.near(1)
 
         first_part(i)
 
-    loop(0, 3, step_7)
-
+    loop(0, 4, step_7)
+
+    gd.near(1)
+    gd.near(0)
+    dk.step(2)
+    dq.step(2)
     first.second()
-    dq.step(2)
+    do.step(3)
     gu.total()
     dk.step(1)
-    do.step(3)
     dq.step(1)
+    gk.total()
+    early.middle()
+    gq.total()
     do.step(2)
-    feed_part(jnp.int32(3))
-    gk.total()
-    gq.total()
-    first_part(jnp.int32(3))
-    early.end()
+    tokens_back()
+    late.start()
     do.step(1)
-    gu.near(1)
     go.total()
     gu.near(0)
-    gq.near(1)
-    tokens_back()
+    gu.near(1)
+    late.middle()
     gk.near(0)
     gk.near(1)
-    late.start()
+    gq.near(1)
+    gd.far()
     go.near(0)
-    gd.far()
+    go.near(1)
     gq.near(0)
-    late.middle()
-    go.near(1)
     gu.far()
     gk.far()
+    gq.far()
     go.far()
     layer_end()
-    gq.far()
     late.end()
+    early.end()
+    write_totals()
+    totals_copy.start()
     for each in (gd, gu, go, gk, gq):
         each.waits()
-    write_totals()
-    for each in (
-        tok, cot, wog, x2, attg, gu, go, gk, gq, gd, codes, att_swap, dat_swap, br_swap, early, late,
-        small_planes, wj, wo, wu, wd, dd, du, do, dk, dq, back, feed, first,
-    ):
-        each.finish()
+    finish(gu, go, gk, gq, gd, early, late, du, do, dk, dq, feed, first)
+    for copy in (layer_copy, grad_copy, totals_copy):
+        copy.wait()
 
 
 def shards(
@@ -1182,50 +1206,55 @@
     assert ctx == CTX and columns == LANES and heads == 2 * ctx and blocks + SEGMENTS <= 64
     assert CTX % shard_blocks == 0 and ff // width == ff_blocks
 
-    vmem, hbm = pl.BlockSpec(memory_space=pltpu.VMEM), pl.BlockSpec(memory_space=pl.ANY)
+    hbm = pl.BlockSpec(memory_space=pl.ANY)
     inputs = dict(
-        tokens=(tokens[0], vmem),
-        cotangent=(cotangent[0], vmem),
-        segments=(segment_ids, vmem),
-        random=(random_blocks[0].transpose(2, 0, 1), vmem),
-        globals=(global_blocks, vmem),
-        gain_one=(first_gain, vmem),
-        bias_one=(first_bias, vmem),
-        gain_two=(second_gain, vmem),
-        bias_two=(second_bias, vmem),
-        bias_up=(up_bias, vmem),
-        bias_down=(down_bias, vmem),
-        joint=(joint_weight, hbm),
-        outw=(output_weight, hbm),
-        up=(up_weight, hbm),
-        down=(down_weight, hbm),
+        tokens_in=tokens[0],
+        cotangent_in=cotangent[0],
+        segments_in=segment_ids,
+        random_in=random_blocks[0].transpose(2, 0, 1),
+        globals_in=global_blocks,
+        gain_one_in=first_gain,
+        bias_one_in=first_bias,
+        gain_two_in=second_gain,
+        bias_two_in=second_bias,
+        bias_up_in=up_bias,
+        bias_down_in=down_bias,
+        joint=joint_weight,
+        outw=output_weight,
+        up=up_weight,
+        down=down_weight,
     )
     outputs = dict(
-        layer_out=((local, width), BF16, vmem),
-        tokens_grad=((local, width), F32, vmem),
-        totals=((8, width), F32, vmem),
-        gk=((ctx, part_rows, 2 * columns), BF16, hbm),
-        gq=((ctx, part_rows, columns), BF16, hbm),
-        go=((ctx, part_rows, columns), BF16, hbm),
-        gu=((ctx, part_rows, ff_part), BF16, hbm),
-        gd=((shard_blocks, LANES, width), BF16, hbm),
+        layer_out=((local, width), BF16),
+        tokens_grad=((local, width), F32),
+        totals=((8, width), F32),
+        gk=((ctx, part_rows, 2 * columns), BF16),
+        gq=((ctx, part_rows, columns), BF16),
+        go=((ctx, part_rows, columns), BF16),
+        gu=((ctx, part_rows, ff_part), BF16),
+        gd=((shard_blocks, LANES, width), BF16),
     )
     dma = lambda n: pltpu.SemaphoreType.DMA((n,))
     v16 = lambda *shape: pltpu.VMEM(shape, BF16)
     v32 = lambda *shape: pltpu.VMEM(shape, F32)
-    others = max(planes - 1, 1)
     scatter = (
         v16(ctx, local, width), v16(4, local, width), v16(2, local // 2, width), v16(2, local, width),
-        dma(4), dma(4), dma(4), dma(4),
-    )
-    gather, swap, plane_sems = (dma(8), dma(ctx + 1)), (dma(ctx - 1), dma(ctx)), (dma(others), dma(planes))
+        dma(1), dma(4), dma(4),
+    )
+    gather, swap = (dma(1), dma(ctx + 1)), (dma(1), dma(1))
     line, toward = (dma(2 * planes), dma(planes)), (dma(planes), dma(planes + 1))
     short = max(part_rows, LANES)
     vectors = lambda rows: (
         v16(rows, LANES), v32(rows, LANES), v16(rows, LANES), v16(ctx, rows, LANES),
-        v16(planes, rows, LANES), swap, plane_sems,
-    )
+        v16(planes, rows, LANES), swap, swap,
+    )
+    copied = lambda name: pltpu.VMEM(inputs[name].shape, inputs[name].dtype)
     scratch = dict(
+        segments=copied("segments_in"), random=copied("random_in"), globals=copied("globals_in"),
+        gain_one=copied("gain_one_in"), bias_one=copied("bias_one_in"),
+        gain_two=copied("gain_two_in"), bias_two=copied("bias_two_in"),
+        bias_up=copied("bias_up_in"), bias_down=copied("bias_down_in"), fetch=dma(14),
+        layer=v16(local, width), grad=v32(local, width), sums=v32(8, width),
         wj=v16(width, 3 * columns), wo=v16(width, width), wu=v16(width, ff_part),
         wd=v16(ff_part, width), tokg=v16(seq, width), cotg=v16(seq, width),
         x1=v16(seq, width), x2=v16(seq, width), attg=v16(seq, width),
@@ -1251,9 +1280,9 @@
         stage=dma(5 + ff_blocks), own=dma(5), wd_sem=(dma(2 * ff_blocks), dma(ff_blocks)),
         dwd_sem=(dma(ff_blocks), dma(ff_blocks + 1)), back=scatter, feed=scatter, first=scatter,
         tok_sem=gather, cot_sem=gather, wog_sem=gather, x2_sem=gather, attg_sem=gather,
-        gk_sem=gather, gq_sem=gather, go_sem=gather, gu_sem=gather, gd_sem=gather,
+        gk_sem=gather, gq_sem=gather, go_sem=gather, gu_sem=gather, gd_sem=gather if shard_blocks == ctx else (dma(ctx - 1), dma(ctx)),
         code_sem=swap, att_sem=swap, dat_sem=swap, br_sem=swap,
-        small_sem=plane_sems, wj_sem=line, wo_sem=line, wu_sem=line,
+        small_sem=swap, wj_sem=line, wo_sem=line, wu_sem=line,
         dk_sem=toward, dq_sem=toward, do_sem=toward, du_sem=toward,
     )
     shapes, scratch_tree = jax.tree.flatten(scratch)
@@ -1266,16 +1295,17 @@
 
     layer_out, tokens_grad, totals, gk, gq, go, gu, gd = pl.pallas_call(
         kernel,
-        out_shape=[jax.ShapeDtypeStruct(shape, dtype) for shape, dtype, _ in outputs.values()],
-        in_specs=[spec for _, spec in inputs.values()],
-        out_specs=[spec for *_, spec in outputs.values()],
+        out_shape=[jax.ShapeDtypeStruct(shape, dtype) for shape, dtype in outputs.values()],
+        in_specs=[hbm] * ins,
+        out_specs=[hbm] * outs,
         scratch_shapes=shapes,
         compiler_params=pltpu.CompilerParams(
-            collective_id=0, has_side_effects=True, vmem_limit_bytes=60 * 1024 * 1024
+            collective_id=0, has_side_effects=True, fuse_transposed_lhs_in_matmul=True,
+            vmem_limit_bytes=60 * 1024 * 1024
         ),
-    )(*(value for value, _ in inputs.values()))
-
-    group = 4
+    )(*inputs.values())
+
+    group = ctx
     quads = ctx // group
     steps = ff_blocks * quads
 
@@ -1296,7 +1326,7 @@
             spread(gk, joint)
 
         spread(gu, up)
-        down[...] = gd[0].astype(F32)
+        down[...] = gd[...].reshape(down.shape).astype(F32)
         out[...] = out_in[...]
         grad[...] = grad_in[...]
         for i, vector in enumerate(vectors[:5]):
@@ -1312,7 +1342,8 @@
     def to_columns(count):
         return pl.BlockSpec((part_rows, group * columns), lambda i: (0, jnp.minimum(i, count - 1)))
 
-    down_place = lambda i: jnp.minimum(i, shard_blocks - 1)
+    down_group = max(shard_blocks // steps, 1)
+    down_place = lambda i: jnp.minimum(i, shard_blocks // down_group - 1)
     whole = pl.BlockSpec(memory_space=pltpu.VMEM)
     tokens_spec = pl.BlockSpec((local // steps, width), lambda i: (i, 0))
     made = pl.pallas_call(
@@ -1334,17 +1365,18 @@
             from_places(0, quads),
             from_places(0, quads),
             from_places(0, steps),
-            pl.BlockSpec((1, LANES, width), lambda i: (down_place(i), 0, 0)),
+            pl.BlockSpec((down_group, LANES, width), lambda i: (down_place(i), 0, 0)),
         ],
         out_specs=[
             to_columns(3 * quads),
             to_columns(quads),
             to_columns(steps),
-            pl.BlockSpec((LANES, width), lambda i: (down_place(i), 0)),
+            pl.BlockSpec((down_group * LANES, width), lambda i: (down_place(i), 0)),
             tokens_spec,
             tokens_spec,
             *([whole] * 6),
         ],
+        compiler_params=pltpu.CompilerParams(vmem_limit_bytes=60 * 1024 * 1024),
     )(layer_out, tokens_grad, totals, gk, gq, go, gu, gd)
     return (
         made[4][None],

time: 154 us -> 147 us (0.955)
  Pallas kernels: 153 us -> 146 us
    pallas_call x1, Pallas kernels: 144 us -> 137 us  [shards(): pl.pallas_call(kernel, out_shape=[jax.ShapeDtypeStruct(shape, dtype) for...]
where the time goes in v5:
time: 147 us
  Pallas kernels  146 us (99%)
    pallas_call x1, Pallas kernels, shards(): pl.pallas_call(kernel, out_shape=[jax.ShapeDtypeStruct(shape, dtype) for...  137 us
    pallas_call x1, Pallas kernels, shards(): pl.pallas_call(finish, grid=(steps,), out_shape=[jax.ShapeDtypeStruct(sha...  8.91 us

profile of v5, /device:TPU:0, one launch (start us, length us, event | category | flops | bytes accessed | tf_op | source)
XLA Modules:
  0.0 146.8 jit_solution(6022680190305880100)
XLA Ops:
  0.7 137.1 %shard_map.238 = (bf16[128,1024]{1,0:T(8,128)(2,1)}, f32[128,1024]{1,0:T(8,128)}, f32[8,1024]{1,0:T(8,128)}, bf16[8,256,256]{2,1,0:T(8,128)(2,1)}, bf16[8,256,12...) custom-call(bf16[128,1024]{1,0:T(8,128)(2,1)} %bitcast.7, ...), custom_call_target="tpu_custom_call" | custom-call | tf_op jit(solution)/shard_map/pallas_call | solution.py:1296
  137.8 8.9 %shard_map.239 = (f32[256,3072]{1,0:T(8,128)}, f32[256,1024]{1,0:T(8,128)}, f32[256,4096]{1,0:T(8,128)}, f32[1024,1024]{1,0:T(8,128)}, bf16[128,1024]{1,0:T(8,12...) custom-call(bf16[128,1024]{1,0:T(8,128)(2,1)} %get-tuple-element.32., ...), custom_call_target="tpu_custom_call" | custom-call | tf_op jit(solution)/shard_map/pallas_call | solution.py:1349

commit v6 on v5

--- a/solution.py
+++ b/solution.py
@@ -1076,15 +1076,16 @@
     loop(0, 3, step_5)
 
     back.second()
+    attg.near(0)
+    attg.near(1)
     dd.step(2)
     feed_part(jnp.int32(0))
     feed_back(jnp.int32(3))
     up_weight_grad()
-    attg.near(0)
-    attg.near(1)
     du.step(3)
     middle_back()
     dat_start()
+    early.start()
     dd.step(1)
     loop(1, 4, feed_part)
     attg.far()
@@ -1095,7 +1096,6 @@
 
         @pl.when(i == 1)
         def _():
-            early.start()
             du.step(2)
             br_start()
 
@@ -1106,6 +1106,7 @@
 
         @pl.when(i == 3)
         def _():
+            early.middle()
             du.step(1)
 
         attend_back(i)
@@ -1141,7 +1142,6 @@
     dk.step(1)
     dq.step(1)
     gk.total()
-    early.middle()
     gq.total()
     do.step(2)
     tokens_back()

time: 147 us -> 147 us (level)
  no operation moved by 1% of the time
where the time goes in v6:
time: 147 us; the launch traced here: 146 us
  Pallas kernels  145 us (99%)
    pallas_call x1, Pallas kernels, shards(): pl.pallas_call(kernel, out_shape=[jax.ShapeDtypeStruct(shape, dtype) for...  137 us
    pallas_call x1, Pallas kernels, shards(): pl.pallas_call(finish, grid=(steps,), out_shape=[jax.ShapeDtypeStruct(sha...  8.91 us

profile of v6, /device:TPU:0, one launch (start us, length us, event | category | flops | bytes accessed | tf_op | source)
XLA Modules:
  0.0 146.3 jit_solution(17723861370162269586)
XLA Ops:
  0.7 136.6 %shard_map.238 = (bf16[128,1024]{1,0:T(8,128)(2,1)}, f32[128,1024]{1,0:T(8,128)}, f32[8,1024]{1,0:T(8,128)}, bf16[8,256,256]{2,1,0:T(8,128)(2,1)}, bf16[8,256,12...) custom-call(bf16[128,1024]{1,0:T(8,128)(2,1)} %bitcast.7, ...), custom_call_target="tpu_custom_call" | custom-call | tf_op jit(solution)/shard_map/pallas_call | solution.py:1296
  137.2 8.9 %shard_map.239 = (f32[256,3072]{1,0:T(8,128)}, f32[256,1024]{1,0:T(8,128)}, f32[256,4096]{1,0:T(8,128)}, f32[1024,1024]{1,0:T(8,128)}, bf16[128,1024]{1,0:T(8,12...) custom-call(bf16[128,1024]{1,0:T(8,128)(2,1)} %get-tuple-element.32., ...), custom_call_target="tpu_custom_call" | custom-call | tf_op jit(solution)/shard_map/pallas_call | solution.py:1349

commit v7 on v6

--- a/solution.py
+++ b/solution.py
@@ -95,8 +95,7 @@
         at = self.at
         c, to = at.same(jnp.int32(1 + i)), at.same(jnp.int32(2 - i))
         block = self.half(c, i)
-        recv = self.recv.at[c] if i == 0 else self.recv.at[CTX]
-        return remote(block, block, self.send, recv, (to, at.f))
+        return remote(block, block, self.send, self.recv.at[c], (to, at.f))
 
     def passed(self, g):
         at = self.at
@@ -119,12 +118,7 @@
         self.passed(1 + i).start()
 
     def far(self):
-        at = self.at
-        for i in range(2):
-            c = at.same(jnp.int32(3))
-            block = self.half(c, i)
-            recv = self.recv.at[c] if i == 0 else self.recv.at[CTX]
-            remote(block, block, self.send, recv, (at.partner, at.f)).wait_recv()
+        self.wait(self.at.same(jnp.int32(3)))
         self.passed(3).start()
 
     def waits(self):
@@ -1030,7 +1024,6 @@
 
         @pl.when(i == 2)
         def _():
-            cot.far()
             wog.near(1)
             wog.near(0)
 
@@ -1039,6 +1032,7 @@
     loop(0, 4, step_3)
 
     att_swap_start()
+    cot.far()
     wog.far()
     wu.passes(2)
     project_out()
@@ -1241,7 +1235,7 @@
         v16(ctx, local, width), v16(4, local, width), v16(2, local // 2, width), v16(2, local, width),
         dma(1), dma(4), dma(4),
     )
-    gather, swap = (dma(1), dma(ctx + 1)), (dma(1), dma(1))
+    gather, swap = (dma(1), dma(ctx)), (dma(1), dma(1))
     line, toward = (dma(2 * planes), dma(planes)), (dma(planes), dma(planes + 1))
     short = max(part_rows, LANES)
     vectors = lambda rows: (

time: 147 us -> 146 us (level)
  no operation moved by 1% of the time
where the time goes in v7:
time: 146 us
  Pallas kernels  145 us (99%)
    pallas_call x1, Pallas kernels, shards(): pl.pallas_call(kernel, out_shape=[jax.ShapeDtypeStruct(shape, dtype) for...  136 us
    pallas_call x1, Pallas kernels, shards(): pl.pallas_call(finish, grid=(steps,), out_shape=[jax.ShapeDtypeStruct(sha...  8.91 us

profile of v7, /device:TPU:0, one launch (start us, length us, event | category | flops | bytes accessed | tf_op | source)
XLA Modules:
  0.0 146.2 jit_solution(11721608535533457880)
XLA Ops:
  0.7 136.5 %shard_map.238 = (bf16[128,1024]{1,0:T(8,128)(2,1)}, f32[128,1024]{1,0:T(8,128)}, f32[8,1024]{1,0:T(8,128)}, bf16[8,256,256]{2,1,0:T(8,128)(2,1)}, bf16[8,256,12...) custom-call(bf16[128,1024]{1,0:T(8,128)(2,1)} %bitcast.7, ...), custom_call_target="tpu_custom_call" | custom-call | tf_op jit(solution)/shard_map/pallas_call | solution.py:1290
  137.1 8.9 %shard_map.239 = (f32[256,3072]{1,0:T(8,128)}, f32[256,1024]{1,0:T(8,128)}, f32[256,4096]{1,0:T(8,128)}, f32[1024,1024]{1,0:T(8,128)}, bf16[128,1024]{1,0:T(8,12...) custom-call(bf16[128,1024]{1,0:T(8,128)(2,1)} %get-tuple-element.32., ...), custom_call_target="tpu_custom_call" | custom-call | tf_op jit(solution)/shard_map/pallas_call | solution.py:1343
